TPU v7x, 512 devices: a whole 4x8x8 slice. The times are simulated.
512 devices in a mesh: dp: 64 (over z, x, core), tensor: 8 (over y).
Axes of the slice: x: 4, y: 8, z: 8, core: 2. Of those that a mesh axis runs over, the one named last changes fastest.
Arguments:
- gradient: bfloat16 [512, 53248], P('dp', 'tensor'), may hold values from -1.5 to 1.5
- block_list: int32 [64, 2], P('dp'), may hold values from 0 to 51, as said below
- block_counts: int32 [64], P('dp'), may hold values from 0 to 2, as said below
- stats: float32 [64, 2, 1024, 1024], P('dp', None, None, 'tensor'), as said below
- basis: bfloat16 [64, 2, 1024, 1024], P('dp', None, None, 'tensor'), may hold values from -0.1875 to 0.1875
- first_moment: float32 [64, 2, 512, 1024], P('dp', None, None, 'tensor'), may hold values from -2 to 2
- second_moment: float32 [64, 2, 512, 1024], P('dp', None, None, 'tensor'), may hold values from 0.01 to 1
Outputs:
- update: bfloat16 [512, 53248], P('dp', 'tensor')
- new_stats: float32 [64, 2, 1024, 1024], P('dp', None, None, 'tensor')
- new_first: float32 [64, 2, 512, 1024], P('dp', None, None, 'tensor')
- new_second: float32 [64, 2, 512, 1024], P('dp', None, None, 'tensor')
Inputs may be any that keep to these rules, and one draw needn't show every extreme that they name: `block_list`: the first block_counts[o] entries of row o name the blocks that owner o updates; over all owners these name every one of the 52 blocks exactly once. Later entries are ignored. `block_counts`: they sum to 52; some owner holds exactly 2 blocks. `stats`: Symmetric.
All inputs are finite; a program needn't handle non-finite values.
Results may differ from a plain program's by a relative error of at most 0.0049.
Values may be sent and summed in bfloat16 or wider, within the bound.
No kernel may reach another device: no remote copies, remote signals or barrier semaphores. Data moves between devices by JAX's collectives and lax.ppermute only.
A program may use at most 64 MiB of HBM per device.

v0:
```python
import jax
import jax.numpy as jnp
from jax import lax
from jax.sharding import PartitionSpec as P

STEP = 10


beta_one = 0.9
beta_two = 0.95
beta_stat = 0.95
epsilon = 1e-08


def on_device(gradient, block_list, block_counts, stats, basis, first_moment, second_moment):
    rows_dev, cols_dev = gradient.shape
    slot_count = block_list.shape[1]
    owner_count = lax.axis_size("dp")
    block_width = stats.shape[2]
    part_width = stats.shape[3]
    column_index = lax.axis_index("tensor")
    lists_all, counts_all = (
        lax.all_gather(block_list, "dp", axis=0, tiled=True),
        lax.all_gather(block_counts, "dp", axis=0, tiled=True),
    )
    full_rows = lax.all_gather(gradient, "tensor", axis=1, tiled=True)
    block_total = full_rows.shape[1] // block_width
    by_block = full_rows.reshape(rows_dev, block_total, block_width).transpose(1, 0, 2)
    targets = lists_all.T
    outgoing = jnp.take(by_block, targets, axis=0)
    arrived = lax.all_to_all(outgoing, "dp", split_axis=1, concat_axis=1, tiled=True)
    block_grad = arrived.reshape(slot_count, owner_count * rows_dev, block_width)
    local_cols = lax.dynamic_slice_in_dim(block_grad, column_index * part_width, part_width, 2)
    basis_here = basis[0]
    rotated = jnp.einsum("srb,sbc->src", block_grad, basis_here, preferred_element_type=jnp.float32)
    gram_part = jnp.einsum(
        "srb,src->sbc", block_grad, local_cols, preferred_element_type=jnp.float32
    )
    bias_one = 1.0 - beta_one**STEP
    bias_two = 1.0 - beta_two**STEP
    moment_one = beta_one * first_moment[0] + (1.0 - beta_one) * rotated
    moment_two = beta_two * second_moment[0] + (1.0 - beta_two) * rotated * rotated
    direction = (moment_one / bias_one / (jnp.sqrt(moment_two / bias_two) + epsilon)).astype(
        jnp.bfloat16
    )
    partial_update = jnp.einsum(
        "src,sbc->srb", direction, basis_here, preferred_element_type=jnp.float32
    )
    new_stat = beta_stat * stats[0] + (1.0 - beta_stat) * gram_part
    live_here = (jnp.arange(slot_count) < block_counts[0])[:, None, None]
    new_stats = jnp.where(live_here, new_stat, stats[0])[None]
    new_first = jnp.where(live_here, moment_one, first_moment[0])[None]
    new_second = jnp.where(live_here, moment_two, second_moment[0])[None]
    flat_lists = targets.reshape(-1)
    live_all = (jnp.arange(slot_count)[:, None] < counts_all[None, :]).reshape(-1)
    select = ((flat_lists[None, :] == jnp.arange(block_total)[:, None]) & live_all[None, :]).astype(
        jnp.bfloat16
    )
    summed = lax.psum(partial_update, "tensor").astype(jnp.bfloat16)
    returned = lax.all_to_all(
        summed.reshape(slot_count, owner_count, rows_dev, block_width),
        "dp",
        split_axis=1,
        concat_axis=1,
        tiled=True,
    )
    placed = jnp.einsum(
        "bk,krc->rbc",
        select,
        returned.reshape(slot_count * owner_count, rows_dev, block_width),
        preferred_element_type=jnp.float32,
    ).astype(jnp.bfloat16)
    whole_rows = placed.reshape(rows_dev, block_total * block_width)
    update = lax.dynamic_slice_in_dim(whole_rows, column_index * cols_dev, cols_dev, 1)
    return (update, new_stats, new_first, new_second)


def solution(mesh):
    placed = (
        P("dp", "tensor"),
        P("dp", None),
        P("dp"),
        P("dp", None, None, "tensor"),
        P("dp", None, None, "tensor"),
        P("dp", None, None, "tensor"),
        P("dp", None, None, "tensor"),
    )
    return jax.shard_map(
        on_device,
        mesh=mesh,
        in_specs=placed,
        out_specs=(
            P("dp", "tensor"),
            P("dp", None, None, "tensor"),
            P("dp", None, None, "tensor"),
            P("dp", None, None, "tensor"),
        ),
        check_vma=False,
    )
```

profile of v0, /device:TPU:6, one launch (start us, length us, event | category | flops | bytes accessed | tf_op | source)
XLA Modules:
  0.0 298.0 jit_solution(9805575470539748198)
XLA Ops:
  0.6 0.0 copy-start
  0.6 44.2 %all-gather = s32[64,1,2]{2,1,0:T(1,128)S(1)} all-gather(s32[1,1,2]{2,1,0:T(1,128)} %bitcast.78), channel_id=1, replica_groups=mesh['dp'=64,'tensor'=8] {'dp'}, dimensions={0}, use_global_device_ids=true | all-gather | bytes 520 | tf_op jit(solution)/shard_map/all_gather | solution.py:23
  44.8 0.1 copy.23
  44.9 0.1 reshape.55
  45.0 28.1 %all_gather.10 = bf16[8,53248]{1,0:T(8,128)(2,1)S(1)} all-gather(bf16[8,6656]{1,0:T(8,128)(2,1)} %param.7), channel_id=1, replica_groups=mesh['dp'=64,'tensor'=8] {'tensor'}, dimensions={1}, use_global_device_ids=true | all-gather | bytes 958464 | tf_op jit(solution)/shard_map/all_gather | solution.py:26
  73.1 0.7 gather_fusion
  73.8 0.3 broadcast_select_fusion
  74.1 0.2 copy.24
  74.4 59.2 %all_to_all.10 = bf16[2,64,8,1024]{3,2,0,1:T(8,128)(2,1)S(1)} all-to-all(bf16[2,64,8,1024]{3,2,0,1:T(8,128)(2,1)S(1)} %copy.24), channel_id=1, replica_groups=mesh['dp'=64,'tensor'=8] {'dp'}, dimensions={1} | all-to-all | bytes 4194304 | tf_op jit(solution)/shard_map/all_to_all | solution.py:31
  133.5 0.0 copy-start.1
  133.5 1.3 copy-done.1
  134.9 0.0 copy-done
  134.9 0.0 copy-start.2
  134.9 0.0 copy-start.3
  134.9 0.7 fusion.8
  135.6 0.0 copy-start.5
  135.6 0.8 copy-done.5
  136.4 0.0 copy-done.2
  136.4 0.0 copy-done.3
  136.4 2.7 fusion.6
  139.1 87.4 %all-reduce.2 = bf16[2,512,1024]{2,1,0:T(8,128)(2,1)S(1)} all-reduce(f32[2,512,1024]{2,1,0:T(8,128)} %fusion.6), channel_id=1, replica_groups=mesh['dp'=64,'tensor'=8] {'tensor'}, use_global_device_ids=true, to_apply=%region_0.1 | all-reduce | flops 1048576 | bytes 6291456 | tf_op jit(solution)/shard_map/psum | solution.py:59
  226.5 1.6 copy.26
  228.0 6.5 %all-to-all-start.1 = ((bf16[2,64,8,1024]{3,2,0,1:T(8,128)(2,1)}), bf16[2,64,8,1024]{3,2,0,1:T(8,128)(2,1)S(1)}, u32[]{:S(2)}, u32[]{:S(2)}) async-start(bf16[2,64,8,1024]{3,2,0,1:T(8,128)(2,1)} %copy.26), calls=%async_computation.1 | async-start | bytes 4194304 | tf_op jit(solution)/shard_map/all_to_all | solution.py:60
  235.2 1.3 dynamic-slice
  236.4 0.8 dynamic-update-slice
  237.2 52.5 %all-reduce = s32[64]{0:T(128)S(1)} all-reduce(s32[64]{0:T(128)S(1)} %dynamic-update-slice), channel_id=1, replica_groups=mesh['dp'=64,'tensor'=8] {'dp'}, use_global_device_ids=true, to_apply=%add | all-reduce | flops 64 | bytes 512
  289.7 0.1 lt.49
  289.8 0.1 eq.15
  289.9 0.0 copy-start.7
  289.9 1.9 copy.33
  291.8 0.0 copy-done.7
  291.8 0.0 copy-start.4
  291.8 0.0 copy-start.6
  291.8 2.0 fusion.2
  293.8 0.0 copy-done.4
  293.8 0.0 copy-done.6
  293.8 1.2 fusion.5
  295.0 0.0 all-to-all-done.1
  295.0 1.2 copy.27
  296.1 0.7 fusion.3
  296.8 0.5 copy.30
  297.3 0.7 constant_dynamic-slice_fusion
  (6 shorter events, 0.0 us)
Async XLA Ops:
  0.6 134.2 %copy-start = (bf16[1,2,1024,128]{3,2,1,0:T(8,128)(2,1)S(1)}, bf16[1,2,1024,128]{3,2,1,0:T(8,128)(2,1)}, u32[]{:S(2)}) copy-start(bf16[1,2,1024,128]{3,2,1,0:T(8,128)(2,1)} %param.11) | copy-start | bytes 1572868
  133.5 1.3 copy-start.1
  134.9 1.5 copy-start.2
  134.9 1.5 copy-start.3
  135.6 0.8 copy-start.5
  228.0 66.9 %all-to-all-start.1 = ((bf16[2,64,8,1024]{3,2,0,1:T(8,128)(2,1)}), bf16[2,64,8,1024]{3,2,0,1:T(8,128)(2,1)S(1)}, u32[]{:S(2)}, u32[]{:S(2)}) async-start(bf16[2,64,8,1024]{3,2,0,1:T(8,128)(2,1)} %copy.26), calls=%async_computation.1 | async-start | bytes 4194304 | tf_op jit(solution)/shard_map/all_to_all | solution.py:60
  289.9 1.9 copy-start.7
  291.8 2.0 copy-start.4
  291.8 2.0 copy-start.6
where the time goes:
time: 298 us
  blocking collectives  271 us (91%)
  local copies, waits for them, and re-layouts  11.1 us (4%)
  starting transfers between devices  6.46 us (2%)
  matrix products  6.11 us (2%)
    psum x1, blocking collectives, on_device(): summed = lax.psum(partial_update, 'tensor').astype(jnp.bfloat16)  87.4 us
    all_to_all x1, blocking collectives, on_device(): lax.all_to_all(outgoing, 'dp', split_axis=1, concat_axis=1, tiled=True)  59.2 us
    unnamed x1, blocking collectives  52.5 us
    all_gather x1, blocking collectives, on_device(): lax.all_gather(block_list, 'dp', axis=0, tiled=True)  44.2 us
    all_gather x1, blocking collectives, on_device(): full_rows = lax.all_gather(gradient, 'tensor', axis=1, tiled=True)  28.1 us
    all_to_all x1, starting transfers between devices, on_device(): lax.all_to_all(summed.reshape(slot_count, owner_count, rows_dev, block_wi...  6.46 us
  transfers between devices with their start and end apart: 1, of which 0 were waited for; matrix products, arithmetic and copies ran while one was open for 2% of the time, Pallas kernels for 0%

commit v1 on v0

v1 whole, which is shorter than its diff:
```python
import jax
import jax.numpy as jnp
from jax import lax
from jax.experimental import pallas as pl
from jax.experimental.pallas import tpu as pltpu
from jax.sharding import PartitionSpec as P

STEP = 10


beta_one = 0.9
beta_two = 0.95
beta_stat = 0.95
epsilon = 1e-08
bias_one = 1.0 - beta_one**STEP
bias_two = 1.0 - beta_two**STEP


def rows_kernel(grad_ref, basis_ref, first_ref, second_ref, rotated_ref, back_ref):
    parts, slots = basis_ref.shape[:2]
    for s in range(slots):
        grad = grad_ref[s]
        total = None
        for k in range(parts):
            basis = basis_ref[k, s]
            rotated = jnp.dot(grad, basis, preferred_element_type=jnp.float32)
            rotated_ref[k, s] = rotated
            moment_one = beta_one * first_ref[k, s] + (1.0 - beta_one) * rotated
            moment_two = (
                beta_two * second_ref[k, s].astype(jnp.float32) + (1.0 - beta_two) * rotated * rotated
            )
            direction = (
                moment_one / bias_one / (jnp.sqrt(moment_two / bias_two) + epsilon)
            ).astype(jnp.bfloat16)
            term = lax.dot_general(
                direction, basis, (((1,), (1,)), ((), ())), preferred_element_type=jnp.float32
            )
            total = term if total is None else total + term
        back_ref[s] = total.astype(back_ref.dtype)


def on_device(gradient, block_list, block_counts, stats, basis, first_moment, second_moment):
    rows_dev, cols_dev = gradient.shape
    slot_count = block_list.shape[1]
    owners = lax.axis_size("dp")
    parts = lax.axis_size("tensor")
    width = stats.shape[2]
    part = stats.shape[3]
    blocks = cols_dev * parts // width

    mine = jnp.concatenate([block_list, block_counts[:, None]], axis=1)
    table = lax.all_to_all(
        jnp.broadcast_to(mine, (owners, slot_count + 1)), "dp", 0, 0, tiled=True
    )
    lists = table[:, :slot_count]
    live = jnp.arange(slot_count)[None, :] < table[:, slot_count:]

    basis_all = lax.all_gather(basis[0], "tensor", axis=0, tiled=False)

    def to_rows(x):
        y = x.reshape(slot_count, owners, parts, part).transpose(2, 0, 1, 3)
        return lax.all_to_all(y, "tensor", 0, 0, tiled=True)

    first_rows = to_rows(first_moment[0])
    second_rows = to_rows(second_moment[0])

    row = lax.all_to_all(
        gradient.reshape(rows_dev, cols_dev // part, part), "tensor", 0, 0, tiled=True
    )
    by_block = row.reshape(blocks, width // part, part)
    outgoing = jnp.take(by_block, lists, axis=0, mode="clip")
    arrived = lax.all_to_all(outgoing, "dp", 0, 0, tiled=True)
    grad_rows = arrived.transpose(1, 0, 2, 3).reshape(slot_count, owners, width)

    rotated, back = pl.pallas_call(
        rows_kernel,
        out_shape=(
            jax.ShapeDtypeStruct(first_rows.shape, jnp.float32),
            jax.ShapeDtypeStruct(grad_rows.shape, jnp.bfloat16),
        ),
        compiler_params=pltpu.CompilerParams(vmem_limit_bytes=48 * 2**20),
        name="rotate_rows",
    )(grad_rows, basis_all, first_rows, second_rows)

    back_out = back.reshape(slot_count, owners, width // part, part).transpose(1, 0, 2, 3)
    returned = lax.all_to_all(back_out, "dp", 0, 0, tiled=True)
    holds = (lists.reshape(-1)[None, :] == jnp.arange(blocks)[:, None]) & live.reshape(-1)[None, :]
    place = jnp.argmax(holds, axis=1)
    placed = jnp.take(
        returned.reshape(owners * slot_count, width // part, part), place, axis=0, mode="clip"
    )
    update = lax.all_to_all(
        placed.reshape(parts, cols_dev // part, part), "tensor", 0, 0, tiled=True
    ).reshape(rows_dev, cols_dev)

    live_here = (jnp.arange(slot_count) < block_counts[0])[:, None, None]
    rotated_cols = (
        lax.all_to_all(rotated, "tensor", 0, 0, tiled=True)
        .transpose(1, 2, 0, 3)
        .reshape(slot_count, owners * parts, part)
    )
    moment_one = beta_one * first_moment[0] + (1.0 - beta_one) * rotated_cols
    moment_two = beta_two * second_moment[0] + (1.0 - beta_two) * rotated_cols * rotated_cols
    grad_all = lax.all_gather(grad_rows, "tensor", axis=1, tiled=True)
    grad_cols = lax.dynamic_slice_in_dim(grad_all, lax.axis_index("tensor") * part, part, 2)
    gram = jnp.einsum("srb,src->sbc", grad_all, grad_cols, preferred_element_type=jnp.float32)
    new_stat = beta_stat * stats[0] + (1.0 - beta_stat) * gram
    new_stats = jnp.where(live_here, new_stat, stats[0])[None]
    new_first = jnp.where(live_here, moment_one, first_moment[0])[None]
    new_second = jnp.where(live_here, moment_two, second_moment[0])[None]
    return (update, new_stats, new_first, new_second)


def solution(mesh):
    placed = (
        P("dp", "tensor"),
        P("dp", None),
        P("dp"),
        P("dp", None, None, "tensor"),
        P("dp", None, None, "tensor"),
        P("dp", None, None, "tensor"),
        P("dp", None, None, "tensor"),
    )
    return jax.shard_map(
        on_device,
        mesh=mesh,
        in_specs=placed,
        out_specs=(
            P("dp", "tensor"),
            P("dp", None, None, "tensor"),
            P("dp", None, None, "tensor"),
            P("dp", None, None, "tensor"),
        ),
        check_vma=False,
    )
```

time: 298 us -> 186 us (0.62); the launches traced: 298 us -> 182 us
  blocking collectives: 271 us -> 28.9 us
  waiting for transfers between devices: 0.01 us -> 76.8 us
  starting transfers between devices: 6.46 us -> 40.8 us
  between operations: 1.41 us -> 14.8 us
  Pallas kernels: 0 us -> 6.54 us
  local copies, waits for them, and re-layouts: 11.1 us -> 8.08 us
    psum x1 -> x0, blocking collectives: 87.4 us -> none  [on_device(): summed = lax.psum(partial_update, 'tensor').astype(jnp.bfloat16)]
    all_to_all x1 -> x6, waiting for transfers between devices: 0.01 us -> 76.1 us  [the longest x2 36.9 us: to_rows(): return lax.all_to_all(y, 'tensor', 0, 0, tiled=True)]
    all_gather x2 -> x0, blocking collectives: 72.3 us -> none  [the longest x1 44.2 us: on_device(): lax.all_gather(block_list, 'dp', axis=0, tiled=True)]
    unnamed x1 -> x0, blocking collectives: 52.5 us -> none
    all_to_all x1 -> x6, starting transfers between devices: 6.46 us -> 40.7 us  [the longest x1 13.8 us: on_device(): lax.all_to_all(jnp.broadcast_to(mine, (owners, slot_count + 1)), 'dp', 0,...]
    all_to_all x1 -> x2, blocking collectives: 59.2 us -> 28.9 us  [the longest x1 17.6 us: on_device(): arrived = lax.all_to_all(outgoing, 'dp', 0, 0, tiled=True)]
    pallas_call x0 -> x1, Pallas kernels: none -> 6.54 us  [on_device(): pl.pallas_call(rows_kernel, out_shape=(jax.ShapeDtypeStruct(first_rows.sh...]
    unnamed x20 -> x10, local copies, waits for them, and re-layouts: 4.64 us -> 0.72 us
  transfers between devices with their start and end apart: 1 -> 8, of which waited for: 0 -> 6; matrix products, arithmetic and copies ran while one was open for 2% -> 7% of each run, Pallas kernels for 0% -> 4%
where the time goes in v1:
time: 186 us; the launch traced here: 182 us
  waiting for transfers between devices  76.8 us (41%)
  starting transfers between devices  40.8 us (22%)
  blocking collectives  28.9 us (16%)
  between operations  14.8 us (8%)
  local copies, waits for them, and re-layouts  8.08 us (4%)
  Pallas kernels  6.54 us (4%)
  matrix products  3.53 us (2%)
  other arithmetic  2.86 us (2%)
    all_to_all x2, waiting for transfers between devices, to_rows(): return lax.all_to_all(y, 'tensor', 0, 0, tiled=True)  36.9 us
    all_to_all x1, blocking collectives, on_device(): arrived = lax.all_to_all(outgoing, 'dp', 0, 0, tiled=True)  17.6 us
    all_to_all x1, starting transfers between devices, on_device(): lax.all_to_all(jnp.broadcast_to(mine, (owners, slot_count + 1)), 'dp', 0,...  13.8 us
    all_to_all x1, waiting for transfers between devices, on_device(): lax.all_to_all(rotated, 'tensor', 0, 0, tiled=True).transpose(1, 2, 0, 3)  11.4 us
    all_to_all x1, blocking collectives, on_device(): lax.all_to_all(placed.reshape(parts, cols_dev // part, part), 'tensor', 0...  11.3 us
    all_to_all x1, waiting for transfers between devices, on_device(): returned = lax.all_to_all(back_out, 'dp', 0, 0, tiled=True)  11.2 us
    all_to_all x1, waiting for transfers between devices, on_device(): lax.all_to_all(gradient.reshape(rows_dev, cols_dev // part, part), 'tenso...  10.4 us
    all_to_all x1, starting transfers between devices, on_device(): returned = lax.all_to_all(back_out, 'dp', 0, 0, tiled=True)  9.34 us
  transfers between devices with their start and end apart: 8, of which 6 were waited for; matrix products, arithmetic and copies ran while one was open for 7% of the time, Pallas kernels for 4%

profile of v1, /device:TPU:6, one launch (start us, length us, event | category | flops | bytes accessed | tf_op | source)
XLA Modules:
  0.0 182.3 jit_solution(7258608583644681936)
XLA Ops:
  7.2 0.0 copy-start.1
  7.2 0.0 all-gather.3.cloned.1.call-start
  7.2 0.7 all-gather.3.cloned.1.call-update
  8.6 0.7 add_bitcast_fusion
  9.3 0.6 broadcast_in_dim.44
  9.9 13.8 %all-to-all-start.1 = ((s32[64,1,3]{2,1,0:T(1,128)}), s32[64,1,3]{2,1,0:T(1,128)S(1)}, u32[]{:S(2)}, u32[]{:S(2)}) async-start(s32[64,1,3]{2,1,0:T(1,128)} %broadcast_in_dim.44), calls=%async_computation.1 | async-start | bytes 65536 | tf_op jit(solution)/shard_map/all_to_all | solution.py:52
  23.7 1.6 copy.38
  25.3 6.2 %all-to-all-done.1 = s32[64,1,3]{2,1,0:T(1,128)S(1)} async-done(((s32[64,1,3]{2,1,0:T(1,128)}), s32[64,1,3]{2,1,0:T(1,128)S(1)}, u32[]{:S(2)}, u32[]{:S(2)}) %all-to-all-start.1) | async-done | bytes 800 | tf_op jit(solution)/shard_map/all_to_all | solution.py:52
  31.5 7.1 %all-to-all-start = ((bf16[8,52,128]{2,1,0:T(8,128)(2,1)}), bf16[8,52,128]{2,1,0:T(8,128)(2,1)S(1)}, u32[]{:S(2)}, u32[]{:S(2)}) async-start(bf16[8,52,128]{2,1,0:T(8,128)(2,1)} %copy.38), calls=%async_computation | async-start | bytes 229376 | tf_op jit(solution)/shard_map/all_to_all | solution.py:67
  38.6 0.0 all-gather.5.cloned.1.call-start
  38.7 0.1 reshape.96
  38.8 10.4 %all-to-all-done = bf16[8,52,128]{2,1,0:T(8,128)(2,1)S(1)} async-done(((bf16[8,52,128]{2,1,0:T(8,128)(2,1)}), bf16[8,52,128]{2,1,0:T(8,128)(2,1)S(1)}, u32[]{:S(2)}, u32[]{:S(2)}) %all-to-all-start) | async-done | bytes 106528 | tf_op jit(solution)/shard_map/all_to_all | solution.py:67
  49.2 0.7 gather_fusion
  49.9 0.0 copy-start.2
  49.9 17.6 %all_to_all.44 = bf16[64,2,8,128]{3,2,1,0:T(8,128)(2,1)S(1)} all-to-all(bf16[64,2,8,128]{3,2,1,0:T(8,128)(2,1)S(1)} %bitcast.58), channel_id=1, replica_groups=mesh['dp'=64,'tensor'=8] {'dp'}, dimensions={0} | all-to-all | bytes 524288 | tf_op jit(solution)/shard_map/all_to_all | solution.py:72
  67.5 0.1 reshape.113
  67.6 0.8 copy.44.grad_ref
  68.4 0.0 all-gather.5.cloned.1.call-update
  68.4 0.0 copy-done.1
  68.4 0.0 copy-start
  68.4 0.9 copy.54
  69.3 3.5 %all-to-all-start.3 = ((f32[8,2,64,128]{3,2,1,0:T(8,128)}), f32[8,2,64,128]{3,2,1,0:T(8,128)S(1)}, u32[]{:S(2)}, u32[]{:S(2)}) async-start(f32[8,2,64,128]{3,2,1,0:T(8,128)} %bitcast.47), calls=%async_computation.3 | async-start | bytes 1048576 | tf_op jit(solution)/shard_map/all_to_all | solution.py:62
  72.8 0.0 copy-done.2
  72.8 0.9 copy.53
  73.7 15.9 %all-to-all-done.3.first_ref = f32[8,2,64,128]{3,2,1,0:T(8,128)S(1)} async-done(((f32[8,2,64,128]{3,2,1,0:T(8,128)}), f32[8,2,64,128]{3,2,1,0:T(8,128)S(1)}, u32[]{:S(2)}, u32[]{:S(2)}) %all-to-all-start.3) | async-done | bytes 524320 | tf_op jit(solution)/shard_map/all_to_all | solution.py:62
  89.6 3.5 %all-to-all-start.4 = ((f32[8,2,64,128]{3,2,1,0:T(8,128)}), f32[8,2,64,128]{3,2,1,0:T(8,128)S(1)}, u32[]{:S(2)}, u32[]{:S(2)}) async-start(f32[8,2,64,128]{3,2,1,0:T(8,128)} %bitcast.46), calls=%async_computation.4 | async-start | bytes 1048576 | tf_op jit(solution)/shard_map/all_to_all | solution.py:62
  93.1 0.2 slice_reduce_fusion
  93.3 21.0 %all-to-all-done.4.second_ref = f32[8,2,64,128]{3,2,1,0:T(8,128)S(1)} async-done(((f32[8,2,64,128]{3,2,1,0:T(8,128)}), f32[8,2,64,128]{3,2,1,0:T(8,128)S(1)}, u32[]{:S(2)}, u32[]{:S(2)}) %all-to-all-start.4) | async-done | bytes 524320 | tf_op jit(solution)/shard_map/all_to_all | solution.py:62
  114.3 0.0 all-gather.3.cloned.1.call-done.basis_ref
  114.3 0.0 copy-done
  114.3 6.5 %rotate_rows.1 = (f32[8,2,64,128]{3,2,1,0:T(8,128)}, bf16[2,64,1024]{2,1,0:T(8,128)(2,1)S(1)}) custom-call(bf16[2,64,1024]{2,1,0:T(8,128)(2,1)S(1)} %copy-done, bf16[8,2,1024,128]{3,2,1,0:T(8,128)(2,1)} %all-gather.3.cloned.1.call-done.basis_ref, f32[8,2,64,128]{3,2,1,0:T(8,128)S(1)} %all-to-all-done.3.first_ref, f32[8,2,64,128]{3,2,1,0:T(8,128)S(1)} %all-to-all-done.4.second_ref), custom_call_target="tpu_custom_call" | custom-call | tf_op jit(solution)/shard_map/rotate_rows/pallas_call | solution.py:75
  120.8 0.0 copy-start.3
  120.8 0.8 copy_bitcast_fusion.2
  121.6 9.3 %all-to-all-start.5 = ((bf16[64,2,8,128]{3,2,1,0:T(8,128)(2,1)}), bf16[64,2,8,128]{3,2,1,0:T(8,128)(2,1)S(1)}, u32[]{:S(2)}, u32[]{:S(2)}) async-start(bf16[64,2,8,128]{3,2,1,0:T(8,128)(2,1)} %copy_bitcast_fusion.2), calls=%async_computation.5 | async-start | bytes 524288 | tf_op jit(solution)/shard_map/all_to_all | solution.py:86
  130.9 0.1 iota_compare_fusion
  131.0 0.2 lt.41
  131.2 0.6 iota_reduce_fusion
  131.8 11.2 %all-to-all-done.5 = bf16[64,2,8,128]{3,2,1,0:T(8,128)(2,1)S(1)} async-done(((bf16[64,2,8,128]{3,2,1,0:T(8,128)(2,1)}), bf16[64,2,8,128]{3,2,1,0:T(8,128)(2,1)S(1)}, u32[]{:S(2)}, u32[]{:S(2)}) %all-to-all-start.5) | async-done | bytes 262176 | tf_op jit(solution)/shard_map/all_to_all | solution.py:86
  143.0 0.6 gather_fusion.1
  143.6 11.3 %all_to_all.45 = bf16[8,52,128]{2,1,0:T(8,128)(2,1)S(1)} all-to-all(bf16[8,52,128]{2,1,0:T(8,128)(2,1)S(1)} %reshape.91), channel_id=1, replica_groups=mesh['dp'=64,'tensor'=8] {'tensor'}, dimensions={0} | all-to-all | bytes 212992 | tf_op jit(solution)/shard_map/all_to_all | solution.py:92
  154.9 3.5 %all-to-all-start.7 = ((f32[8,2,64,128]{3,2,1,0:T(8,128)}), f32[8,2,64,128]{3,2,1,0:T(8,128)S(1)}, u32[]{:S(2)}, u32[]{:S(2)}) async-start(f32[8,2,64,128]{3,2,1,0:T(8,128)} %get-tuple-element.9), calls=%async_computation.7 | async-start | bytes 1048576 | tf_op jit(solution)/shard_map/all_to_all | solution.py:98
  158.4 0.0 all-gather.5.cloned.1.call-done
  158.5 0.0 copy-done.3
  158.5 3.5 %fusion.2 = f32[1,2,1024,128]{3,2,1,0:T(8,128)} fusion(bf16[2,512,1024]{2,1,0:T(8,128)(2,1)} %all-gather.5.cloned.1.call-done, f32[1,2,1024,128]{3,2,1,0:T(8,128)S(1)} %copy-done.3, pred[2]{0:T(512)(128)(4,1)S(1)} %iota_compare_fusion.2, s32[]{:T(128)S(6)} %select_n.20), kind=kOutput, calls=%fused_computation.5 | convolution fusion | flops 269484032 | bytes 4456454 | tf_op jit(solution)/shard_map/srb,src->sbc/dot_general | solution.py:106
  162.0 0.7 copy.55
  162.6 11.4 %all-to-all-done.7 = f32[8,2,64,128]{3,2,1,0:T(8,128)S(1)} async-done(((f32[8,2,64,128]{3,2,1,0:T(8,128)}), f32[8,2,64,128]{3,2,1,0:T(8,128)S(1)}, u32[]{:S(2)}, u32[]{:S(2)}) %all-to-all-start.7) | async-done | bytes 524320 | tf_op jit(solution)/shard_map/all_to_all | solution.py:98
  174.1 1.4 fusion.4
  (6 shorter events, 0.1 us)
Async XLA Ops:
  7.2 61.2 %copy-start.1 = (f32[1,2,512,128]{3,2,1,0:T(8,128)S(1)}, f32[1,2,512,128]{3,2,1,0:T(8,128)}, u32[]{:S(2)}) copy-start(f32[1,2,512,128]{3,2,1,0:T(8,128)} %param.12) | copy-start | bytes 1572868
  7.2 107.1 %all-gather.3.cloned.1.call-start = ((), (), s32[]{:S(2)}) async-start(), calls=%async_computation.8 | async-start | bytes 4718592 | tf_op jit(solution)/shard_map/all_gather | solution.py:58
  9.9 21.6 %all-to-all-start.1 = ((s32[64,1,3]{2,1,0:T(1,128)}), s32[64,1,3]{2,1,0:T(1,128)S(1)}, u32[]{:S(2)}, u32[]{:S(2)}) async-start(s32[64,1,3]{2,1,0:T(1,128)} %broadcast_in_dim.44), calls=%async_computation.1 | async-start | bytes 65536 | tf_op jit(solution)/shard_map/all_to_all | solution.py:52
  31.5 17.7 %all-to-all-start = ((bf16[8,52,128]{2,1,0:T(8,128)(2,1)}), bf16[8,52,128]{2,1,0:T(8,128)(2,1)S(1)}, u32[]{:S(2)}, u32[]{:S(2)}) async-start(bf16[8,52,128]{2,1,0:T(8,128)(2,1)} %copy.38), calls=%async_computation | async-start | bytes 229376 | tf_op jit(solution)/shard_map/all_to_all | solution.py:67
  38.6 119.8 %all-gather.5.cloned.1.call-start = ((), (), s32[]{:S(2)}) async-start(), calls=%async_computation.9 | async-start | bytes 2359296 | tf_op jit(solution)/shard_map/all_gather | solution.py:104
  49.9 22.9 %copy-start.2 = (f32[1,2,512,128]{3,2,1,0:T(8,128)S(1)}, f32[1,2,512,128]{3,2,1,0:T(8,128)}, u32[]{:S(2)}) copy-start(f32[1,2,512,128]{3,2,1,0:T(8,128)} %param.13) | copy-start | bytes 1572868
  68.4 45.9 %copy-start = (bf16[2,64,1024]{2,1,0:T(8,128)(2,1)S(1)}, bf16[2,64,1024]{2,1,0:T(8,128)(2,1)}, u32[]{:S(2)}) copy-start(bf16[2,64,1024]{2,1,0:T(8,128)(2,1)} %copy.44.grad_ref) | copy-start | bytes 786436
  69.3 20.3 %all-to-all-start.3 = ((f32[8,2,64,128]{3,2,1,0:T(8,128)}), f32[8,2,64,128]{3,2,1,0:T(8,128)S(1)}, u32[]{:S(2)}, u32[]{:S(2)}) async-start(f32[8,2,64,128]{3,2,1,0:T(8,128)} %bitcast.47), calls=%async_computation.3 | async-start | bytes 1048576 | tf_op jit(solution)/shard_map/all_to_all | solution.py:62
  89.6 24.7 %all-to-all-start.4 = ((f32[8,2,64,128]{3,2,1,0:T(8,128)}), f32[8,2,64,128]{3,2,1,0:T(8,128)S(1)}, u32[]{:S(2)}, u32[]{:S(2)}) async-start(f32[8,2,64,128]{3,2,1,0:T(8,128)} %bitcast.46), calls=%async_computation.4 | async-start | bytes 1048576 | tf_op jit(solution)/shard_map/all_to_all | solution.py:62
  120.8 37.7 %copy-start.3 = (f32[1,2,1024,128]{3,2,1,0:T(8,128)S(1)}, f32[1,2,1024,128]{3,2,1,0:T(8,128)}, u32[]{:S(2)}) copy-start(f32[1,2,1024,128]{3,2,1,0:T(8,128)} %param.10) | copy-start | bytes 3145732
  121.6 21.4 %all-to-all-start.5 = ((bf16[64,2,8,128]{3,2,1,0:T(8,128)(2,1)}), bf16[64,2,8,128]{3,2,1,0:T(8,128)(2,1)S(1)}, u32[]{:S(2)}, u32[]{:S(2)}) async-start(bf16[64,2,8,128]{3,2,1,0:T(8,128)(2,1)} %copy_bitcast_fusion.2), calls=%async_computation.5 | async-start | bytes 524288 | tf_op jit(solution)/shard_map/all_to_all | solution.py:86
  154.9 19.2 %all-to-all-start.7 = ((f32[8,2,64,128]{3,2,1,0:T(8,128)}), f32[8,2,64,128]{3,2,1,0:T(8,128)S(1)}, u32[]{:S(2)}, u32[]{:S(2)}) async-start(f32[8,2,64,128]{3,2,1,0:T(8,128)} %get-tuple-element.9), calls=%async_computation.7 | async-start | bytes 1048576 | tf_op jit(solution)/shard_map/all_to_all | solution.py:98
Sparse Core Ops, SparseCore 0:
  10.1 64.1 all-gather.2
  77.0 54.5 all-gather.4

commit v2 on v1

v2 whole, which is shorter than its diff:
```python
import jax
import jax.numpy as jnp
from jax import lax
from jax.experimental import pallas as pl
from jax.experimental.pallas import tpu as pltpu
from jax.sharding import PartitionSpec as P

STEP = 10


beta_one = 0.9
beta_two = 0.95
beta_stat = 0.95
epsilon = 1e-08
bias_one = 1.0 - beta_one**STEP
bias_two = 1.0 - beta_two**STEP


def rows_kernel(grad_ref, basis_ref, moved_ref, back_ref):
    parts, slots = basis_ref.shape[:2]
    rows = grad_ref.shape[1]
    for s in range(slots):
        grad = grad_ref[s]
        total = None
        for k in range(parts):
            basis = basis_ref[k, s]
            rotated = jnp.dot(grad, basis, preferred_element_type=jnp.float32)
            first_high, first_low, second = (
                moved_ref[k, pl.ds((i * slots + s) * rows, rows), :].astype(jnp.float32)
                for i in range(3)
            )
            moment_one = beta_one * (first_high + first_low) + (1.0 - beta_one) * rotated
            moment_two = beta_two * second + (1.0 - beta_two) * rotated * rotated
            direction = (
                moment_one / bias_one / (jnp.sqrt(moment_two / bias_two) + epsilon)
            ).astype(jnp.bfloat16)
            term = lax.dot_general(
                direction, basis, (((1,), (1,)), ((), ())), preferred_element_type=jnp.float32
            )
            total = term if total is None else total + term
        back_ref[s] = total.astype(back_ref.dtype)


def state_kernel(
    count_ref, grad_ref, basis_ref, stats_ref, first_ref, second_ref,
    new_stats_ref, new_first_ref, new_second_ref,
):
    parts, slots, rows, width = grad_ref.shape
    part = basis_ref.shape[2]
    start = pl.multiple_of(lax.axis_index("tensor") * part, part)
    for s in range(slots):
        live = s < count_ref[0]
        grad = grad_ref[:, s].reshape(parts * rows, width)
        grad_cols = grad_ref[:, s, :, pl.ds(start, part)].reshape(parts * rows, part)
        gram = lax.dot_general(
            grad, grad_cols, (((0,), (0,)), ((), ())), preferred_element_type=jnp.float32
        )
        stats = stats_ref[s]
        new_stats_ref[s] = jnp.where(live, beta_stat * stats + (1.0 - beta_stat) * gram, stats)
        rotated_all = jnp.dot(grad, basis_ref[s], preferred_element_type=jnp.float32)
        for t in range(parts):
            rotated = rotated_all[t * rows : (t + 1) * rows]
            here = pl.ds(t, rows, stride=parts)
            first = first_ref[s, here, :]
            second = second_ref[s, here, :]
            new_first_ref[s, here, :] = jnp.where(
                live, beta_one * first + (1.0 - beta_one) * rotated, first
            )
            new_second_ref[s, here, :] = jnp.where(
                live, beta_two * second + (1.0 - beta_two) * rotated * rotated, second
            )


def on_device(gradient, block_list, block_counts, stats, basis, first_moment, second_moment):
    rows_dev, cols_dev = gradient.shape
    slot_count = block_list.shape[1]
    owners = lax.axis_size("dp")
    parts = lax.axis_size("tensor")
    width = stats.shape[2]
    part = stats.shape[3]
    blocks = cols_dev * parts // width

    basis_all = lax.all_gather(basis[0], "tensor", axis=0, tiled=False)

    mine = jnp.concatenate([block_list[0], block_counts])
    is_me = jnp.arange(owners)[:, None] == lax.axis_index("dp")
    table = lax.psum(jnp.where(is_me, mine[None, :], 0), "dp")
    lists = table[:, :slot_count]
    live = jnp.arange(slot_count)[None, :] < table[:, slot_count:]

    def rows_of(x):
        return x.reshape(slot_count, owners, parts, part).transpose(2, 0, 1, 3).reshape(
            parts, slot_count * owners, part
        )

    first = rows_of(first_moment[0])
    first_high = first.astype(jnp.bfloat16)
    first_low = (first - first_high.astype(jnp.float32)).astype(jnp.bfloat16)
    second_high = rows_of(second_moment[0]).astype(jnp.bfloat16)
    sent = jnp.concatenate(
        [first_high, first_low, second_high, gradient.reshape(rows_dev, cols_dev // part, part)],
        axis=1,
    )
    moved = lax.all_to_all(sent, "tensor", 0, 0, tiled=True)
    by_block = moved[:, 3 * slot_count * owners :].reshape(blocks, width // part, part)

    outgoing = jnp.take(by_block, lists, axis=0, mode="clip")
    arrived = lax.all_to_all(outgoing, "dp", 0, 0, tiled=True)
    grad_rows = arrived.transpose(1, 0, 2, 3).reshape(slot_count, owners, width)

    back = pl.pallas_call(
        rows_kernel,
        out_shape=jax.ShapeDtypeStruct(grad_rows.shape, jnp.bfloat16),
        compiler_params=pltpu.CompilerParams(vmem_limit_bytes=48 * 2**20),
        name="rotate_rows",
    )(grad_rows, basis_all, moved)

    back_out = back.reshape(slot_count, owners, width // part, part).transpose(1, 0, 2, 3)
    returned = lax.all_to_all(back_out, "dp", 0, 0, tiled=True)
    holds = (lists.reshape(-1)[None, :] == jnp.arange(blocks)[:, None]) & live.reshape(-1)[None, :]
    place = jnp.argmax(holds, axis=1)
    placed = jnp.take(
        returned.reshape(owners * slot_count, width // part, part), place, axis=0, mode="clip"
    )
    update = lax.all_to_all(
        placed.reshape(parts, cols_dev // part, part), "tensor", 0, 0, tiled=True
    ).reshape(rows_dev, cols_dev)

    grad_all = lax.all_gather(grad_rows, "tensor", axis=0, tiled=False)
    vmem = pl.BlockSpec(memory_space=pltpu.VMEM)
    new_stats, new_first, new_second = pl.pallas_call(
        state_kernel,
        out_shape=(
            jax.ShapeDtypeStruct(stats.shape[1:], jnp.float32),
            jax.ShapeDtypeStruct(first_moment.shape[1:], jnp.float32),
            jax.ShapeDtypeStruct(second_moment.shape[1:], jnp.float32),
        ),
        in_specs=[pl.BlockSpec(memory_space=pltpu.SMEM)] + [vmem] * 5,
        out_specs=(vmem,) * 3,
        compiler_params=pltpu.CompilerParams(vmem_limit_bytes=48 * 2**20),
        name="new_state",
    )(block_counts, grad_all, basis[0], stats[0], first_moment[0], second_moment[0])
    return (update, new_stats[None], new_first[None], new_second[None])


def solution(mesh):
    placed = (
        P("dp", "tensor"),
        P("dp", None),
        P("dp"),
        P("dp", None, None, "tensor"),
        P("dp", None, None, "tensor"),
        P("dp", None, None, "tensor"),
        P("dp", None, None, "tensor"),
    )
    return jax.shard_map(
        on_device,
        mesh=mesh,
        in_specs=placed,
        out_specs=(
            P("dp", "tensor"),
            P("dp", None, None, "tensor"),
            P("dp", None, None, "tensor"),
            P("dp", None, None, "tensor"),
        ),
        check_vma=False,
    )
```

time: 186 us -> 143 us (0.77); the launches traced: 182 us -> 142 us
  waiting for transfers between devices: 76.8 us -> 29.7 us
  blocking collectives: 28.9 us -> 53.7 us
  starting transfers between devices: 40.8 us -> 25.5 us
  matrix products: 3.53 us -> 0 us
    all_to_all x5 -> x2, waiting for transfers between devices: 64.9 us -> 4.4 us  [the longest x1 4.4 us: on_device(): moved = lax.all_to_all(sent, 'tensor', 0, 0, tiled=True)]
    psum x0 -> x1, blocking collectives: none -> 25 us  [on_device(): table = lax.psum(jnp.where(is_me, mine[None, :], 0), 'dp')]
    all_to_all x5 -> x2, starting transfers between devices: 31.4 us -> 11.6 us  [the longest x1 7.1 us: on_device(): moved = lax.all_to_all(sent, 'tensor', 0, 0, tiled=True)]
    all_gather x1, waiting for transfers between devices: 0.02 us -> 11.6 us  [on_device(): grad_all = lax.all_gather(grad_rows, 'tensor', axis=0, tiled=False)]
    all_to_all x1 -> x0, blocking collectives: 11.3 us -> none  [on_device(): lax.all_to_all(placed.reshape(parts, cols_dev // part, part), 'tensor', 0...]
    all_to_all x1, blocking collectives: 17.6 us -> 28.7 us  [on_device(): arrived = lax.all_to_all(outgoing, 'dp', 0, 0, tiled=True)]
    all_to_all x1, starting transfers between devices: 9.34 us -> 13.8 us  [on_device(): returned = lax.all_to_all(back_out, 'dp', 0, 0, tiled=True)]
    unnamed x10 -> x18, local copies, waits for them, and re-layouts: 0.72 us -> 4.51 us
  transfers between devices with their start and end apart: 8 -> 5, of which waited for: 6 -> 4; matrix products, arithmetic and copies ran while one was open for 7% -> 5% of each run, Pallas kernels for 4% -> 5%
where the time goes in v2:
time: 143 us; the launch traced here: 142 us
  blocking collectives  53.7 us (38%)
  waiting for transfers between devices  29.7 us (21%)
  starting transfers between devices  25.5 us (18%)
  between operations  14.9 us (10%)
  local copies, waits for them, and re-layouts  9.82 us (7%)
  Pallas kernels  6.51 us (5%)
  other arithmetic  1.98 us (1%)
    all_to_all x1, blocking collectives, on_device(): arrived = lax.all_to_all(outgoing, 'dp', 0, 0, tiled=True)  28.7 us
    psum x1, blocking collectives, on_device(): table = lax.psum(jnp.where(is_me, mine[None, :], 0), 'dp')  25 us
    all_to_all x1, starting transfers between devices, on_device(): returned = lax.all_to_all(back_out, 'dp', 0, 0, tiled=True)  13.8 us
    all_gather x1, waiting for transfers between devices, on_device(): grad_all = lax.all_gather(grad_rows, 'tensor', axis=0, tiled=False)  11.6 us
    all_to_all x1, waiting for transfers between devices, on_device(): returned = lax.all_to_all(back_out, 'dp', 0, 0, tiled=True)  11.1 us
    all_to_all x1, starting transfers between devices, on_device(): moved = lax.all_to_all(sent, 'tensor', 0, 0, tiled=True)  7.1 us
    all_to_all x1, starting transfers between devices, on_device(): lax.all_to_all(placed.reshape(parts, cols_dev // part, part), 'tensor', 0...  4.53 us
    unnamed x18, local copies, waits for them, and re-layouts  4.51 us
  transfers between devices with their start and end apart: 5, of which 4 were waited for; matrix products, arithmetic and copies ran while one was open for 5% of the time, Pallas kernels for 5%

profile of v2, /device:TPU:6, one launch (start us, length us, event | category | flops | bytes accessed | tf_op | source)
XLA Modules:
  0.0 142.1 jit_solution(4882225253002583619)
XLA Ops:
  7.2 0.0 copy-start.2
  7.2 0.0 copy-start.6
  7.2 0.0 all-gather.3.cloned.1.call-start
  7.2 0.7 all-gather.3.cloned.1.call-update
  7.9 1.1 copy.35
  9.1 0.0 copy-done.2
  9.2 0.0 copy-done.6
  9.2 0.1 fusion
  9.3 0.0 copy-start.7
  9.3 1.0 pad_maximum_fusion
  10.3 7.1 %all-to-all-start = ((bf16[8,436,128]{2,1,0:T(8,128)(2,1)}), bf16[8,436,128]{2,1,0:T(8,128)(2,1)S(1)}, u32[]{:S(2)}, u32[]{:S(2)}) async-start(bf16[8,436,128]{2,1,0:T(8,128)(2,1)} %pad_maximum_fusion), calls=%async_computation | async-start | bytes 1802240 | tf_op jit(solution)/shard_map/all_to_all | solution.py:104
  17.4 0.0 all-gather.5.cloned.1.call-start
  18.1 0.0 copy-done.7
  18.1 0.1 pad_add_fusion
  18.2 0.1 broadcast_select_fusion
  18.3 25.0 %psum.7 = s32[64,3]{0,1:T(4,128)S(1)} all-reduce(s32[64,3]{0,1:T(4,128)S(1)} %broadcast_select_fusion), channel_id=1, replica_groups=mesh['dp'=64,'tensor'=8] {'dp'}, use_global_device_ids=true, to_apply=%region_0.1 | all-reduce | flops 192 | bytes 1536 | tf_op jit(solution)/shard_map/psum | solution.py:87
  43.3 0.1 copy.38
  43.4 0.1 reshape.66
  43.5 4.4 %all-to-all-done.moved_ref = bf16[8,436,128]{2,1,0:T(8,128)(2,1)S(1)} async-done(((bf16[8,436,128]{2,1,0:T(8,128)(2,1)}), bf16[8,436,128]{2,1,0:T(8,128)(2,1)S(1)}, u32[]{:S(2)}, u32[]{:S(2)}) %all-to-all-start) | async-done | bytes 892960 | tf_op jit(solution)/shard_map/all_to_all | solution.py:104
  47.9 0.7 gather_fusion
  48.6 28.7 %all_to_all.20 = bf16[64,2,8,128]{3,2,1,0:T(8,128)(2,1)S(1)} all-to-all(bf16[64,2,8,128]{3,2,1,0:T(8,128)(2,1)S(1)} %bitcast.59), channel_id=1, replica_groups=mesh['dp'=64,'tensor'=8] {'dp'}, dimensions={0} | all-to-all | bytes 524288 | tf_op jit(solution)/shard_map/all_to_all | solution.py:108
  77.4 0.1 all_gather_reshape.3
  77.5 0.8 copy.41
  78.2 0.0 all-gather.5.cloned.1.call-update
  78.2 0.1 reshape.83
  78.4 1.9 %all-gather.3.cloned.1.call-done.basis_ref = bf16[8,2,1024,128]{3,2,1,0:T(8,128)(2,1)} async-done(((bf16[1,2,1024,128]{3,2,1,0:T(8,128)(2,1)}), bf16[8,2,1024,128]{3,2,1,0:T(8,128)(2,1)}) %all-gather.3.cloned.1.call-update) | async-done | bytes 4194320 | tf_op jit(solution)/shard_map/all_gather | solution.py:83
  80.2 0.0 copy-start
  80.2 2.2 %copy-done = bf16[8,2,1024,128]{3,2,1,0:T(8,128)(2,1)S(1)} copy-done((bf16[8,2,1024,128]{3,2,1,0:T(8,128)(2,1)S(1)}, bf16[8,2,1024,128]{3,2,1,0:T(8,128)(2,1)}, u32[]{:S(2)}) %copy-start) | copy-done | bytes 4194328
  82.4 3.7 %rotate_rows.1 = bf16[2,64,1024]{2,1,0:T(8,128)(2,1)S(1)} custom-call(bf16[2,64,1024]{2,1,0:T(8,128)(2,1)S(1)} %copy.42.grad_ref, bf16[8,2,1024,128]{3,2,1,0:T(8,128)(2,1)S(1)} %copy-done, bf16[8,436,128]{2,1,0:T(8,128)(2,1)S(1)} %all-to-all-done.moved_ref), custom_call_target="tpu_custom_call" | custom-call | tf_op jit(solution)/shard_map/rotate_rows/pallas_call | solution.py:111
  86.1 0.0 copy-start.3
  86.1 0.0 copy-start.4
  86.2 0.0 copy-start.5
  86.2 0.8 copy_bitcast_fusion
  87.0 13.8 %all-to-all-start.2 = ((bf16[64,2,8,128]{3,2,1,0:T(8,128)(2,1)}), bf16[64,2,8,128]{3,2,1,0:T(8,128)(2,1)S(1)}, u32[]{:S(2)}, u32[]{:S(2)}) async-start(bf16[64,2,8,128]{3,2,1,0:T(8,128)(2,1)} %copy_bitcast_fusion), calls=%async_computation.2 | async-start | bytes 524288 | tf_op jit(solution)/shard_map/all_to_all | solution.py:119
  100.8 0.1 iota_compare_fusion
  100.9 0.2 lt.28
  101.0 0.6 iota_reduce_fusion
  101.7 11.1 %all-to-all-done.2 = bf16[64,2,8,128]{3,2,1,0:T(8,128)(2,1)S(1)} async-done(((bf16[64,2,8,128]{3,2,1,0:T(8,128)(2,1)}), bf16[64,2,8,128]{3,2,1,0:T(8,128)(2,1)S(1)}, u32[]{:S(2)}, u32[]{:S(2)}) %all-to-all-start.2) | async-done | bytes 262176 | tf_op jit(solution)/shard_map/all_to_all | solution.py:119
  112.8 0.6 gather_fusion.1
  113.4 0.7 reshape.62
  114.0 4.5 %all-to-all-start.3 = ((bf16[8,52,128]{2,1,0:T(8,128)(2,1)}), bf16[8,52,128]{2,1,0:T(8,128)(2,1)S(1)}, u32[]{:S(2)}, u32[]{:S(2)}) async-start(bf16[8,52,128]{2,1,0:T(8,128)(2,1)} %reshape.62), calls=%async_computation.3 | async-start | bytes 229376 | tf_op jit(solution)/shard_map/all_to_all | solution.py:125
  118.6 11.6 %all-gather.5.cloned.1.call-done.grad_ref = bf16[8,2,64,1024]{3,2,1,0:T(8,128)(2,1)} async-done(((bf16[1,2,64,1024]{3,2,1,0:T(8,128)(2,1)}), bf16[8,2,64,1024]{3,2,1,0:T(8,128)(2,1)}) %all-gather.5.cloned.1.call-update) | async-done | bytes 2097168 | tf_op jit(solution)/shard_map/all_gather | solution.py:129
  130.2 0.0 copy-done.3
  130.2 0.0 copy-done.4
  130.2 0.0 copy-done.5
  130.2 0.0 copy-start.1
  130.2 1.6 %copy-done.1 = bf16[8,2,64,1024]{3,2,1,0:T(8,128)(2,1)S(1)} copy-done((bf16[8,2,64,1024]{3,2,1,0:T(8,128)(2,1)S(1)}, bf16[8,2,64,1024]{3,2,1,0:T(8,128)(2,1)}, u32[]{:S(2)}) %copy-start.1) | copy-done | bytes 2097176
  131.8 2.8 %new_state.1 = (f32[2,1024,128]{2,1,0:T(8,128)}, f32[2,512,128]{2,1,0:T(8,128)}, f32[2,512,128]{2,1,0:T(8,128)}) custom-call(s32[1]{0:T(128)S(6)} %copy.48.count_ref, bf16[8,2,64,1024]{3,2,1,0:T(8,128)(2,1)S(1)} %copy-done.1, bf16[2,1024,128]{2,1,0:T(8,128)(2,1)S(1)} %bitcast.53, f32[2,1024,128]{2,1,0:T(8,128)S(1)} %bitcast.54, f32[2,512,128]{2,1,0:T(8,128)S(1)} %bitcast.52, ...), custom_call_target="tpu_custom_call" | custom-call | tf_op jit(solution)/shard_map/new_state/pallas_call | solution.py:131
  134.6 0.0 all-to-all-done.3
  134.6 0.7 copy.47
  (12 shorter events, 0.3 us)
Async XLA Ops:
  7.2 1.9 %copy-start.2 = (f32[1,2,512,128]{3,2,1,0:T(8,128)S(1)}, f32[1,2,512,128]{3,2,1,0:T(8,128)}, u32[]{:S(2)}) copy-start(f32[1,2,512,128]{3,2,1,0:T(8,128)} %param.13) | copy-start | bytes 1572868
  7.2 2.0 %copy-start.6 = (bf16[8,6656]{1,0:T(8,128)(2,1)S(1)}, bf16[8,6656]{1,0:T(8,128)(2,1)}, u32[]{:S(2)}) copy-start(bf16[8,6656]{1,0:T(8,128)(2,1)} %param.7) | copy-start | bytes 319492
  7.2 73.0 %all-gather.3.cloned.1.call-start = ((), (), s32[]{:S(2)}) async-start(), calls=%async_computation.4 | async-start | bytes 4718592 | tf_op jit(solution)/shard_map/all_gather | solution.py:83
  9.3 8.8 %copy-start.7 = (s32[1,2]{1,0:T(1,128)S(1)}, s32[1,2]{1,0:T(1,128)}, u32[]{:S(2)}) copy-start(s32[1,2]{1,0:T(1,128)} %param.8) | copy-start | bytes 28
  10.3 37.6 %all-to-all-start = ((bf16[8,436,128]{2,1,0:T(8,128)(2,1)}), bf16[8,436,128]{2,1,0:T(8,128)(2,1)S(1)}, u32[]{:S(2)}, u32[]{:S(2)}) async-start(bf16[8,436,128]{2,1,0:T(8,128)(2,1)} %pad_maximum_fusion), calls=%async_computation | async-start | bytes 1802240 | tf_op jit(solution)/shard_map/all_to_all | solution.py:104
  17.4 112.8 %all-gather.5.cloned.1.call-start = ((), (), s32[]{:S(2)}) async-start(), calls=%async_computation.5 | async-start | bytes 2359296 | tf_op jit(solution)/shard_map/all_gather | solution.py:129
  80.2 2.2 %copy-start = (bf16[8,2,1024,128]{3,2,1,0:T(8,128)(2,1)S(1)}, bf16[8,2,1024,128]{3,2,1,0:T(8,128)(2,1)}, u32[]{:S(2)}) copy-start(bf16[8,2,1024,128]{3,2,1,0:T(8,128)(2,1)} %all-gather.3.cloned.1.call-done.basis_ref) | copy-start | bytes 12582916
  86.1 44.1 %copy-start.3 = (f32[1,2,512,128]{3,2,1,0:T(8,128)S(1)}, f32[1,2,512,128]{3,2,1,0:T(8,128)}, u32[]{:S(2)}) copy-start(f32[1,2,512,128]{3,2,1,0:T(8,128)} %param.12) | copy-start | bytes 1572868
  86.1 44.0 %copy-start.4 = (bf16[1,2,1024,128]{3,2,1,0:T(8,128)(2,1)S(1)}, bf16[1,2,1024,128]{3,2,1,0:T(8,128)(2,1)}, u32[]{:S(2)}) copy-start(bf16[1,2,1024,128]{3,2,1,0:T(8,128)(2,1)} %param.11) | copy-start | bytes 1572868
  86.2 44.0 %copy-start.5 = (f32[1,2,1024,128]{3,2,1,0:T(8,128)S(1)}, f32[1,2,1024,128]{3,2,1,0:T(8,128)}, u32[]{:S(2)}) copy-start(f32[1,2,1024,128]{3,2,1,0:T(8,128)} %param.10) | copy-start | bytes 3145732
  87.0 25.8 %all-to-all-start.2 = ((bf16[64,2,8,128]{3,2,1,0:T(8,128)(2,1)}), bf16[64,2,8,128]{3,2,1,0:T(8,128)(2,1)S(1)}, u32[]{:S(2)}, u32[]{:S(2)}) async-start(bf16[64,2,8,128]{3,2,1,0:T(8,128)(2,1)} %copy_bitcast_fusion), calls=%async_computation.2 | async-start | bytes 524288 | tf_op jit(solution)/shard_map/all_to_all | solution.py:119
  114.0 20.6 %all-to-all-start.3 = ((bf16[8,52,128]{2,1,0:T(8,128)(2,1)}), bf16[8,52,128]{2,1,0:T(8,128)(2,1)S(1)}, u32[]{:S(2)}, u32[]{:S(2)}) async-start(bf16[8,52,128]{2,1,0:T(8,128)(2,1)} %reshape.62), calls=%async_computation.3 | async-start | bytes 229376 | tf_op jit(solution)/shard_map/all_to_all | solution.py:125
  130.2 1.6 %copy-start.1 = (bf16[8,2,64,1024]{3,2,1,0:T(8,128)(2,1)S(1)}, bf16[8,2,64,1024]{3,2,1,0:T(8,128)(2,1)}, u32[]{:S(2)}) copy-start(bf16[8,2,64,1024]{3,2,1,0:T(8,128)(2,1)} %all-gather.5.cloned.1.call-done.grad_ref) | copy-start | bytes 6291460
Sparse Core Ops, SparseCore 0:
  10.1 70.0 all-gather.2
  82.9 47.2 all-gather.4

commit v3 on v2

v3 whole, which is shorter than its diff:
```python
import jax
import jax.numpy as jnp
from jax import lax
from jax.experimental import pallas as pl
from jax.experimental.pallas import tpu as pltpu
from jax.sharding import PartitionSpec as P

STEP = 10


beta_one = 0.9
beta_two = 0.95
beta_stat = 0.95
epsilon = 1e-08
bias_one = 1.0 - beta_one**STEP
bias_two = 1.0 - beta_two**STEP

GROUPS = 4


def shifted(x, parts, by):
    return lax.ppermute(x, "tensor", [((i + by) % parts, i) for i in range(parts)])


def pack_kernel(share, after_ref, basis_ref, first_ref, second_ref, to_left_ref, to_right_ref):
    slots, width, _ = basis_ref.shape
    rows = first_ref.shape[1]
    owners = rows // (GROUPS * share)
    me = lax.axis_index("tensor") + GROUPS
    piece = 4 * share * owners

    def put(ref, at, target, s):
        base = lax.rem(target, GROUPS) * share
        for i, source in enumerate((first_ref, second_ref)):
            for r in range(share):
                x = source[s, pl.ds(base + r, owners, stride=GROUPS * share), :]
                high = x.astype(jnp.bfloat16)
                low = (x - high.astype(jnp.float32)).astype(jnp.bfloat16)
                here = at + (2 * i * share + r) * owners
                ref[pl.ds(here, owners), :] = high
                ref[pl.ds(here + share * owners, owners), :] = low

    for ref, far, step in ((to_left_ref, 0, -1), (to_right_ref, 1, 1)):
        ref[pl.ds(0, width), :] = basis_ref[far]
        put(ref, width, me + 2 * step, far)
        ref[pl.ds(width + piece, width), :] = basis_ref[1 - far]
        for s in range(slots):
            put(ref, 2 * width + (1 + s) * piece, me + step, s)


def rows_kernel(
    share, arrived_ref, basis_ref, first_ref, second_ref, right_ref, left_ref, far_right_ref,
    far_left_ref, grad_ref, back_ref, rotated_ref, direction_ref, spread_ref,
):
    slots, rows, width = grad_ref.shape
    part = basis_ref.shape[2]
    pieces = width // part
    owners = rows // share
    base = lax.rem(lax.axis_index("tensor"), GROUPS) * share
    piece = 4 * share * owners
    for s in range(slots):
        far_ref = (far_right_ref, far_left_ref)[s]
        near = 2 * width + (1 + s) * piece
        sources = (
            (right_ref, (0, width + piece)[s], near),
            (left_ref, (width + piece, 0)[s], near),
            (far_ref, 0, width),
        )
        basis = jnp.concatenate(
            [basis_ref[s]] + [ref[pl.ds(at, width), :] for ref, at, _ in sources], axis=1
        )
        spread_ref[s] = arrived_ref[:, s].reshape(rows * pieces, part).astype(jnp.float32)
        grad = jnp.concatenate(
            [spread_ref[s, pl.ds(j, rows, stride=pieces), :] for j in range(pieces)], axis=1
        ).astype(jnp.bfloat16)
        grad_ref[s] = grad
        rotated = jnp.dot(grad, basis, preferred_element_type=jnp.float32)
        for i in range(GROUPS):
            rotated_ref[s, i] = rotated[:, i * part : (i + 1) * part]
            for r in range(share):
                local = pl.ds(r, owners, stride=share)
                if i == 0:
                    here = pl.ds(base + r, owners, stride=GROUPS * share)
                    first, second = first_ref[s, here, :], second_ref[s, here, :]
                else:
                    ref, _, at = sources[i - 1]
                    first, second = (
                        ref[pl.ds(at + (2 * m * share + r) * owners, owners), :].astype(jnp.float32)
                        + ref[
                            pl.ds(at + ((2 * m + 1) * share + r) * owners, owners), :
                        ].astype(jnp.float32)
                        for m in range(2)
                    )
                turned = rotated_ref[s, i, local, :]
                moment_one = beta_one * first + (1.0 - beta_one) * turned
                moment_two = beta_two * second + (1.0 - beta_two) * turned * turned
                direction_ref[s, i, local, :] = (
                    moment_one / bias_one / (jnp.sqrt(moment_two / bias_two) + epsilon)
                )
        direction = jnp.concatenate([direction_ref[s, i] for i in range(GROUPS)], axis=1)
        back = lax.dot_general(
            direction.astype(jnp.bfloat16),
            basis,
            (((1,), (1,)), ((), ())),
            preferred_element_type=jnp.float32,
        )
        for j in range(pieces):
            spread_ref[s, pl.ds(j, rows, stride=pieces), :] = back[:, j * part : (j + 1) * part]
        back_ref[:, s] = (
            spread_ref[s].astype(back_ref.dtype).reshape(owners, share, pieces, part)
        )


def state_kernel(
    share, count_ref, grad_ref, right_ref, left_ref, far_ref, basis_ref, stats_ref, first_ref,
    second_ref, new_stats_ref, new_first_ref, new_second_ref, rotated_ref,
):
    slots, rows, _ = grad_ref.shape
    part = basis_ref.shape[2]
    owners = rows // share
    me = lax.axis_index("tensor")
    start = pl.multiple_of(me * part, part)
    for s in range(slots):
        live = s < count_ref[0]
        sources = (grad_ref.at[s], right_ref.at[s], left_ref.at[s], far_ref.at[s])
        grad = jnp.concatenate([ref[...] for ref in sources], axis=0)
        grad_cols = jnp.concatenate([ref[:, pl.ds(start, part)] for ref in sources], axis=0)
        gram = lax.dot_general(
            grad, grad_cols, (((0,), (0,)), ((), ())), preferred_element_type=jnp.float32
        )
        stats = stats_ref[s]
        new_stats_ref[s] = jnp.where(live, beta_stat * stats + (1.0 - beta_stat) * gram, stats)
        rotated_ref[s] = jnp.dot(grad, basis_ref[s], preferred_element_type=jnp.float32)
        for i, offset in enumerate((0, 1, GROUPS - 1, 2)):
            base = lax.rem(me + offset, GROUPS) * share
            for r in range(share):
                rotated = rotated_ref[s, pl.ds(i * rows + r, owners, stride=share), :]
                here = pl.ds(base + r, owners, stride=GROUPS * share)
                first = first_ref[s, here, :]
                second = second_ref[s, here, :]
                new_first_ref[s, here, :] = jnp.where(
                    live, beta_one * first + (1.0 - beta_one) * rotated, first
                )
                new_second_ref[s, here, :] = jnp.where(
                    live, beta_two * second + (1.0 - beta_two) * rotated * rotated, second
                )


def on_device(gradient, block_list, block_counts, stats, basis, first_moment, second_moment):
    rows_dev, cols_dev = gradient.shape
    slot_count = block_list.shape[1]
    owners = lax.axis_size("dp")
    parts = lax.axis_size("tensor")
    width = stats.shape[2]
    part = stats.shape[3]
    blocks = cols_dev * parts // width
    share = rows_dev // GROUPS
    pieces = cols_dev // part
    vmem = pl.BlockSpec(memory_space=pltpu.VMEM)
    params = pltpu.CompilerParams(vmem_limit_bytes=48 * 2**20)

    def own(kernel):
        return lambda *refs: kernel(share, *refs)

    mine = jnp.concatenate([block_list[0], block_counts])
    is_me = jnp.arange(owners)[:, None] == lax.axis_index("dp")
    flat = lax.psum(jnp.where(is_me, mine[None, :], 0).reshape(-1), "dp")
    table = flat.reshape(owners, slot_count + 1)
    lists = table[:, :slot_count]
    live = jnp.arange(slot_count)[None, :] < table[:, slot_count:]

    groups = gradient.reshape(GROUPS, share, pieces, part).transpose(0, 2, 1, 3)
    leaving = jnp.tile(groups, (parts // GROUPS, 1, 1, 1))
    moved = lax.all_to_all(leaving, "tensor", 0, 0, tiled=True)
    by_block = moved.reshape(blocks, width // part, share, part).transpose(0, 2, 1, 3)

    piece = 4 * share * owners
    sent = jax.ShapeDtypeStruct((2 * width + 3 * piece, part), jnp.bfloat16)
    packed = pl.pallas_call(
        own(pack_kernel),
        out_shape=(sent, sent),
        in_specs=[pl.BlockSpec(memory_space=pl.ANY)] + [vmem] * 3,
        out_specs=(vmem,) * 2,
        compiler_params=params,
        name="pack",
    )(leaving, basis[0], first_moment[0], second_moment[0])
    right, left = shifted(packed[0], parts, 1), shifted(packed[1], parts, -1)
    far = (shifted(x[: width + piece], parts, by) for x, by in ((right, 1), (left, -1)))

    outgoing = jnp.take(by_block, lists, axis=0, mode="clip")
    arrived = lax.all_to_all(outgoing, "dp", 0, 0, tiled=True)
    grad_rows, back = pl.pallas_call(
        own(rows_kernel),
        out_shape=(
            jax.ShapeDtypeStruct((slot_count, owners * share, width), jnp.bfloat16),
            jax.ShapeDtypeStruct(arrived.shape, jnp.bfloat16),
        ),
        scratch_shapes=[
            pltpu.VMEM((slot_count, GROUPS, owners * share, part), jnp.float32),
            pltpu.VMEM((slot_count, GROUPS, owners * share, part), jnp.float32),
            pltpu.VMEM((slot_count, owners * share * (width // part), part), jnp.float32),
        ],
        compiler_params=params,
        name="rotate_rows",
    )(arrived, basis[0], first_moment[0], second_moment[0], right, left, *far)

    returned = lax.all_to_all(back, "dp", 0, 0, tiled=True)
    holds = (lists.reshape(-1)[None, :] == jnp.arange(blocks)[:, None]) & live.reshape(-1)[None, :]
    place = jnp.argmax(holds, axis=1)
    placed = jnp.take(
        returned.reshape(owners * slot_count, share, width // part, part), place, axis=0, mode="clip"
    ).transpose(0, 2, 1, 3)
    partial = lax.all_to_all(
        placed.reshape(parts, pieces, share, part), "tensor", 0, 0, tiled=True
    )
    update = (
        partial.reshape(parts // GROUPS, GROUPS, pieces, share, part)
        .astype(jnp.float32)
        .sum(0)
        .astype(jnp.bfloat16)
        .transpose(0, 2, 1, 3)
        .reshape(rows_dev, cols_dev)
    )

    right_rows, left_rows = shifted(grad_rows, parts, 1), shifted(grad_rows, parts, -1)
    others = right_rows, left_rows, shifted(right_rows, parts, 1)
    new_stats, new_first, new_second = pl.pallas_call(
        own(state_kernel),
        out_shape=(
            jax.ShapeDtypeStruct(stats.shape[1:], jnp.float32),
            jax.ShapeDtypeStruct(first_moment.shape[1:], jnp.float32),
            jax.ShapeDtypeStruct(second_moment.shape[1:], jnp.float32),
        ),
        in_specs=[pl.BlockSpec(memory_space=pltpu.SMEM)] + [vmem] * 8,
        out_specs=(vmem,) * 3,
        scratch_shapes=[pltpu.VMEM((slot_count, GROUPS * owners * share, part), jnp.float32)],
        compiler_params=params,
        cost_estimate=pl.CostEstimate(flops=2**30, bytes_accessed=2**24, transcendentals=0),
        name="new_state",
    )(block_counts, grad_rows, *others, basis[0], stats[0], first_moment[0], second_moment[0])
    return (update, new_stats[None], new_first[None], new_second[None])


def solution(mesh):
    placed = (
        P("dp", "tensor"),
        P("dp", None),
        P("dp"),
        P("dp", None, None, "tensor"),
        P("dp", None, None, "tensor"),
        P("dp", None, None, "tensor"),
        P("dp", None, None, "tensor"),
    )
    return jax.shard_map(
        on_device,
        mesh=mesh,
        in_specs=placed,
        out_specs=(
            P("dp", "tensor"),
            P("dp", None, None, "tensor"),
            P("dp", None, None, "tensor"),
            P("dp", None, None, "tensor"),
        ),
        check_vma=False,
    )
```

time: 143 us -> 133 us (0.930)
  blocking collectives: 53.7 us -> 25 us
  starting transfers between devices: 25.5 us -> 52.3 us
  between operations: 14.9 us -> 1.54 us
  local copies, waits for them, and re-layouts: 9.82 us -> 14 us
  Pallas kernels: 6.51 us -> 8.5 us
    ppermute x0 -> x7, waiting for transfers between devices: none -> 28.9 us  [shifted(): lax.ppermute(x, 'tensor', [((i + by) % parts, i) for i in range(parts)])]
    all_to_all x1 -> x0, blocking collectives: 28.7 us -> none  [on_device(): arrived = lax.all_to_all(outgoing, 'dp', 0, 0, tiled=True)]
    ppermute x0 -> x7, starting transfers between devices: none -> 23.5 us  [shifted(): lax.ppermute(x, 'tensor', [((i + by) % parts, i) for i in range(parts)])]
    all_to_all x3 -> x4, waiting for transfers between devices: 15.5 us -> 0.01 us  [the longest x1 0.01 us: on_device(): moved = lax.all_to_all(leaving, 'tensor', 0, 0, tiled=True)]
    all_gather x2 -> x0, waiting for transfers between devices: 13.5 us -> none  [the longest x1 11.6 us: on_device(): grad_all = lax.all_gather(grad_rows, 'tensor', axis=0, tiled=False)]
    all_to_all x3 -> x4, starting transfers between devices: 25.4 us -> 28.9 us  [the longest x1 10.7 us: on_device(): returned = lax.all_to_all(back, 'dp', 0, 0, tiled=True)]
    unnamed x18 -> x23, local copies, waits for them, and re-layouts: 4.51 us -> 6.64 us
    pallas_call x2 -> x3, Pallas kernels: 6.51 us -> 8.5 us  [the longest x1 4.18 us: on_device(): pl.pallas_call(own(state_kernel), out_shape=(jax.ShapeDtypeStruct(stats.s...]
  transfers between devices with their start and end apart: 5 -> 11, of which waited for: 4 -> 4; matrix products, arithmetic and copies ran while one was open for 5% -> 5% of each run, Pallas kernels for 5% -> 4%
where the time goes in v3:
time: 133 us; the launch traced here: 132 us
  starting transfers between devices  52.3 us (39%)
  waiting for transfers between devices  28.9 us (22%)
  blocking collectives  25 us (19%)
  local copies, waits for them, and re-layouts  14 us (11%)
  Pallas kernels  8.5 us (6%)
  between operations  1.54 us (1%)
    ppermute x7, waiting for transfers between devices, shifted(): lax.ppermute(x, 'tensor', [((i + by) % parts, i) for i in range(parts)])  28.9 us
    psum x1, blocking collectives, on_device(): flat = lax.psum(jnp.where(is_me, mine[None, :], 0).reshape(-1), 'dp')  25 us
    ppermute x7, starting transfers between devices, shifted(): lax.ppermute(x, 'tensor', [((i + by) % parts, i) for i in range(parts)])  23.5 us
    all_to_all x1, starting transfers between devices, on_device(): returned = lax.all_to_all(back, 'dp', 0, 0, tiled=True)  10.7 us
    all_to_all x1, starting transfers between devices, on_device(): moved = lax.all_to_all(leaving, 'tensor', 0, 0, tiled=True)  7.1 us
    unnamed x23, local copies, waits for them, and re-layouts  6.64 us
    all_to_all x1, starting transfers between devices, on_device(): arrived = lax.all_to_all(outgoing, 'dp', 0, 0, tiled=True)  6.53 us
    all_to_all x1, starting transfers between devices, on_device(): lax.all_to_all(placed.reshape(parts, pieces, share, part), 'tensor', 0, 0...  4.54 us
  transfers between devices with their start and end apart: 11, of which 4 were waited for; matrix products, arithmetic and copies ran while one was open for 5% of the time, Pallas kernels for 4%

profile of v3, /device:TPU:6, one launch (start us, length us, event | category | flops | bytes accessed | tf_op | source)
XLA Modules:
  0.0 131.5 jit_solution(4208597346992298591)
XLA Ops:
  0.6 0.0 copy-start.1
  0.6 1.0 reshape.59
  1.7 0.0 copy-start
  1.7 0.1 copy.25
  1.8 0.8 tile.4
  2.6 7.1 %all-to-all-start = ((bf16[8,52,2,128]{3,2,1,0:T(2,128)(2,1)}), bf16[8,52,2,128]{3,2,1,0:T(2,128)(2,1)S(1)}, u32[]{:S(2)}, u32[]{:S(2)}) async-start(bf16[8,52,2,128]{3,2,1,0:T(2,128)(2,1)} %bitcast.1.refs_0_), calls=%async_computation | async-start | bytes 425984 | tf_op jit(solution)/shard_map/all_to_all | solution.py:174
  9.7 0.0 copy-done.1
  9.7 0.0 copy-done
  9.7 0.0 copy-start.2
  9.7 1.0 copy-done.2
  10.7 1.4 %pack.1 = (bf16[3584,128]{1,0:T(8,128)(2,1)}, bf16[3584,128]{1,0:T(8,128)(2,1)}) custom-call(bf16[8,52,2,128]{3,2,1,0:T(2,128)(2,1)} %bitcast.1.refs_0_, bf16[2,1024,128]{2,1,0:T(8,128)(2,1)S(1)} %bitcast.27, f32[2,512,128]{2,1,0:T(8,128)S(1)} %bitcast.30, f32[2,512,128]{2,1,0:T(8,128)S(1)} %bitcast.33), custom_call_target="tpu_custom_call" | custom-call | tf_op jit(solution)/shard_map/pack/pallas_call | solution.py:179
  12.2 5.1 %collective-permute-start = (bf16[3584,128]{1,0:T(8,128)(2,1)}, bf16[3584,128]{1,0:T(8,128)(2,1)S(1)}, u32[]{:S(2)}, u32[]{:S(2)}) collective-permute-start(bf16[3584,128]{1,0:T(8,128)(2,1)} %get-tuple-element.12), channel_id=1, source_target_pairs={{1,0},{2,1},{3,2},{4,3},{5,4},{6,5},{7,6},{0,7},{9,8},{10,9},{11,1... | collective-permute-start | bytes 2752520 | tf_op jit(solution)/shard_map/ppermute | solution.py:22
  17.3 1.9 %collective-permute-start.1 = (bf16[3584,128]{1,0:T(8,128)(2,1)}, bf16[3584,128]{1,0:T(8,128)(2,1)}, u32[]{:S(2)}, u32[]{:S(2)}) collective-permute-start(bf16[3584,128]{1,0:T(8,128)(2,1)} %get-tuple-element.13), channel_id=1, source_target_pairs={{7,0},{0,1},{1,2},{2,3},{3,4},{4,5},{5,6},{6,7},{15,8},{8,9},{9,10... | collective-permute-start | bytes 2752520 | tf_op jit(solution)/shard_map/ppermute | solution.py:22
  19.9 0.0 copy-start.10
  19.9 0.6 copy-done.10
  20.5 0.1 pad_add_fusion
  20.6 0.1 broadcast_select_fusion
  20.7 25.0 %psum.7 = s32[64,3]{0,1:T(4,128)S(1)} all-reduce(s32[64,3]{0,1:T(4,128)S(1)} %broadcast_select_fusion), channel_id=1, replica_groups=mesh['dp'=64,'tensor'=8] {'dp'}, use_global_device_ids=true, to_apply=%region_0.1 | all-reduce | flops 192 | bytes 1536 | tf_op jit(solution)/shard_map/psum | solution.py:167
  45.7 0.1 copy.27
  45.8 0.1 reshape.69
  45.9 0.0 all-to-all-done
  46.0 1.5 %gather_fusion = bf16[128,2,8,128]{3,2,1,0:T(8,128)(2,1)} fusion(bf16[52,2,8,128]{3,2,1,0:T(8,128)(2,1)S(1)} %bitcast.37, s32[1024]{0:T(1024)S(1)} %pad_clamp_fusion.1), kind=kCustom, calls=%fused_computation | custom fusion | bytes 1049088 | tf_op jit(solution)/shard_map/jit(_take)/gather | solution.py:190
  47.5 6.5 %all-to-all-start.1 = ((bf16[64,2,2,8,128]{4,3,2,1,0:T(8,128)(2,1)}), bf16[64,2,2,8,128]{4,3,2,1,0:T(8,128)(2,1)S(1)}, u32[]{:S(2)}, u32[]{:S(2)}) async-start(bf16[64,2,2,8,128]{4,3,2,1,0:T(8,128)(2,1)} %bitcast.5), calls=%async_computation.1 | async-start | bytes 1048576 | tf_op jit(solution)/shard_map/all_to_all | solution.py:191
  54.0 0.0 collective-permute-done.refs_4_
  54.0 0.0 copy-start.3
  54.1 5.3 %collective-permute-start.2 = (bf16[1536,128]{1,0:T(8,128)(2,1)S(1)}, bf16[1536,128]{1,0:T(8,128)(2,1)S(1)}, u32[]{:S(2)}, u32[]{:S(2)}) collective-permute-start(bf16[1536,128]{1,0:T(8,128)(2,1)S(1)} %slice.20), channel_id=1, source_target_pairs={{1,0},{2,1},{3,2},{4,3},{5,4},{6,5},{7,6},{0,7},{9,8},{10,9},{11,1... | collective-permute-start | bytes 1179656 | tf_op jit(solution)/shard_map/ppermute | solution.py:22
  59.3 0.0 collective-permute-done.1.refs_5_
  59.3 1.0 slice.21
  60.4 1.9 %collective-permute-start.3 = (bf16[1536,128]{1,0:T(8,128)(2,1)S(1)}, bf16[1536,128]{1,0:T(8,128)(2,1)S(1)}, u32[]{:S(2)}, u32[]{:S(2)}) collective-permute-start(bf16[1536,128]{1,0:T(8,128)(2,1)S(1)} %slice.21), channel_id=1, source_target_pairs={{7,0},{0,1},{1,2},{2,3},{3,4},{4,5},{5,6},{6,7},{15,8},{8,9},{9,10... | collective-permute-start | bytes 1179656 | tf_op jit(solution)/shard_map/ppermute | solution.py:22
  62.3 5.7 %collective-permute-done.2.refs_6_ = bf16[1536,128]{1,0:T(8,128)(2,1)S(1)} collective-permute-done((bf16[1536,128]{1,0:T(8,128)(2,1)S(1)}, bf16[1536,128]{1,0:T(8,128)(2,1)S(1)}, u32[]{:S(2)}, u32[]{:S(2)}) %collective-permute-start.2) | collective-permute-done | bytes 393248 | tf_op jit(solution)/shard_map/ppermute | solution.py:22
  68.0 0.0 copy-start.6
  68.0 0.7 copy-done.6
  68.7 5.6 %collective-permute-done.3.refs_7_ = bf16[1536,128]{1,0:T(8,128)(2,1)S(1)} collective-permute-done((bf16[1536,128]{1,0:T(8,128)(2,1)S(1)}, bf16[1536,128]{1,0:T(8,128)(2,1)S(1)}, u32[]{:S(2)}, u32[]{:S(2)}) %collective-permute-start.3) | collective-permute-done | bytes 393248 | tf_op jit(solution)/shard_map/ppermute | solution.py:22
  74.4 0.0 copy-start.8
  74.4 0.7 copy-done.8
  75.1 0.0 all-to-all-done.1.refs_0_
  75.1 0.0 copy-done.3
  75.1 0.0 copy-start.7
  75.1 1.0 copy-done.7
  76.1 0.0 copy-start.9
  76.1 1.0 copy-done.9
  77.1 2.9 %rotate_rows.1 = (bf16[2,128,1024]{2,1,0:T(8,128)(2,1)S(1)}, bf16[64,2,2,8,128]{4,3,2,1,0:T(8,128)(2,1)S(1)}) custom-call(bf16[64,2,2,8,128]{4,3,2,1,0:T(8,128)(2,1)S(1)} %all-to-all-done.1.refs_0_, bf16[2,1024,128]{2,1,0:T(8,128)(2,1)S(1)} %bitcast.28, f32[2,512,128]{2,1,0:T(8,128)S(1)} %bitcast.31, f32[2,512,128]{2,1,0:T(8,128)S(1)} %bitcast.34, ...), custom_call_target="tpu_custom_call" | custom-call | tf_op jit(solution)/shard_map/rotate_rows/pallas_call | solution.py:192
  80.0 0.0 copy-start.5
  80.0 0.8 copy-done.5
  80.8 0.0 copy-start.4
  80.8 10.7 %all-to-all-start.2 = ((bf16[64,2,2,8,128]{4,3,2,1,0:T(8,128)(2,1)}), bf16[64,2,2,8,128]{4,3,2,1,0:T(8,128)(2,1)}, u32[]{:S(2)}, u32[]{:S(2)}) async-start(bf16[64,2,2,8,128]{4,3,2,1,0:T(8,128)(2,1)} %copy-done.5), calls=%async_computation.2 | async-start | bytes 1048576 | tf_op jit(solution)/shard_map/all_to_all | solution.py:207
  91.5 1.9 %collective-permute-start.4 = (bf16[2,128,1024]{2,1,0:T(8,128)(2,1)S(1)}, bf16[2,128,1024]{2,1,0:T(8,128)(2,1)}, u32[]{:S(2)}, u32[]{:S(2)}) collective-permute-start(bf16[2,128,1024]{2,1,0:T(8,128)(2,1)S(1)} %get-tuple-element.16.refs_1_), channel_id=1, source_target_pairs={{1,0},{2,1},{3,2},{4,3},{5,4},{6,5},{7,6},{0,7},{9,8},{10,9},{11,1... | collective-permute-start | bytes 1572872 | tf_op jit(solution)/shard_map/ppermute | solution.py:22
  93.5 0.1 iota_compare_fusion
  93.5 0.2 lt.28
  93.7 3.9 %collective-permute-start.5 = (bf16[2,128,1024]{2,1,0:T(8,128)(2,1)S(1)}, bf16[2,128,1024]{2,1,0:T(8,128)(2,1)}, u32[]{:S(2)}, u32[]{:S(2)}) collective-permute-start(bf16[2,128,1024]{2,1,0:T(8,128)(2,1)S(1)} %get-tuple-element.16.refs_1_), channel_id=1, source_target_pairs={{7,0},{0,1},{1,2},{2,3},{3,4},{4,5},{5,6},{6,7},{15,8},{8,9},{9,10... | collective-permute-start | bytes 1572872 | tf_op jit(solution)/shard_map/ppermute | solution.py:22
  97.6 9.9 %collective-permute-done.4.refs_2_ = bf16[2,128,1024]{2,1,0:T(8,128)(2,1)} collective-permute-done((bf16[2,128,1024]{2,1,0:T(8,128)(2,1)S(1)}, bf16[2,128,1024]{2,1,0:T(8,128)(2,1)}, u32[]{:S(2)}, u32[]{:S(2)}) %collective-permute-start.4) | collective-permute-done | bytes 524320 | tf_op jit(solution)/shard_map/ppermute | solution.py:22
  107.5 3.4 %collective-permute-start.6 = (bf16[2,128,1024]{2,1,0:T(8,128)(2,1)}, bf16[2,128,1024]{2,1,0:T(8,128)(2,1)}, u32[]{:S(2)}, u32[]{:S(2)}) collective-permute-start(bf16[2,128,1024]{2,1,0:T(8,128)(2,1)} %collective-permute-done.4.refs_2_), channel_id=1, source_target_pairs={{1,0},{2,1},{3,2},{4,3},{5,4},{6,5},{7,6},{0,7},{9,8},{10,9},{11,1... | collective-permute-start | bytes 1572872 | tf_op jit(solution)/shard_map/ppermute | solution.py:22
  110.9 0.6 iota_reduce_fusion
  111.5 0.0 all-to-all-done.2
  111.5 1.7 %gather_fusion.1 = bf16[52,2,8,128]{3,2,1,0:T(8,128)(2,1)S(1)} fusion(bf16[128,2,8,128]{3,2,1,0:T(8,128)(2,1)} %bitcast.9, s32[1024]{0:T(1024)S(1)} %pad_clamp_fusion), kind=kCustom, calls=%fused_computation.1 | custom fusion | bytes 426192 | tf_op jit(solution)/shard_map/jit(_take)/gather | solution.py:210
  113.2 0.8 copy.28
  114.0 4.5 %all-to-all-start.3 = ((bf16[8,52,2,128]{3,2,1,0:T(2,128)(2,1)}), bf16[8,52,2,128]{3,2,1,0:T(2,128)(2,1)S(1)}, u32[]{:S(2)}, u32[]{:S(2)}) async-start(bf16[8,52,2,128]{3,2,1,0:T(2,128)(2,1)} %bitcast.40), calls=%async_computation.3 | async-start | bytes 425984 | tf_op jit(solution)/shard_map/all_to_all | solution.py:213
  118.6 0.0 collective-permute-done.5.refs_3_
  118.6 7.7 %collective-permute-done.6.refs_4_ = bf16[2,128,1024]{2,1,0:T(8,128)(2,1)} collective-permute-done((bf16[2,128,1024]{2,1,0:T(8,128)(2,1)}, bf16[2,128,1024]{2,1,0:T(8,128)(2,1)}, u32[]{:S(2)}, u32[]{:S(2)}) %collective-permute-start.6) | collective-permute-done | bytes 524320 | tf_op jit(solution)/shard_map/ppermute | solution.py:22
  126.3 0.0 copy-done.4
  126.3 4.2 %new_state.1 = (f32[2,1024,128]{2,1,0:T(8,128)}, f32[2,512,128]{2,1,0:T(8,128)}, f32[2,512,128]{2,1,0:T(8,128)}) custom-call(s32[1]{0:T(128)S(6)} %copy.35.refs_0_, bf16[2,128,1024]{2,1,0:T(8,128)(2,1)S(1)} %get-tuple-element.16.refs_1_, bf16[2,128,1024]{2,1,0:T(8,128)(2,1)} %collective-permute-done.4.refs_2_, ...), custom_call_target="tpu_custom_call" | custom-call | flops 1073741824 | bytes 16777216 | tf_op jit(solution)/shard_map/new_state/pallas_call | solution.py:227
  130.4 0.0 all-to-all-done.3
  130.4 0.4 reduce_sum.12
  130.9 0.7 copy.34
  (8 shorter events, 0.1 us)
Async XLA Ops:
  0.6 9.0 %copy-start.1 = (f32[1,2,512,128]{3,2,1,0:T(8,128)S(1)}, f32[1,2,512,128]{3,2,1,0:T(8,128)}, u32[]{:S(2)}) copy-start(f32[1,2,512,128]{3,2,1,0:T(8,128)} %param.12) | copy-start | bytes 1572868
  1.7 8.0 %copy-start = (bf16[1,2,1024,128]{3,2,1,0:T(8,128)(2,1)S(1)}, bf16[1,2,1024,128]{3,2,1,0:T(8,128)(2,1)}, u32[]{:S(2)}) copy-start(bf16[1,2,1024,128]{3,2,1,0:T(8,128)(2,1)} %param.11) | copy-start | bytes 1572868
  2.6 43.4 %all-to-all-start = ((bf16[8,52,2,128]{3,2,1,0:T(2,128)(2,1)}), bf16[8,52,2,128]{3,2,1,0:T(2,128)(2,1)S(1)}, u32[]{:S(2)}, u32[]{:S(2)}) async-start(bf16[8,52,2,128]{3,2,1,0:T(2,128)(2,1)} %bitcast.1.refs_0_), calls=%async_computation | async-start | bytes 425984 | tf_op jit(solution)/shard_map/all_to_all | solution.py:174
  9.7 1.0 copy-start.2
  12.2 41.8 %collective-permute-start = (bf16[3584,128]{1,0:T(8,128)(2,1)}, bf16[3584,128]{1,0:T(8,128)(2,1)S(1)}, u32[]{:S(2)}, u32[]{:S(2)}) collective-permute-start(bf16[3584,128]{1,0:T(8,128)(2,1)} %get-tuple-element.12), channel_id=1, source_target_pairs={{1,0},{2,1},{3,2},{4,3},{5,4},{6,5},{7,6},{0,7},{9,8},{10,9},{11,1... | collective-permute-start | bytes 2752520 | tf_op jit(solution)/shard_map/ppermute | solution.py:22
  17.3 42.0 %collective-permute-start.1 = (bf16[3584,128]{1,0:T(8,128)(2,1)}, bf16[3584,128]{1,0:T(8,128)(2,1)}, u32[]{:S(2)}, u32[]{:S(2)}) collective-permute-start(bf16[3584,128]{1,0:T(8,128)(2,1)} %get-tuple-element.13), channel_id=1, source_target_pairs={{7,0},{0,1},{1,2},{2,3},{3,4},{4,5},{5,6},{6,7},{15,8},{8,9},{9,10... | collective-permute-start | bytes 2752520 | tf_op jit(solution)/shard_map/ppermute | solution.py:22
  19.9 0.7 copy-start.10
  47.5 27.6 %all-to-all-start.1 = ((bf16[64,2,2,8,128]{4,3,2,1,0:T(8,128)(2,1)}), bf16[64,2,2,8,128]{4,3,2,1,0:T(8,128)(2,1)S(1)}, u32[]{:S(2)}, u32[]{:S(2)}) async-start(bf16[64,2,2,8,128]{4,3,2,1,0:T(8,128)(2,1)} %bitcast.5), calls=%async_computation.1 | async-start | bytes 1048576 | tf_op jit(solution)/shard_map/all_to_all | solution.py:191
  54.0 21.1 %copy-start.3 = (f32[1,2,512,128]{3,2,1,0:T(8,128)S(1)}, f32[1,2,512,128]{3,2,1,0:T(8,128)}, u32[]{:S(2)}) copy-start(f32[1,2,512,128]{3,2,1,0:T(8,128)} %param.13) | copy-start | bytes 1572868
  54.1 13.9 %collective-permute-start.2 = (bf16[1536,128]{1,0:T(8,128)(2,1)S(1)}, bf16[1536,128]{1,0:T(8,128)(2,1)S(1)}, u32[]{:S(2)}, u32[]{:S(2)}) collective-permute-start(bf16[1536,128]{1,0:T(8,128)(2,1)S(1)} %slice.20), channel_id=1, source_target_pairs={{1,0},{2,1},{3,2},{4,3},{5,4},{6,5},{7,6},{0,7},{9,8},{10,9},{11,1... | collective-permute-start | bytes 1179656 | tf_op jit(solution)/shard_map/ppermute | solution.py:22
  60.4 14.0 %collective-permute-start.3 = (bf16[1536,128]{1,0:T(8,128)(2,1)S(1)}, bf16[1536,128]{1,0:T(8,128)(2,1)S(1)}, u32[]{:S(2)}, u32[]{:S(2)}) collective-permute-start(bf16[1536,128]{1,0:T(8,128)(2,1)S(1)} %slice.21), channel_id=1, source_target_pairs={{7,0},{0,1},{1,2},{2,3},{3,4},{4,5},{5,6},{6,7},{15,8},{8,9},{9,10... | collective-permute-start | bytes 1179656 | tf_op jit(solution)/shard_map/ppermute | solution.py:22
  68.0 0.7 copy-start.6
  74.4 0.7 copy-start.8
  75.1 1.0 copy-start.7
  76.1 1.0 copy-start.9
  80.0 0.8 copy-start.5
  80.8 45.5 %copy-start.4 = (f32[1,2,1024,128]{3,2,1,0:T(8,128)S(1)}, f32[1,2,1024,128]{3,2,1,0:T(8,128)}, u32[]{:S(2)}) copy-start(f32[1,2,1024,128]{3,2,1,0:T(8,128)} %param.10) | copy-start | bytes 3145732
  80.8 30.7 %all-to-all-start.2 = ((bf16[64,2,2,8,128]{4,3,2,1,0:T(8,128)(2,1)}), bf16[64,2,2,8,128]{4,3,2,1,0:T(8,128)(2,1)}, u32[]{:S(2)}, u32[]{:S(2)}) async-start(bf16[64,2,2,8,128]{4,3,2,1,0:T(8,128)(2,1)} %copy-done.5), calls=%async_computation.2 | async-start | bytes 1048576 | tf_op jit(solution)/shard_map/all_to_all | solution.py:207
  91.5 16.0 %collective-permute-start.4 = (bf16[2,128,1024]{2,1,0:T(8,128)(2,1)S(1)}, bf16[2,128,1024]{2,1,0:T(8,128)(2,1)}, u32[]{:S(2)}, u32[]{:S(2)}) collective-permute-start(bf16[2,128,1024]{2,1,0:T(8,128)(2,1)S(1)} %get-tuple-element.16.refs_1_), channel_id=1, source_target_pairs={{1,0},{2,1},{3,2},{4,3},{5,4},{6,5},{7,6},{0,7},{9,8},{10,9},{11,1... | collective-permute-start | bytes 1572872 | tf_op jit(solution)/shard_map/ppermute | solution.py:22
  93.7 24.9 %collective-permute-start.5 = (bf16[2,128,1024]{2,1,0:T(8,128)(2,1)S(1)}, bf16[2,128,1024]{2,1,0:T(8,128)(2,1)}, u32[]{:S(2)}, u32[]{:S(2)}) collective-permute-start(bf16[2,128,1024]{2,1,0:T(8,128)(2,1)S(1)} %get-tuple-element.16.refs_1_), channel_id=1, source_target_pairs={{7,0},{0,1},{1,2},{2,3},{3,4},{4,5},{5,6},{6,7},{15,8},{8,9},{9,10... | collective-permute-start | bytes 1572872 | tf_op jit(solution)/shard_map/ppermute | solution.py:22
  107.5 18.8 %collective-permute-start.6 = (bf16[2,128,1024]{2,1,0:T(8,128)(2,1)}, bf16[2,128,1024]{2,1,0:T(8,128)(2,1)}, u32[]{:S(2)}, u32[]{:S(2)}) collective-permute-start(bf16[2,128,1024]{2,1,0:T(8,128)(2,1)} %collective-permute-done.4.refs_2_), channel_id=1, source_target_pairs={{1,0},{2,1},{3,2},{4,3},{5,4},{6,5},{7,6},{0,7},{9,8},{10,9},{11,1... | collective-permute-start | bytes 1572872 | tf_op jit(solution)/shard_map/ppermute | solution.py:22
  114.0 16.4 %all-to-all-start.3 = ((bf16[8,52,2,128]{3,2,1,0:T(2,128)(2,1)}), bf16[8,52,2,128]{3,2,1,0:T(2,128)(2,1)S(1)}, u32[]{:S(2)}, u32[]{:S(2)}) async-start(bf16[8,52,2,128]{3,2,1,0:T(2,128)(2,1)} %bitcast.40), calls=%async_computation.3 | async-start | bytes 425984 | tf_op jit(solution)/shard_map/all_to_all | solution.py:213

commit v4 on v3

--- a/solution.py
+++ b/solution.py
@@ -16,6 +16,8 @@
 bias_two = 1.0 - beta_two**STEP
 
 GROUPS = 4
+ROWS_VMEM = 58 * 2**20
+ROWS_FLOPS = 2**34
 
 
 def shifted(x, parts, by):
@@ -48,32 +50,56 @@
             put(ref, 2 * width + (1 + s) * piece, me + step, s)
 
 
+def spread_rows(tiles, spread_ref):
+    rows, pieces, part = tiles.shape
+    spread_ref[...] = tiles.reshape(rows * pieces, part).astype(jnp.float32)
+    return jnp.concatenate(
+        [spread_ref[pl.ds(j, rows, stride=pieces), :] for j in range(pieces)], axis=1
+    ).astype(jnp.bfloat16)
+
+
 def rows_kernel(
-    share, arrived_ref, basis_ref, first_ref, second_ref, right_ref, left_ref, far_right_ref,
-    far_left_ref, grad_ref, back_ref, rotated_ref, direction_ref, spread_ref,
+    share, arrived_hbm, basis_hbm, first_hbm, second_hbm, right_hbm, left_hbm, far_right_hbm,
+    far_left_hbm, place_hbm, back_ref, rotated_ref, direction_ref, spread_ref, arrived_ref, basis_ref,
+    first_ref, second_ref, right_ref, left_ref, far_ref, sems,
 ):
-    slots, rows, width = grad_ref.shape
-    part = basis_ref.shape[2]
-    pieces = width // part
-    owners = rows // share
+    owners, slots, _, pieces, part = arrived_ref.shape
+    rows = owners * share
+    width = pieces * part
     base = lax.rem(lax.axis_index("tensor"), GROUPS) * share
     piece = 4 * share * owners
+    stay = width + piece
+
+    def needed(s):
+        near = stay + width + s * piece
+        yield arrived_hbm.at[:, s], arrived_ref.at[:, s]
+        yield basis_hbm.at[s], basis_ref.at[s]
+        for hbm, ref, at in ((right_hbm, right_ref, (0, stay)[s]), (left_hbm, left_ref, (stay, 0)[s])):
+            for first, size in ((at, width), (near, piece)):
+                yield hbm.at[pl.ds(first, size)], ref.at[pl.ds(first, size)]
+        yield (far_right_hbm, far_left_hbm)[s], far_ref.at[s]
+        yield first_hbm.at[s], first_ref.at[s]
+        yield second_hbm.at[s], second_ref.at[s]
+
+    copies = [
+        [pltpu.make_async_copy(*ends, sems.at[s, i]) for i, ends in enumerate(needed(s))]
+        for s in range(slots)
+    ]
+    for copy in copies[0] + copies[1]:
+        copy.start()
     for s in range(slots):
-        far_ref = (far_right_ref, far_left_ref)[s]
+        for copy in copies[s]:
+            copy.wait()
         near = 2 * width + (1 + s) * piece
         sources = (
             (right_ref, (0, width + piece)[s], near),
             (left_ref, (width + piece, 0)[s], near),
-            (far_ref, 0, width),
+            (far_ref.at[s], 0, width),
         )
         basis = jnp.concatenate(
             [basis_ref[s]] + [ref[pl.ds(at, width), :] for ref, at, _ in sources], axis=1
         )
-        spread_ref[s] = arrived_ref[:, s].reshape(rows * pieces, part).astype(jnp.float32)
-        grad = jnp.concatenate(
-            [spread_ref[s, pl.ds(j, rows, stride=pieces), :] for j in range(pieces)], axis=1
-        ).astype(jnp.bfloat16)
-        grad_ref[s] = grad
+        grad = spread_rows(arrived_ref[:, s].reshape(rows, pieces, part), spread_ref)
         rotated = jnp.dot(grad, basis, preferred_element_type=jnp.float32)
         for i in range(GROUPS):
             rotated_ref[s, i] = rotated[:, i * part : (i + 1) * part]
@@ -105,33 +131,35 @@
             preferred_element_type=jnp.float32,
         )
         for j in range(pieces):
-            spread_ref[s, pl.ds(j, rows, stride=pieces), :] = back[:, j * part : (j + 1) * part]
+            spread_ref[pl.ds(j, rows, stride=pieces), :] = back[:, j * part : (j + 1) * part]
         back_ref[:, s] = (
-            spread_ref[s].astype(back_ref.dtype).reshape(owners, share, pieces, part)
-        )
-
-
-def state_kernel(
-    share, count_ref, grad_ref, right_ref, left_ref, far_ref, basis_ref, stats_ref, first_ref,
-    second_ref, new_stats_ref, new_first_ref, new_second_ref, rotated_ref,
+            spread_ref[...].astype(back_ref.dtype).reshape(owners, share, pieces, part)
+        )
+
+
+def near_kernel(
+    share, count_ref, grad_ref, right_ref, left_ref, basis_ref, stats_ref, first_ref, second_ref,
+    new_stats_ref, new_first_ref, new_second_ref, rotated_ref, spread_ref, all_ref,
 ):
-    slots, rows, _ = grad_ref.shape
-    part = basis_ref.shape[2]
-    owners = rows // share
+    owners, slots, _, pieces, part = grad_ref.shape
+    rows = owners * share
     me = lax.axis_index("tensor")
     start = pl.multiple_of(me * part, part)
     for s in range(slots):
         live = s < count_ref[0]
-        sources = (grad_ref.at[s], right_ref.at[s], left_ref.at[s], far_ref.at[s])
-        grad = jnp.concatenate([ref[...] for ref in sources], axis=0)
-        grad_cols = jnp.concatenate([ref[:, pl.ds(start, part)] for ref in sources], axis=0)
+        for i, ref in enumerate((grad_ref, right_ref, left_ref)):
+            all_ref[s, pl.ds(i * rows, rows), :] = spread_rows(
+                ref[:, s].reshape(rows, pieces, part), spread_ref
+            )
+        grad = all_ref[s]
+        grad_cols = all_ref[s, :, pl.ds(start, part)]
         gram = lax.dot_general(
             grad, grad_cols, (((0,), (0,)), ((), ())), preferred_element_type=jnp.float32
         )
         stats = stats_ref[s]
         new_stats_ref[s] = jnp.where(live, beta_stat * stats + (1.0 - beta_stat) * gram, stats)
         rotated_ref[s] = jnp.dot(grad, basis_ref[s], preferred_element_type=jnp.float32)
-        for i, offset in enumerate((0, 1, GROUPS - 1, 2)):
+        for i, offset in enumerate((0, 1, GROUPS - 1)):
             base = lax.rem(me + offset, GROUPS) * share
             for r in range(share):
                 rotated = rotated_ref[s, pl.ds(i * rows + r, owners, stride=share), :]
@@ -144,6 +172,69 @@
                 new_second_ref[s, here, :] = jnp.where(
                     live, beta_two * second + (1.0 - beta_two) * rotated * rotated, second
                 )
+        base = lax.rem(me + 2, GROUPS) * share
+        for r in range(share):
+            here = pl.ds(base + r, owners, stride=GROUPS * share)
+            new_first_ref[s, here, :] = first_ref[s, here, :]
+            new_second_ref[s, here, :] = second_ref[s, here, :]
+
+
+def far_kernel(
+    share, count_ref, far_ref, basis_ref, stats_ref, first_ref, second_ref,
+    new_stats_hbm, new_first_hbm, new_second_hbm,
+    new_stats_ref, new_first_ref, new_second_ref, rotated_ref, spread_ref, grad_ref, sems,
+):
+    owners, slots, _, pieces, part = far_ref.shape
+    rows = owners * share
+    me = lax.axis_index("tensor")
+    start = pl.multiple_of(me * part, part)
+    base = lax.rem(me + 2, GROUPS) * share
+    copies = []
+    for s in range(slots):
+        live = s < count_ref[0]
+        grad_ref[s] = spread_rows(far_ref[:, s].reshape(rows, pieces, part), spread_ref)
+        gram = lax.dot_general(
+            grad_ref[s],
+            grad_ref[s, :, pl.ds(start, part)],
+            (((0,), (0,)), ((), ())),
+            preferred_element_type=jnp.float32,
+        )
+        stats = stats_ref[s]
+        new_stats_ref[s] = jnp.where(live, stats + (1.0 - beta_stat) * gram, stats)
+        rotated_ref[s] = jnp.dot(grad_ref[s], basis_ref[s], preferred_element_type=jnp.float32)
+        new_first_ref[s] = first_ref[s]
+        new_second_ref[s] = second_ref[s]
+        for r in range(share):
+            rotated = rotated_ref[s, pl.ds(r, owners, stride=share), :]
+            here = pl.ds(base + r, owners, stride=GROUPS * share)
+            first = first_ref[s, here, :]
+            second = second_ref[s, here, :]
+            new_first_ref[s, here, :] = jnp.where(
+                live, beta_one * first + (1.0 - beta_one) * rotated, first
+            )
+            new_second_ref[s, here, :] = jnp.where(
+                live, beta_two * second + (1.0 - beta_two) * rotated * rotated, second
+            )
+        for i, (ref, hbm) in enumerate((
+            (new_stats_ref, new_stats_hbm),
+            (new_first_ref, new_first_hbm),
+            (new_second_ref, new_second_hbm),
+        )):
+            copy = pltpu.make_async_copy(ref.at[s], hbm.at[s], sems.at[s, i])
+            copy.start()
+            copies.append(copy)
+    for copy in copies:
+        copy.wait()
+
+
+def add_kernel(partial_ref, update_ref):
+    groups, share = GROUPS, partial_ref.shape[2]
+    pieces, part = partial_ref.shape[1], partial_ref.shape[3]
+    total = partial_ref[:groups].astype(jnp.float32) + partial_ref[groups:].astype(jnp.float32)
+    for c in range(pieces):
+        update_ref[:, c * part : (c + 1) * part] = (
+            total[:, c].reshape(groups * share, part).astype(update_ref.dtype)
+        )
 
 
 def on_device(gradient, block_list, block_counts, stats, basis, first_moment, second_moment):
@@ -157,7 +248,7 @@
     share = rows_dev // GROUPS
     pieces = cols_dev // part
     vmem = pl.BlockSpec(memory_space=pltpu.VMEM)
-    params = pltpu.CompilerParams(vmem_limit_bytes=48 * 2**20)
+    params = pltpu.CompilerParams(vmem_limit_bytes=24 * 2**20)
 
     def own(kernel):
         return lambda *refs: kernel(share, *refs)
@@ -189,55 +280,77 @@
 
     outgoing = jnp.take(by_block, lists, axis=0, mode="clip")
     arrived = lax.all_to_all(outgoing, "dp", 0, 0, tiled=True)
-    grad_rows, back = pl.pallas_call(
-        own(rows_kernel),
-        out_shape=(
-            jax.ShapeDtypeStruct((slot_count, owners * share, width), jnp.bfloat16),
-            jax.ShapeDtypeStruct(arrived.shape, jnp.bfloat16),
-        ),
-        scratch_shapes=[
-            pltpu.VMEM((slot_count, GROUPS, owners * share, part), jnp.float32),
-            pltpu.VMEM((slot_count, GROUPS, owners * share, part), jnp.float32),
-            pltpu.VMEM((slot_count, owners * share * (width // part), part), jnp.float32),
-        ],
-        compiler_params=params,
-        name="rotate_rows",
-    )(arrived, basis[0], first_moment[0], second_moment[0], right, left, *far)
-
-    returned = lax.all_to_all(back, "dp", 0, 0, tiled=True)
     holds = (lists.reshape(-1)[None, :] == jnp.arange(blocks)[:, None]) & live.reshape(-1)[None, :]
     place = jnp.argmax(holds, axis=1)
+    rows = owners * share
+    operands = (arrived, basis[0], first_moment[0], second_moment[0], right, left, *far)
+    back = pl.pallas_call(
+        own(rows_kernel),
+        out_shape=jax.ShapeDtypeStruct(arrived.shape, jnp.bfloat16),
+        in_specs=[pl.BlockSpec(memory_space=pl.ANY)] * (len(operands) + 1),
+        out_specs=vmem,
+        scratch_shapes=[
+            pltpu.VMEM((slot_count, GROUPS, rows, part), jnp.float32),
+            pltpu.VMEM((slot_count, GROUPS, rows, part), jnp.float32),
+            pltpu.VMEM((rows * (width // part), part), jnp.float32),
+            *(pltpu.VMEM(x.shape, x.dtype) for x in operands[:6]),
+            pltpu.VMEM((slot_count, width + piece, part), jnp.bfloat16),
+            pltpu.SemaphoreType.DMA((slot_count, len(operands) + 1)),
+        ],
+        compiler_params=pltpu.CompilerParams(vmem_limit_bytes=ROWS_VMEM),
+        cost_estimate=pl.CostEstimate(flops=ROWS_FLOPS, bytes_accessed=2**23, transcendentals=0),
+        name="rotate_rows",
+    )(*operands, place)
+
+    returned = lax.all_to_all(back, "dp", 0, 0, tiled=True)
     placed = jnp.take(
         returned.reshape(owners * slot_count, share, width // part, part), place, axis=0, mode="clip"
     ).transpose(0, 2, 1, 3)
     partial = lax.all_to_all(
         placed.reshape(parts, pieces, share, part), "tensor", 0, 0, tiled=True
     )
-    update = (
-        partial.reshape(parts // GROUPS, GROUPS, pieces, share, part)
-        .astype(jnp.float32)
-        .sum(0)
-        .astype(jnp.bfloat16)
-        .transpose(0, 2, 1, 3)
-        .reshape(rows_dev, cols_dev)
-    )
-
-    right_rows, left_rows = shifted(grad_rows, parts, 1), shifted(grad_rows, parts, -1)
-    others = right_rows, left_rows, shifted(right_rows, parts, 1)
+    update = pl.pallas_call(
+        add_kernel,
+        out_shape=jax.ShapeDtypeStruct(gradient.shape, gradient.dtype),
+        compiler_params=params,
+        name="add",
+    )(partial)
+
+    right_rows, left_rows = shifted(arrived, parts, 1), shifted(arrived, parts, -1)
+    far_rows = shifted(right_rows, parts, 1)
+    states = (stats[0], first_moment[0], second_moment[0])
+    shapes = tuple(jax.ShapeDtypeStruct(x.shape, jnp.float32) for x in states)
+    smem = pl.BlockSpec(memory_space=pltpu.SMEM)
+    spread = pltpu.VMEM((rows * (width // part), part), jnp.float32)
+    near = pl.pallas_call(
+        own(near_kernel),
+        out_shape=shapes,
+        in_specs=[smem] + [vmem] * 7,
+        out_specs=(vmem,) * 3,
+        scratch_shapes=[
+            pltpu.VMEM((slot_count, 3 * rows, part), jnp.float32),
+            spread,
+            pltpu.VMEM((slot_count, 3 * rows, width), jnp.bfloat16),
+        ],
+        compiler_params=params,
+        cost_estimate=pl.CostEstimate(flops=2**32, bytes_accessed=2**24, transcendentals=0),
+        name="near_state",
+    )(block_counts, arrived, right_rows, left_rows, basis[0], *states)
     new_stats, new_first, new_second = pl.pallas_call(
-        own(state_kernel),
-        out_shape=(
-            jax.ShapeDtypeStruct(stats.shape[1:], jnp.float32),
-            jax.ShapeDtypeStruct(first_moment.shape[1:], jnp.float32),
-            jax.ShapeDtypeStruct(second_moment.shape[1:], jnp.float32),
-        ),
-        in_specs=[pl.BlockSpec(memory_space=pltpu.SMEM)] + [vmem] * 8,
-        out_specs=(vmem,) * 3,
-        scratch_shapes=[pltpu.VMEM((slot_count, GROUPS * owners * share, part), jnp.float32)],
+        own(far_kernel),
+        out_shape=shapes,
+        in_specs=[smem] + [vmem] * 5,
+        out_specs=(pl.BlockSpec(memory_space=pl.ANY),) * 3,
+        scratch_shapes=[
+            *(pltpu.VMEM(x.shape, x.dtype) for x in shapes),
+            pltpu.VMEM((slot_count, rows, part), jnp.float32),
+            spread,
+            pltpu.VMEM((slot_count, rows, width), jnp.bfloat16),
+            pltpu.SemaphoreType.DMA((slot_count, 3)),
+        ],
         compiler_params=params,
-        cost_estimate=pl.CostEstimate(flops=2**30, bytes_accessed=2**24, transcendentals=0),
-        name="new_state",
-    )(block_counts, grad_rows, *others, basis[0], stats[0], first_moment[0], second_moment[0])
+        name="far_state",
+    )(block_counts, far_rows, basis[0], *near)
     return (update, new_stats[None], new_first[None], new_second[None])
 
 

time: 133 us -> 129 us (0.970)
  local copies, waits for them, and re-layouts: 14 us -> 10.2 us
  waiting for transfers between devices: 28.9 us -> 25.8 us
  Pallas kernels: 8.5 us -> 11.3 us
    pallas_call x2 -> x4, Pallas kernels: 7.07 us -> 10.2 us  [the longest x1 4.35 us: on_device(): pl.pallas_call(own(rows_kernel), out_shape=jax.ShapeDtypeStruct(arrived.s...]
    ppermute x7, waiting for transfers between devices: 28.9 us -> 25.8 us  [shifted(): lax.ppermute(x, 'tensor', [((i + by) % parts, i) for i in range(parts)])]
    unnamed x23 -> x28, local copies, waits for them, and re-layouts: 6.64 us -> 3.86 us
  transfers between devices with their start and end apart: 11 -> 11, of which waited for: 4 -> 4; matrix products, arithmetic and copies ran while one was open for 5% -> 4% of each run, Pallas kernels for 4% -> 5%
where the time goes in v4:
time: 129 us; the launch traced here: 127 us
  starting transfers between devices  52 us (40%)
  waiting for transfers between devices  25.8 us (20%)
  blocking collectives  25 us (19%)
  Pallas kernels  11.3 us (9%)
  local copies, waits for them, and re-layouts  10.2 us (8%)
  between operations  1.64 us (1%)
    ppermute x7, waiting for transfers between devices, shifted(): lax.ppermute(x, 'tensor', [((i + by) % parts, i) for i in range(parts)])  25.8 us
    psum x1, blocking collectives, on_device(): flat = lax.psum(jnp.where(is_me, mine[None, :], 0).reshape(-1), 'dp')  25 us
    ppermute x7, starting transfers between devices, shifted(): lax.ppermute(x, 'tensor', [((i + by) % parts, i) for i in range(parts)])  23.3 us
    all_to_all x1, starting transfers between devices, on_device(): returned = lax.all_to_all(back, 'dp', 0, 0, tiled=True)  10.5 us
    all_to_all x1, starting transfers between devices, on_device(): moved = lax.all_to_all(leaving, 'tensor', 0, 0, tiled=True)  7.1 us
    all_to_all x1, starting transfers between devices, on_device(): arrived = lax.all_to_all(outgoing, 'dp', 0, 0, tiled=True)  6.53 us
    all_to_all x1, starting transfers between devices, on_device(): lax.all_to_all(placed.reshape(parts, pieces, share, part), 'tensor', 0, 0...  4.54 us
    pallas_call x1, Pallas kernels, on_device(): pl.pallas_call(own(rows_kernel), out_shape=jax.ShapeDtypeStruct(arrived.s...  4.35 us
  transfers between devices with their start and end apart: 11, of which 4 were waited for; matrix products, arithmetic and copies ran while one was open for 4% of the time, Pallas kernels for 5%

profile of v4, /device:TPU:6, one launch (start us, length us, event | category | flops | bytes accessed | tf_op | source)
XLA Modules:
  0.0 126.9 jit_solution(4830039981703645670)
XLA Ops:
  0.6 0.0 copy-start.2
  0.6 1.0 reshape.53
  1.7 0.0 copy-start
  1.7 0.1 copy.17
  1.8 0.8 tile.4
  2.6 7.1 %all-to-all-start = ((bf16[8,52,2,128]{3,2,1,0:T(2,128)(2,1)}), bf16[8,52,2,128]{3,2,1,0:T(2,128)(2,1)S(1)}, u32[]{:S(2)}, u32[]{:S(2)}) async-start(bf16[8,52,2,128]{3,2,1,0:T(2,128)(2,1)} %bitcast.1.refs_0_), calls=%async_computation | async-start | bytes 425984 | tf_op jit(solution)/shard_map/all_to_all | solution.py:265
  9.7 0.0 copy-done.2
  9.7 0.0 copy-done
  9.7 0.0 copy-start.4
  9.7 1.0 copy-done.4
  10.7 1.1 pack.1
  11.9 5.1 %collective-permute-start = (bf16[3584,128]{1,0:T(8,128)(2,1)}, bf16[3584,128]{1,0:T(8,128)(2,1)S(1)}, u32[]{:S(2)}, u32[]{:S(2)}) collective-permute-start(bf16[3584,128]{1,0:T(8,128)(2,1)} %get-tuple-element.13), channel_id=1, source_target_pairs={{1,0},{2,1},{3,2},{4,3},{5,4},{6,5},{7,6},{0,7},{9,8},{10,9},{11,1... | collective-permute-start | bytes 2752520 | tf_op jit(solution)/shard_map/ppermute | solution.py:24
  17.0 1.9 %collective-permute-start.1 = (bf16[3584,128]{1,0:T(8,128)(2,1)S(1)}, bf16[3584,128]{1,0:T(8,128)(2,1)}, u32[]{:S(2)}, u32[]{:S(2)}) collective-permute-start(bf16[3584,128]{1,0:T(8,128)(2,1)S(1)} %get-tuple-element.14), channel_id=1, source_target_pairs={{7,0},{0,1},{1,2},{2,3},{3,4},{4,5},{5,6},{6,7},{15,8},{8,9},{9,10... | collective-permute-start | bytes 2752520 | tf_op jit(solution)/shard_map/ppermute | solution.py:24
  19.6 0.0 copy-start.13
  19.6 0.6 copy-done.13
  20.2 0.1 pad_add_fusion
  20.3 0.1 broadcast_select_fusion
  20.4 25.0 %psum.7 = s32[64,3]{0,1:T(4,128)S(1)} all-reduce(s32[64,3]{0,1:T(4,128)S(1)} %broadcast_select_fusion), channel_id=1, replica_groups=mesh['dp'=64,'tensor'=8] {'dp'}, use_global_device_ids=true, to_apply=%region_0.1 | all-reduce | flops 192 | bytes 1536 | tf_op jit(solution)/shard_map/psum | solution.py:258
  45.4 0.1 copy.19
  45.5 0.1 reshape.61
  45.6 0.0 all-to-all-done
  45.7 1.5 %gather_fusion = bf16[128,2,8,128]{3,2,1,0:T(8,128)(2,1)} fusion(bf16[52,2,8,128]{3,2,1,0:T(8,128)(2,1)S(1)} %bitcast.31, s32[1024]{0:T(1024)S(1)} %pad_clamp_fusion.1), kind=kCustom, calls=%fused_computation | custom fusion | bytes 1049088 | tf_op jit(solution)/shard_map/jit(_take)/gather | solution.py:281
  47.2 6.5 %all-to-all-start.1 = ((bf16[64,2,2,8,128]{4,3,2,1,0:T(8,128)(2,1)}), bf16[64,2,2,8,128]{4,3,2,1,0:T(8,128)(2,1)S(1)}, u32[]{:S(2)}, u32[]{:S(2)}) async-start(bf16[64,2,2,8,128]{4,3,2,1,0:T(8,128)(2,1)} %bitcast.5), calls=%async_computation.1 | async-start | bytes 1048576 | tf_op jit(solution)/shard_map/all_to_all | solution.py:282
  53.7 0.0 collective-permute-done.refs_4_
  53.7 0.0 copy-start.9
  53.8 5.1 %collective-permute-start.2 = (bf16[1536,128]{1,0:T(8,128)(2,1)S(1)}, bf16[1536,128]{1,0:T(8,128)(2,1)S(1)}, u32[]{:S(2)}, u32[]{:S(2)}) collective-permute-start(bf16[1536,128]{1,0:T(8,128)(2,1)S(1)} %slice.20), channel_id=1, source_target_pairs={{1,0},{2,1},{3,2},{4,3},{5,4},{6,5},{7,6},{0,7},{9,8},{10,9},{11,1... | collective-permute-start | bytes 1179656 | tf_op jit(solution)/shard_map/ppermute | solution.py:24
  58.9 0.0 collective-permute-done.1.refs_5_
  58.9 1.0 slice.21
  60.0 1.9 %collective-permute-start.3 = (bf16[1536,128]{1,0:T(8,128)(2,1)S(1)}, bf16[1536,128]{1,0:T(8,128)(2,1)S(1)}, u32[]{:S(2)}, u32[]{:S(2)}) collective-permute-start(bf16[1536,128]{1,0:T(8,128)(2,1)S(1)} %slice.21), channel_id=1, source_target_pairs={{7,0},{0,1},{1,2},{2,3},{3,4},{4,5},{5,6},{6,7},{15,8},{8,9},{9,10... | collective-permute-start | bytes 1179656 | tf_op jit(solution)/shard_map/ppermute | solution.py:24
  61.9 0.1 iota_compare_fusion
  62.0 0.2 lt.28
  62.1 0.7 iota_reduce_fusion
  62.8 4.8 %collective-permute-done.2.refs_6_ = bf16[1536,128]{1,0:T(8,128)(2,1)S(1)} collective-permute-done((bf16[1536,128]{1,0:T(8,128)(2,1)S(1)}, bf16[1536,128]{1,0:T(8,128)(2,1)S(1)}, u32[]{:S(2)}, u32[]{:S(2)}) %collective-permute-start.2) | collective-permute-done | bytes 393248 | tf_op jit(solution)/shard_map/ppermute | solution.py:24
  67.6 6.4 %collective-permute-done.3.refs_7_ = bf16[1536,128]{1,0:T(8,128)(2,1)S(1)} collective-permute-done((bf16[1536,128]{1,0:T(8,128)(2,1)S(1)}, bf16[1536,128]{1,0:T(8,128)(2,1)S(1)}, u32[]{:S(2)}, u32[]{:S(2)}) %collective-permute-start.3) | collective-permute-done | bytes 393248 | tf_op jit(solution)/shard_map/ppermute | solution.py:24
  73.9 0.0 all-to-all-done.1.refs_0_.refs_1_
  74.0 0.0 copy-done.9
  74.0 0.0 copy-done.11
  74.0 0.7 copy-done.12
  74.7 0.2 copy-done.6
  74.9 4.4 %rotate_rows.1 = bf16[64,2,2,8,128]{4,3,2,1,0:T(8,128)(2,1)} custom-call(bf16[64,2,2,8,128]{4,3,2,1,0:T(8,128)(2,1)} %copy-done.6, bf16[2,1024,128]{2,1,0:T(8,128)(2,1)} %bitcast.20, f32[2,512,128]{2,1,0:T(8,128)} %bitcast.24, f32[2,512,128]{2,1,0:T(8,128)} %bitcast.27, bf16[3584,128]{1,0:T(8,128)(2,1)} %copy-done.9, ...), custom_call_target="tpu_custom_call" | custom-call | flops 17179869184 | bytes 8388608 | tf_op jit(solution)/shard_map/rotate_rows/pallas_call | solution.py:287
  79.2 0.0 copy-start.7
  79.2 0.0 copy-start.5
  79.3 10.5 %all-to-all-start.2 = ((bf16[64,2,2,8,128]{4,3,2,1,0:T(8,128)(2,1)}), bf16[64,2,2,8,128]{4,3,2,1,0:T(8,128)(2,1)S(1)}, u32[]{:S(2)}, u32[]{:S(2)}) async-start(bf16[64,2,2,8,128]{4,3,2,1,0:T(8,128)(2,1)} %rotate_rows.1), calls=%async_computation.2 | async-start | bytes 1048576 | tf_op jit(solution)/shard_map/all_to_all | solution.py:305
  89.8 0.0 copy-done.7
  89.8 1.9 %collective-permute-start.4 = (bf16[64,2,2,8,128]{4,3,2,1,0:T(8,128)(2,1)S(1)}, bf16[64,2,2,8,128]{4,3,2,1,0:T(8,128)(2,1)S(1)}, u32[]{:S(2)}, u32[]{:S(2)}) collective-permute-start(bf16[64,2,2,8,128]{4,3,2,1,0:T(8,128)(2,1)S(1)} %copy-done.7), channel_id=1, source_target_pairs={{1,0},{2,1},{3,2},{4,3},{5,4},{6,5},{7,6},{0,7},{9,8},{10,9},{11,1... | collective-permute-start | bytes 1572872 | tf_op jit(solution)/shard_map/ppermute | solution.py:24
  91.7 3.9 %collective-permute-start.6 = (bf16[64,2,2,8,128]{4,3,2,1,0:T(8,128)(2,1)S(1)}, bf16[64,2,2,8,128]{4,3,2,1,0:T(8,128)(2,1)}, u32[]{:S(2)}, u32[]{:S(2)}) collective-permute-start(bf16[64,2,2,8,128]{4,3,2,1,0:T(8,128)(2,1)S(1)} %copy-done.7), channel_id=1, source_target_pairs={{7,0},{0,1},{1,2},{2,3},{3,4},{4,5},{5,6},{6,7},{15,8},{8,9},{9,10... | collective-permute-start | bytes 1572872 | tf_op jit(solution)/shard_map/ppermute | solution.py:24
  95.7 10.0 %collective-permute-done.4.refs_2_ = bf16[64,2,2,8,128]{4,3,2,1,0:T(8,128)(2,1)S(1)} collective-permute-done((bf16[64,2,2,8,128]{4,3,2,1,0:T(8,128)(2,1)S(1)}, bf16[64,2,2,8,128]{4,3,2,1,0:T(8,128)(2,1)S(1)}, u32[]{:S(2)}, u32[]{:S(2)}) %collective-permute-start.4) | collective-permute-done | bytes 524320 | tf_op jit(solution)/shard_map/ppermute | solution.py:24
  105.7 3.4 %collective-permute-start.5 = (bf16[64,2,2,8,128]{4,3,2,1,0:T(8,128)(2,1)S(1)}, bf16[64,2,2,8,128]{4,3,2,1,0:T(8,128)(2,1)S(1)}, u32[]{:S(2)}, u32[]{:S(2)}) collective-permute-start(bf16[64,2,2,8,128]{4,3,2,1,0:T(8,128)(2,1)S(1)} %collective-permute-done.4.refs_2_), channel_id=1, source_target_pairs={{1,0},{2,1},{3,2},{4,3},{5,4},{6,5},{7,6},{0,7},{9,8},{10,9},{11,1... | collective-permute-start | bytes 1572872 | tf_op jit(solution)/shard_map/ppermute | solution.py:24
  109.1 0.0 copy-done.10
  109.1 0.0 all-to-all-done.2
  109.1 0.0 copy-start.3
  109.1 0.6 gather_fusion.1
  109.7 0.0 copy-start.1
  109.7 0.9 copy.20
  110.6 4.5 %all-to-all-start.3 = ((bf16[8,52,2,128]{3,2,1,0:T(2,128)(2,1)}), bf16[8,52,2,128]{3,2,1,0:T(2,128)(2,1)S(1)}, u32[]{:S(2)}, u32[]{:S(2)}) async-start(bf16[8,52,2,128]{3,2,1,0:T(2,128)(2,1)} %bitcast.34), calls=%async_computation.3 | async-start | bytes 425984 | tf_op jit(solution)/shard_map/all_to_all | solution.py:309
  115.1 0.0 collective-permute-done.6.refs_3_
  115.2 0.0 copy-done.5
  115.2 0.0 copy-start.8
  115.2 1.2 copy-done.8
  116.4 3.2 %near_state.1 = (f32[2,1024,128]{2,1,0:T(8,128)S(1)}, f32[2,512,128]{2,1,0:T(8,128)S(1)}, f32[2,512,128]{2,1,0:T(8,128)S(1)}) custom-call(s32[1]{0:T(128)S(6)} %copy.23.refs_0_, bf16[64,2,2,8,128]{4,3,2,1,0:T(8,128)(2,1)S(1)} %copy-done.7, bf16[64,2,2,8,128]{4,3,2,1,0:T(8,128)(2,1)S(1)} %collective-permute-done.4.refs_2_, ...), custom_call_target="tpu_custom_call" | custom-call | flops 4294967296 | bytes 16777216 | tf_op jit(solution)/shard_map/near_state/pallas_call | solution.py:325
  119.6 4.6 %collective-permute-done.5.refs_1_ = bf16[64,2,2,8,128]{4,3,2,1,0:T(8,128)(2,1)S(1)} collective-permute-done((bf16[64,2,2,8,128]{4,3,2,1,0:T(8,128)(2,1)S(1)}, bf16[64,2,2,8,128]{4,3,2,1,0:T(8,128)(2,1)S(1)}, u32[]{:S(2)}, u32[]{:S(2)}) %collective-permute-start.5) | collective-permute-done | bytes 524320 | tf_op jit(solution)/shard_map/ppermute | solution.py:24
  124.2 1.9 %far_state.1 = (f32[2,1024,128]{2,1,0:T(8,128)}, f32[2,512,128]{2,1,0:T(8,128)}, f32[2,512,128]{2,1,0:T(8,128)}) custom-call(s32[1]{0:T(128)S(6)} %copy.23.refs_0_, bf16[64,2,2,8,128]{4,3,2,1,0:T(8,128)(2,1)S(1)} %collective-permute-done.5.refs_1_, bf16[2,1024,128]{2,1,0:T(8,128)(2,1)S(1)} %bitcast.23, f32[2,1024,128]{2,1,0:T(8,128)S(1)} %get-tuple-element.16.refs_3_, ...), custom_call_target="tpu_custom_call" | custom-call | tf_op jit(solution)/shard_map/far_state/pallas_call | solution.py:339
  126.2 0.0 all-to-all-done.3.partial_ref
  126.2 0.8 add.5
  (13 shorter events, 0.1 us)
Async XLA Ops:
  0.6 9.0 %copy-start.2 = (f32[1,2,512,128]{3,2,1,0:T(8,128)S(1)}, f32[1,2,512,128]{3,2,1,0:T(8,128)}, u32[]{:S(2)}) copy-start(f32[1,2,512,128]{3,2,1,0:T(8,128)} %param.12) | copy-start | bytes 1572868
  1.7 8.0 %copy-start = (bf16[1,2,1024,128]{3,2,1,0:T(8,128)(2,1)S(1)}, bf16[1,2,1024,128]{3,2,1,0:T(8,128)(2,1)}, u32[]{:S(2)}) copy-start(bf16[1,2,1024,128]{3,2,1,0:T(8,128)(2,1)} %param.11) | copy-start | bytes 1572868
  2.6 43.1 %all-to-all-start = ((bf16[8,52,2,128]{3,2,1,0:T(2,128)(2,1)}), bf16[8,52,2,128]{3,2,1,0:T(2,128)(2,1)S(1)}, u32[]{:S(2)}, u32[]{:S(2)}) async-start(bf16[8,52,2,128]{3,2,1,0:T(2,128)(2,1)} %bitcast.1.refs_0_), calls=%async_computation | async-start | bytes 425984 | tf_op jit(solution)/shard_map/all_to_all | solution.py:265
  9.7 1.0 copy-start.4
  11.9 41.9 %collective-permute-start = (bf16[3584,128]{1,0:T(8,128)(2,1)}, bf16[3584,128]{1,0:T(8,128)(2,1)S(1)}, u32[]{:S(2)}, u32[]{:S(2)}) collective-permute-start(bf16[3584,128]{1,0:T(8,128)(2,1)} %get-tuple-element.13), channel_id=1, source_target_pairs={{1,0},{2,1},{3,2},{4,3},{5,4},{6,5},{7,6},{0,7},{9,8},{10,9},{11,1... | collective-permute-start | bytes 2752520 | tf_op jit(solution)/shard_map/ppermute | solution.py:24
  17.0 41.9 %collective-permute-start.1 = (bf16[3584,128]{1,0:T(8,128)(2,1)S(1)}, bf16[3584,128]{1,0:T(8,128)(2,1)}, u32[]{:S(2)}, u32[]{:S(2)}) collective-permute-start(bf16[3584,128]{1,0:T(8,128)(2,1)S(1)} %get-tuple-element.14), channel_id=1, source_target_pairs={{7,0},{0,1},{1,2},{2,3},{3,4},{4,5},{5,6},{6,7},{15,8},{8,9},{9,10... | collective-permute-start | bytes 2752520 | tf_op jit(solution)/shard_map/ppermute | solution.py:24
  19.6 0.7 copy-start.13
  47.2 26.8 %all-to-all-start.1 = ((bf16[64,2,2,8,128]{4,3,2,1,0:T(8,128)(2,1)}), bf16[64,2,2,8,128]{4,3,2,1,0:T(8,128)(2,1)S(1)}, u32[]{:S(2)}, u32[]{:S(2)}) async-start(bf16[64,2,2,8,128]{4,3,2,1,0:T(8,128)(2,1)} %bitcast.5), calls=%async_computation.1 | async-start | bytes 1048576 | tf_op jit(solution)/shard_map/all_to_all | solution.py:282
  53.7 20.2 %copy-start.9 = (bf16[3584,128]{1,0:T(8,128)(2,1)}, bf16[3584,128]{1,0:T(8,128)(2,1)S(1)}, u32[]{:S(2)}) copy-start(bf16[3584,128]{1,0:T(8,128)(2,1)S(1)} %collective-permute-done.refs_4_) | copy-start | bytes 2752516
  53.8 13.8 %collective-permute-start.2 = (bf16[1536,128]{1,0:T(8,128)(2,1)S(1)}, bf16[1536,128]{1,0:T(8,128)(2,1)S(1)}, u32[]{:S(2)}, u32[]{:S(2)}) collective-permute-start(bf16[1536,128]{1,0:T(8,128)(2,1)S(1)} %slice.20), channel_id=1, source_target_pairs={{1,0},{2,1},{3,2},{4,3},{5,4},{6,5},{7,6},{0,7},{9,8},{10,9},{11,1... | collective-permute-start | bytes 1179656 | tf_op jit(solution)/shard_map/ppermute | solution.py:24
  60.0 14.0 %collective-permute-start.3 = (bf16[1536,128]{1,0:T(8,128)(2,1)S(1)}, bf16[1536,128]{1,0:T(8,128)(2,1)S(1)}, u32[]{:S(2)}, u32[]{:S(2)}) collective-permute-start(bf16[1536,128]{1,0:T(8,128)(2,1)S(1)} %slice.21), channel_id=1, source_target_pairs={{7,0},{0,1},{1,2},{2,3},{3,4},{4,5},{5,6},{6,7},{15,8},{8,9},{9,10... | collective-permute-start | bytes 1179656 | tf_op jit(solution)/shard_map/ppermute | solution.py:24
  67.6 6.4 %copy-start.11 = (bf16[1536,128]{1,0:T(8,128)(2,1)}, bf16[1536,128]{1,0:T(8,128)(2,1)S(1)}, u32[]{:S(2)}) copy-start(bf16[1536,128]{1,0:T(8,128)(2,1)S(1)} %collective-permute-done.2.refs_6_) | copy-start | bytes 1179652
  73.9 0.8 copy-start.12
  73.9 0.9 copy-start.6
  74.9 34.2 %copy-start.10 = (s32[52]{0:T(128)S(1)}, s32[52]{0:T(128)}, u32[]{:S(2)}) copy-start(s32[52]{0:T(128)} %get-tuple-element.15.refs_8_) | copy-start | bytes 628
  79.2 10.6 %copy-start.7 = (bf16[64,2,2,8,128]{4,3,2,1,0:T(8,128)(2,1)S(1)}, bf16[64,2,2,8,128]{4,3,2,1,0:T(8,128)(2,1)}, u32[]{:S(2)}) copy-start(bf16[64,2,2,8,128]{4,3,2,1,0:T(8,128)(2,1)} %copy-done.6) | copy-start | bytes 1572868
  79.2 35.9 %copy-start.5 = (f32[1,2,512,128]{3,2,1,0:T(8,128)S(1)}, f32[1,2,512,128]{3,2,1,0:T(8,128)}, u32[]{:S(2)}) copy-start(f32[1,2,512,128]{3,2,1,0:T(8,128)} %param.13) | copy-start | bytes 1572868
  79.3 29.8 %all-to-all-start.2 = ((bf16[64,2,2,8,128]{4,3,2,1,0:T(8,128)(2,1)}), bf16[64,2,2,8,128]{4,3,2,1,0:T(8,128)(2,1)S(1)}, u32[]{:S(2)}, u32[]{:S(2)}) async-start(bf16[64,2,2,8,128]{4,3,2,1,0:T(8,128)(2,1)} %rotate_rows.1), calls=%async_computation.2 | async-start | bytes 1048576 | tf_op jit(solution)/shard_map/all_to_all | solution.py:305
  89.8 15.9 %collective-permute-start.4 = (bf16[64,2,2,8,128]{4,3,2,1,0:T(8,128)(2,1)S(1)}, bf16[64,2,2,8,128]{4,3,2,1,0:T(8,128)(2,1)S(1)}, u32[]{:S(2)}, u32[]{:S(2)}) collective-permute-start(bf16[64,2,2,8,128]{4,3,2,1,0:T(8,128)(2,1)S(1)} %copy-done.7), channel_id=1, source_target_pairs={{1,0},{2,1},{3,2},{4,3},{5,4},{6,5},{7,6},{0,7},{9,8},{10,9},{11,1... | collective-permute-start | bytes 1572872 | tf_op jit(solution)/shard_map/ppermute | solution.py:24
  91.7 23.4 %collective-permute-start.6 = (bf16[64,2,2,8,128]{4,3,2,1,0:T(8,128)(2,1)S(1)}, bf16[64,2,2,8,128]{4,3,2,1,0:T(8,128)(2,1)}, u32[]{:S(2)}, u32[]{:S(2)}) collective-permute-start(bf16[64,2,2,8,128]{4,3,2,1,0:T(8,128)(2,1)S(1)} %copy-done.7), channel_id=1, source_target_pairs={{7,0},{0,1},{1,2},{2,3},{3,4},{4,5},{5,6},{6,7},{15,8},{8,9},{9,10... | collective-permute-start | bytes 1572872 | tf_op jit(solution)/shard_map/ppermute | solution.py:24
  105.7 18.6 %collective-permute-start.5 = (bf16[64,2,2,8,128]{4,3,2,1,0:T(8,128)(2,1)S(1)}, bf16[64,2,2,8,128]{4,3,2,1,0:T(8,128)(2,1)S(1)}, u32[]{:S(2)}, u32[]{:S(2)}) collective-permute-start(bf16[64,2,2,8,128]{4,3,2,1,0:T(8,128)(2,1)S(1)} %collective-permute-done.4.refs_2_), channel_id=1, source_target_pairs={{1,0},{2,1},{3,2},{4,3},{5,4},{6,5},{7,6},{0,7},{9,8},{10,9},{11,1... | collective-permute-start | bytes 1572872 | tf_op jit(solution)/shard_map/ppermute | solution.py:24
  109.1 6.1 %copy-start.3 = (f32[1,2,512,128]{3,2,1,0:T(8,128)S(1)}, f32[1,2,512,128]{3,2,1,0:T(8,128)}, u32[]{:S(2)}) copy-start(f32[1,2,512,128]{3,2,1,0:T(8,128)} %param.12) | copy-start | bytes 1572868
  109.7 5.4 %copy-start.1 = (bf16[1,2,1024,128]{3,2,1,0:T(8,128)(2,1)S(1)}, bf16[1,2,1024,128]{3,2,1,0:T(8,128)(2,1)}, u32[]{:S(2)}) copy-start(bf16[1,2,1024,128]{3,2,1,0:T(8,128)(2,1)} %param.11) | copy-start | bytes 1572868
  110.6 15.5 %all-to-all-start.3 = ((bf16[8,52,2,128]{3,2,1,0:T(2,128)(2,1)}), bf16[8,52,2,128]{3,2,1,0:T(2,128)(2,1)S(1)}, u32[]{:S(2)}, u32[]{:S(2)}) async-start(bf16[8,52,2,128]{3,2,1,0:T(2,128)(2,1)} %bitcast.34), calls=%async_computation.3 | async-start | bytes 425984 | tf_op jit(solution)/shard_map/all_to_all | solution.py:309
  115.2 1.2 copy-start.8

commit v5 on v4

--- a/solution.py
+++ b/solution.py
@@ -22,6 +22,15 @@
 
 def shifted(x, parts, by):
     return lax.ppermute(x, "tensor", [((i + by) % parts, i) for i in range(parts)])
+
+
+def list_kernel(list_ref, count_ref, after_ref, sent_ref):
+    slots = list_ref.shape[1]
+    place = lax.broadcasted_iota(jnp.int32, sent_ref.shape, 2)
+    entry = jnp.where(place == slots, count_ref[0], 0)
+    for s in range(slots):
+        entry = jnp.where(place == s, list_ref[0, s], entry)
+    sent_ref[...] = entry
 
 
 def pack_kernel(share, after_ref, basis_ref, first_ref, second_ref, to_left_ref, to_right_ref):
@@ -248,22 +257,28 @@
     share = rows_dev // GROUPS
     pieces = cols_dev // part
     vmem = pl.BlockSpec(memory_space=pltpu.VMEM)
+    smem = pl.BlockSpec(memory_space=pltpu.SMEM)
     params = pltpu.CompilerParams(vmem_limit_bytes=24 * 2**20)
 
     def own(kernel):
         return lambda *refs: kernel(share, *refs)
-
-    mine = jnp.concatenate([block_list[0], block_counts])
-    is_me = jnp.arange(owners)[:, None] == lax.axis_index("dp")
-    flat = lax.psum(jnp.where(is_me, mine[None, :], 0).reshape(-1), "dp")
-    table = flat.reshape(owners, slot_count + 1)
-    lists = table[:, :slot_count]
-    live = jnp.arange(slot_count)[None, :] < table[:, slot_count:]
 
     groups = gradient.reshape(GROUPS, share, pieces, part).transpose(0, 2, 1, 3)
     leaving = jnp.tile(groups, (parts // GROUPS, 1, 1, 1))
     moved = lax.all_to_all(leaving, "tensor", 0, 0, tiled=True)
     by_block = moved.reshape(blocks, width // part, share, part).transpose(0, 2, 1, 3)
+
+    mine = pl.pallas_call(
+        list_kernel,
+        out_shape=jax.ShapeDtypeStruct((owners, 1, part), jnp.int32),
+        in_specs=[smem, smem, pl.BlockSpec(memory_space=pl.ANY)],
+        out_specs=vmem,
+        compiler_params=params,
+        name="list",
+    )(block_list, block_counts, moved)
+    table = lax.all_to_all(mine, "dp", 0, 0, tiled=True).reshape(owners, part)
+    lists = table[:, :slot_count]
+    live = jnp.arange(slot_count)[None, :] < table[:, slot_count : slot_count + 1]
 
     piece = 4 * share * owners
     sent = jax.ShapeDtypeStruct((2 * width + 3 * piece, part), jnp.bfloat16)
@@ -320,7 +335,6 @@
     far_rows = shifted(right_rows, parts, 1)
     states = (stats[0], first_moment[0], second_moment[0])
     shapes = tuple(jax.ShapeDtypeStruct(x.shape, jnp.float32) for x in states)
-    smem = pl.BlockSpec(memory_space=pltpu.SMEM)
     spread = pltpu.VMEM((rows * (width // part), part), jnp.float32)
     near = pl.pallas_call(
         own(near_kernel),

time: 129 us -> 126 us (0.977)
  blocking collectives: 25 us -> 0 us
  starting transfers between devices: 52 us -> 64.7 us
  waiting for transfers between devices: 25.8 us -> 34.6 us
    psum x1 -> x0, blocking collectives: 25 us -> none  [on_device(): flat = lax.psum(jnp.where(is_me, mine[None, :], 0).reshape(-1), 'dp')]
    all_to_all x0 -> x1, starting transfers between devices: none -> 13.8 us  [on_device(): table = lax.all_to_all(mine, 'dp', 0, 0, tiled=True).reshape(owners, part)]
    all_to_all x0 -> x1, waiting for transfers between devices: none -> 7.77 us  [on_device(): table = lax.all_to_all(mine, 'dp', 0, 0, tiled=True).reshape(owners, part)]
  transfers between devices with their start and end apart: 11 -> 12, of which waited for: 4 -> 6; matrix products, arithmetic and copies ran while one was open for 4% -> 4% of each run, Pallas kernels for 5% -> 6%
where the time goes in v5:
time: 126 us; the launch traced here: 124 us
  starting transfers between devices  64.7 us (51%)
  waiting for transfers between devices  34.6 us (27%)
  Pallas kernels  12.5 us (10%)
  local copies, waits for them, and re-layouts  9.6 us (8%)
  between operations  1.62 us (1%)
    ppermute x7, waiting for transfers between devices, shifted(): lax.ppermute(x, 'tensor', [((i + by) % parts, i) for i in range(parts)])  25.9 us
    ppermute x7, starting transfers between devices, shifted(): lax.ppermute(x, 'tensor', [((i + by) % parts, i) for i in range(parts)])  22.4 us
    all_to_all x1, starting transfers between devices, on_device(): table = lax.all_to_all(mine, 'dp', 0, 0, tiled=True).reshape(owners, part)  13.8 us
    all_to_all x1, starting transfers between devices, on_device(): returned = lax.all_to_all(back, 'dp', 0, 0, tiled=True)  10.5 us
    all_to_all x1, waiting for transfers between devices, on_device(): table = lax.all_to_all(mine, 'dp', 0, 0, tiled=True).reshape(owners, part)  7.77 us
    all_to_all x1, starting transfers between devices, on_device(): moved = lax.all_to_all(leaving, 'tensor', 0, 0, tiled=True)  7.1 us
    all_to_all x1, starting transfers between devices, on_device(): arrived = lax.all_to_all(outgoing, 'dp', 0, 0, tiled=True)  6.28 us
    all_to_all x1, starting transfers between devices, on_device(): lax.all_to_all(placed.reshape(parts, pieces, share, part), 'tensor', 0, 0...  4.52 us
  transfers between devices with their start and end apart: 12, of which 6 were waited for; matrix products, arithmetic and copies ran while one was open for 4% of the time, Pallas kernels for 6%

profile of v5, /device:TPU:6, one launch (start us, length us, event | category | flops | bytes accessed | tf_op | source)
XLA Modules:
  0.0 123.7 jit_solution(14085281718118042032)
XLA Ops:
  0.6 0.0 copy-start.2
  0.6 1.0 reshape.42
  1.7 0.0 copy-start
  1.7 0.1 copy.15
  1.8 0.8 tile.4
  2.6 7.1 %all-to-all-start = ((bf16[8,52,2,128]{3,2,1,0:T(2,128)(2,1)}), bf16[8,52,2,128]{3,2,1,0:T(2,128)(2,1)S(1)}, u32[]{:S(2)}, u32[]{:S(2)}) async-start(bf16[8,52,2,128]{3,2,1,0:T(2,128)(2,1)} %bitcast.1.refs_0_), calls=%async_computation | async-start | bytes 425984 | tf_op jit(solution)/shard_map/all_to_all | solution.py:268
  9.7 0.0 copy-done.2
  9.7 0.0 copy-done
  9.7 0.0 copy-start.4
  9.7 1.0 copy-done.4
  10.7 1.1 pack.1
  11.9 5.1 %collective-permute-start = (bf16[3584,128]{1,0:T(8,128)(2,1)}, bf16[3584,128]{1,0:T(8,128)(2,1)S(1)}, u32[]{:S(2)}, u32[]{:S(2)}) collective-permute-start(bf16[3584,128]{1,0:T(8,128)(2,1)} %get-tuple-element.13), channel_id=1, source_target_pairs={{1,0},{2,1},{3,2},{4,3},{5,4},{6,5},{7,6},{0,7},{9,8},{10,9},{11,1... | collective-permute-start | bytes 2752520 | tf_op jit(solution)/shard_map/ppermute | solution.py:24
  17.0 0.0 copy-start.8
  17.0 1.9 %collective-permute-start.1 = (bf16[3584,128]{1,0:T(8,128)(2,1)S(1)}, bf16[3584,128]{1,0:T(8,128)(2,1)}, u32[]{:S(2)}, u32[]{:S(2)}) collective-permute-start(bf16[3584,128]{1,0:T(8,128)(2,1)S(1)} %get-tuple-element.14), channel_id=1, source_target_pairs={{7,0},{0,1},{1,2},{2,3},{3,4},{4,5},{5,6},{6,7},{15,8},{8,9},{9,10... | collective-permute-start | bytes 2752520 | tf_op jit(solution)/shard_map/ppermute | solution.py:24
  19.6 0.9 all-to-all-done.after_ref
  20.5 0.0 copy-done.8
  20.5 1.2 list.1
  21.7 13.8 %all-to-all-start.1 = ((s32[64,1,128]{2,1,0:T(1,128)}), s32[64,1,128]{2,1,0:T(1,128)S(1)}, u32[]{:S(2)}, u32[]{:S(2)}) async-start(s32[64,1,128]{2,1,0:T(1,128)} %list.1), calls=%async_computation.1 | async-start | bytes 65536 | tf_op jit(solution)/shard_map/all_to_all | solution.py:279
  35.5 7.8 %all-to-all-done.1 = s32[64,1,128]{2,1,0:T(1,128)S(1)} async-done(((s32[64,1,128]{2,1,0:T(1,128)}), s32[64,1,128]{2,1,0:T(1,128)S(1)}, u32[]{:S(2)}, u32[]{:S(2)}) %all-to-all-start.1) | async-done | bytes 32800 | tf_op jit(solution)/shard_map/all_to_all | solution.py:279
  43.3 0.1 reshape.49
  43.5 1.5 %gather_fusion = bf16[128,2,8,128]{3,2,1,0:T(8,128)(2,1)} fusion(bf16[52,2,8,128]{3,2,1,0:T(8,128)(2,1)S(1)} %bitcast.31, s32[1024]{0:T(1024)S(1)} %pad_clamp_fusion.1), kind=kCustom, calls=%fused_computation | custom fusion | bytes 1049088 | tf_op jit(solution)/shard_map/jit(_take)/gather | solution.py:296
  44.9 6.3 %all-to-all-start.2 = ((bf16[64,2,2,8,128]{4,3,2,1,0:T(8,128)(2,1)}), bf16[64,2,2,8,128]{4,3,2,1,0:T(8,128)(2,1)S(1)}, u32[]{:S(2)}, u32[]{:S(2)}) async-start(bf16[64,2,2,8,128]{4,3,2,1,0:T(8,128)(2,1)} %bitcast.5), calls=%async_computation.2 | async-start | bytes 1048576 | tf_op jit(solution)/shard_map/all_to_all | solution.py:297
  51.2 0.2 slice_reduce_fusion
  51.4 0.0 collective-permute-done.refs_4_
  51.4 0.0 copy-start.10
  51.4 4.2 %collective-permute-start.2 = (bf16[1536,128]{1,0:T(8,128)(2,1)S(1)}, bf16[1536,128]{1,0:T(8,128)(2,1)S(1)}, u32[]{:S(2)}, u32[]{:S(2)}) collective-permute-start(bf16[1536,128]{1,0:T(8,128)(2,1)S(1)} %slice.21), channel_id=1, source_target_pairs={{1,0},{2,1},{3,2},{4,3},{5,4},{6,5},{7,6},{0,7},{9,8},{10,9},{11,1... | collective-permute-start | bytes 1179656 | tf_op jit(solution)/shard_map/ppermute | solution.py:24
  55.7 0.0 collective-permute-done.1.refs_5_
  55.7 1.0 slice.22
  56.7 1.9 %collective-permute-start.3 = (bf16[1536,128]{1,0:T(8,128)(2,1)S(1)}, bf16[1536,128]{1,0:T(8,128)(2,1)S(1)}, u32[]{:S(2)}, u32[]{:S(2)}) collective-permute-start(bf16[1536,128]{1,0:T(8,128)(2,1)S(1)} %slice.22), channel_id=1, source_target_pairs={{7,0},{0,1},{1,2},{2,3},{3,4},{4,5},{5,6},{6,7},{15,8},{8,9},{9,10... | collective-permute-start | bytes 1179656 | tf_op jit(solution)/shard_map/ppermute | solution.py:24
  58.7 0.1 iota_compare_fusion
  58.7 0.2 lt.28
  58.9 0.6 iota_reduce_fusion
  59.5 5.0 %collective-permute-done.2.refs_6_ = bf16[1536,128]{1,0:T(8,128)(2,1)S(1)} collective-permute-done((bf16[1536,128]{1,0:T(8,128)(2,1)S(1)}, bf16[1536,128]{1,0:T(8,128)(2,1)S(1)}, u32[]{:S(2)}, u32[]{:S(2)}) %collective-permute-start.2) | collective-permute-done | bytes 393248 | tf_op jit(solution)/shard_map/ppermute | solution.py:24
  64.5 6.2 %collective-permute-done.3.refs_7_ = bf16[1536,128]{1,0:T(8,128)(2,1)S(1)} collective-permute-done((bf16[1536,128]{1,0:T(8,128)(2,1)S(1)}, bf16[1536,128]{1,0:T(8,128)(2,1)S(1)}, u32[]{:S(2)}, u32[]{:S(2)}) %collective-permute-start.3) | collective-permute-done | bytes 393248 | tf_op jit(solution)/shard_map/ppermute | solution.py:24
  70.7 0.0 all-to-all-done.2.refs_0_.refs_1_
  70.7 0.0 copy-done.10
  70.7 0.0 copy-done.12
  70.7 0.7 copy-done.13
  71.5 0.2 copy-done.6
  71.7 4.4 %rotate_rows.1 = bf16[64,2,2,8,128]{4,3,2,1,0:T(8,128)(2,1)} custom-call(bf16[64,2,2,8,128]{4,3,2,1,0:T(8,128)(2,1)} %copy-done.6, bf16[2,1024,128]{2,1,0:T(8,128)(2,1)} %bitcast.19, f32[2,512,128]{2,1,0:T(8,128)} %bitcast.24, f32[2,512,128]{2,1,0:T(8,128)} %bitcast.27, bf16[3584,128]{1,0:T(8,128)(2,1)} %copy-done.10, ...), custom_call_target="tpu_custom_call" | custom-call | flops 17179869184 | bytes 8388608 | tf_op jit(solution)/shard_map/rotate_rows/pallas_call | solution.py:302
  76.0 0.0 copy-start.7
  76.0 0.0 copy-start.5
  76.0 10.5 %all-to-all-start.3 = ((bf16[64,2,2,8,128]{4,3,2,1,0:T(8,128)(2,1)}), bf16[64,2,2,8,128]{4,3,2,1,0:T(8,128)(2,1)S(1)}, u32[]{:S(2)}, u32[]{:S(2)}) async-start(bf16[64,2,2,8,128]{4,3,2,1,0:T(8,128)(2,1)} %rotate_rows.1), calls=%async_computation.3 | async-start | bytes 1048576 | tf_op jit(solution)/shard_map/all_to_all | solution.py:320
  86.6 1.9 %collective-permute-start.4 = (bf16[64,2,2,8,128]{4,3,2,1,0:T(8,128)(2,1)S(1)}, bf16[64,2,2,8,128]{4,3,2,1,0:T(8,128)(2,1)S(1)}, u32[]{:S(2)}, u32[]{:S(2)}) collective-permute-start(bf16[64,2,2,8,128]{4,3,2,1,0:T(8,128)(2,1)S(1)} %copy-done.7), channel_id=1, source_target_pairs={{1,0},{2,1},{3,2},{4,3},{5,4},{6,5},{7,6},{0,7},{9,8},{10,9},{11,1... | collective-permute-start | bytes 1572872 | tf_op jit(solution)/shard_map/ppermute | solution.py:24
  88.5 3.9 %collective-permute-start.6 = (bf16[64,2,2,8,128]{4,3,2,1,0:T(8,128)(2,1)S(1)}, bf16[64,2,2,8,128]{4,3,2,1,0:T(8,128)(2,1)}, u32[]{:S(2)}, u32[]{:S(2)}) collective-permute-start(bf16[64,2,2,8,128]{4,3,2,1,0:T(8,128)(2,1)S(1)} %copy-done.7), channel_id=1, source_target_pairs={{7,0},{0,1},{1,2},{2,3},{3,4},{4,5},{5,6},{6,7},{15,8},{8,9},{9,10... | collective-permute-start | bytes 1572872 | tf_op jit(solution)/shard_map/ppermute | solution.py:24
  92.4 10.0 %collective-permute-done.4.refs_2_ = bf16[64,2,2,8,128]{4,3,2,1,0:T(8,128)(2,1)S(1)} collective-permute-done((bf16[64,2,2,8,128]{4,3,2,1,0:T(8,128)(2,1)S(1)}, bf16[64,2,2,8,128]{4,3,2,1,0:T(8,128)(2,1)S(1)}, u32[]{:S(2)}, u32[]{:S(2)}) %collective-permute-start.4) | collective-permute-done | bytes 524320 | tf_op jit(solution)/shard_map/ppermute | solution.py:24
  102.5 3.4 %collective-permute-start.5 = (bf16[64,2,2,8,128]{4,3,2,1,0:T(8,128)(2,1)S(1)}, bf16[64,2,2,8,128]{4,3,2,1,0:T(8,128)(2,1)S(1)}, u32[]{:S(2)}, u32[]{:S(2)}) collective-permute-start(bf16[64,2,2,8,128]{4,3,2,1,0:T(8,128)(2,1)S(1)} %collective-permute-done.4.refs_2_), channel_id=1, source_target_pairs={{1,0},{2,1},{3,2},{4,3},{5,4},{6,5},{7,6},{0,7},{9,8},{10,9},{11,1... | collective-permute-start | bytes 1572872 | tf_op jit(solution)/shard_map/ppermute | solution.py:24
  105.9 0.0 all-to-all-done.3
  105.9 0.0 copy-start.3
  105.9 0.6 gather_fusion.1
  106.5 0.0 copy-start.1
  106.5 0.8 copy.17
  107.4 4.5 %all-to-all-start.4 = ((bf16[8,52,2,128]{3,2,1,0:T(2,128)(2,1)}), bf16[8,52,2,128]{3,2,1,0:T(2,128)(2,1)S(1)}, u32[]{:S(2)}, u32[]{:S(2)}) async-start(bf16[8,52,2,128]{3,2,1,0:T(2,128)(2,1)} %bitcast.33), calls=%async_computation.4 | async-start | bytes 425984 | tf_op jit(solution)/shard_map/all_to_all | solution.py:324
  111.9 0.0 collective-permute-done.6.refs_3_
  111.9 0.0 copy-done.5
  111.9 0.0 copy-done.3
  111.9 0.0 copy-done.1
  111.9 0.0 copy-start.9
  111.9 1.2 copy-done.9
  113.2 3.2 %near_state.1 = (f32[2,1024,128]{2,1,0:T(8,128)S(1)}, f32[2,512,128]{2,1,0:T(8,128)S(1)}, f32[2,512,128]{2,1,0:T(8,128)S(1)}) custom-call(s32[1]{0:T(128)S(6)} %copy.20.count_ref.refs_0_, bf16[64,2,2,8,128]{4,3,2,1,0:T(8,128)(2,1)S(1)} %copy-done.7, bf16[64,2,2,8,128]{4,3,2,1,0:T(8,128)(2,1)S(1)} %collective-permute-done.4.refs_2_, ...), custom_call_target="tpu_custom_call" | custom-call | flops 4294967296 | bytes 16777216 | tf_op jit(solution)/shard_map/near_state/pallas_call | solution.py:339
  116.3 4.7 %collective-permute-done.5.refs_1_ = bf16[64,2,2,8,128]{4,3,2,1,0:T(8,128)(2,1)S(1)} collective-permute-done((bf16[64,2,2,8,128]{4,3,2,1,0:T(8,128)(2,1)S(1)}, bf16[64,2,2,8,128]{4,3,2,1,0:T(8,128)(2,1)S(1)}, u32[]{:S(2)}, u32[]{:S(2)}) %collective-permute-start.5) | collective-permute-done | bytes 524320 | tf_op jit(solution)/shard_map/ppermute | solution.py:24
  121.0 1.9 %far_state.1 = (f32[2,1024,128]{2,1,0:T(8,128)}, f32[2,512,128]{2,1,0:T(8,128)}, f32[2,512,128]{2,1,0:T(8,128)}) custom-call(s32[1]{0:T(128)S(6)} %copy.20.count_ref.refs_0_, bf16[64,2,2,8,128]{4,3,2,1,0:T(8,128)(2,1)S(1)} %collective-permute-done.5.refs_1_, bf16[2,1024,128]{2,1,0:T(8,128)(2,1)S(1)} %bitcast.22, ...), custom_call_target="tpu_custom_call" | custom-call | tf_op jit(solution)/shard_map/far_state/pallas_call | solution.py:353
  122.9 0.0 all-to-all-done.4.partial_ref
  123.0 0.8 add.2
  (10 shorter events, 0.1 us)
Async XLA Ops:
  0.6 9.0 %copy-start.2 = (f32[1,2,512,128]{3,2,1,0:T(8,128)S(1)}, f32[1,2,512,128]{3,2,1,0:T(8,128)}, u32[]{:S(2)}) copy-start(f32[1,2,512,128]{3,2,1,0:T(8,128)} %param.12) | copy-start | bytes 1572868
  1.7 8.0 %copy-start = (bf16[1,2,1024,128]{3,2,1,0:T(8,128)(2,1)S(1)}, bf16[1,2,1024,128]{3,2,1,0:T(8,128)(2,1)}, u32[]{:S(2)}) copy-start(bf16[1,2,1024,128]{3,2,1,0:T(8,128)(2,1)} %param.11) | copy-start | bytes 1572868
  2.6 17.9 %all-to-all-start = ((bf16[8,52,2,128]{3,2,1,0:T(2,128)(2,1)}), bf16[8,52,2,128]{3,2,1,0:T(2,128)(2,1)S(1)}, u32[]{:S(2)}, u32[]{:S(2)}) async-start(bf16[8,52,2,128]{3,2,1,0:T(2,128)(2,1)} %bitcast.1.refs_0_), calls=%async_computation | async-start | bytes 425984 | tf_op jit(solution)/shard_map/all_to_all | solution.py:268
  9.7 1.0 copy-start.4
  11.9 39.5 %collective-permute-start = (bf16[3584,128]{1,0:T(8,128)(2,1)}, bf16[3584,128]{1,0:T(8,128)(2,1)S(1)}, u32[]{:S(2)}, u32[]{:S(2)}) collective-permute-start(bf16[3584,128]{1,0:T(8,128)(2,1)} %get-tuple-element.13), channel_id=1, source_target_pairs={{1,0},{2,1},{3,2},{4,3},{5,4},{6,5},{7,6},{0,7},{9,8},{10,9},{11,1... | collective-permute-start | bytes 2752520 | tf_op jit(solution)/shard_map/ppermute | solution.py:24
  17.0 3.5 %copy-start.8 = (s32[1,2]{1,0:T(1,128)S(1)}, s32[1,2]{1,0:T(1,128)}, u32[]{:S(2)}) copy-start(s32[1,2]{1,0:T(1,128)} %list_ref.1) | copy-start | bytes 28
  17.0 38.7 %collective-permute-start.1 = (bf16[3584,128]{1,0:T(8,128)(2,1)S(1)}, bf16[3584,128]{1,0:T(8,128)(2,1)}, u32[]{:S(2)}, u32[]{:S(2)}) collective-permute-start(bf16[3584,128]{1,0:T(8,128)(2,1)S(1)} %get-tuple-element.14), channel_id=1, source_target_pairs={{7,0},{0,1},{1,2},{2,3},{3,4},{4,5},{5,6},{6,7},{15,8},{8,9},{9,10... | collective-permute-start | bytes 2752520 | tf_op jit(solution)/shard_map/ppermute | solution.py:24
  21.7 21.6 %all-to-all-start.1 = ((s32[64,1,128]{2,1,0:T(1,128)}), s32[64,1,128]{2,1,0:T(1,128)S(1)}, u32[]{:S(2)}, u32[]{:S(2)}) async-start(s32[64,1,128]{2,1,0:T(1,128)} %list.1), calls=%async_computation.1 | async-start | bytes 65536 | tf_op jit(solution)/shard_map/all_to_all | solution.py:279
  44.9 25.8 %all-to-all-start.2 = ((bf16[64,2,2,8,128]{4,3,2,1,0:T(8,128)(2,1)}), bf16[64,2,2,8,128]{4,3,2,1,0:T(8,128)(2,1)S(1)}, u32[]{:S(2)}, u32[]{:S(2)}) async-start(bf16[64,2,2,8,128]{4,3,2,1,0:T(8,128)(2,1)} %bitcast.5), calls=%async_computation.2 | async-start | bytes 1048576 | tf_op jit(solution)/shard_map/all_to_all | solution.py:297
  51.4 19.3 %copy-start.10 = (bf16[3584,128]{1,0:T(8,128)(2,1)}, bf16[3584,128]{1,0:T(8,128)(2,1)S(1)}, u32[]{:S(2)}) copy-start(bf16[3584,128]{1,0:T(8,128)(2,1)S(1)} %collective-permute-done.refs_4_) | copy-start | bytes 2752516
  51.4 13.1 %collective-permute-start.2 = (bf16[1536,128]{1,0:T(8,128)(2,1)S(1)}, bf16[1536,128]{1,0:T(8,128)(2,1)S(1)}, u32[]{:S(2)}, u32[]{:S(2)}) collective-permute-start(bf16[1536,128]{1,0:T(8,128)(2,1)S(1)} %slice.21), channel_id=1, source_target_pairs={{1,0},{2,1},{3,2},{4,3},{5,4},{6,5},{7,6},{0,7},{9,8},{10,9},{11,1... | collective-permute-start | bytes 1179656 | tf_op jit(solution)/shard_map/ppermute | solution.py:24
  56.7 14.0 %collective-permute-start.3 = (bf16[1536,128]{1,0:T(8,128)(2,1)S(1)}, bf16[1536,128]{1,0:T(8,128)(2,1)S(1)}, u32[]{:S(2)}, u32[]{:S(2)}) collective-permute-start(bf16[1536,128]{1,0:T(8,128)(2,1)S(1)} %slice.22), channel_id=1, source_target_pairs={{7,0},{0,1},{1,2},{2,3},{3,4},{4,5},{5,6},{6,7},{15,8},{8,9},{9,10... | collective-permute-start | bytes 1179656 | tf_op jit(solution)/shard_map/ppermute | solution.py:24
  64.5 6.2 %copy-start.12 = (bf16[1536,128]{1,0:T(8,128)(2,1)}, bf16[1536,128]{1,0:T(8,128)(2,1)S(1)}, u32[]{:S(2)}) copy-start(bf16[1536,128]{1,0:T(8,128)(2,1)S(1)} %collective-permute-done.2.refs_6_) | copy-start | bytes 1179652
  70.7 0.7 copy-start.13
  70.7 0.9 copy-start.6
  71.6 34.2 %copy-start.11 = (s32[52]{0:T(128)S(1)}, s32[52]{0:T(128)}, u32[]{:S(2)}) copy-start(s32[52]{0:T(128)} %get-tuple-element.15.refs_8_) | copy-start | bytes 628
  76.0 10.6 %copy-start.7 = (bf16[64,2,2,8,128]{4,3,2,1,0:T(8,128)(2,1)S(1)}, bf16[64,2,2,8,128]{4,3,2,1,0:T(8,128)(2,1)}, u32[]{:S(2)}) copy-start(bf16[64,2,2,8,128]{4,3,2,1,0:T(8,128)(2,1)} %copy-done.6) | copy-start | bytes 1572868
  76.0 35.9 %copy-start.5 = (f32[1,2,512,128]{3,2,1,0:T(8,128)S(1)}, f32[1,2,512,128]{3,2,1,0:T(8,128)}, u32[]{:S(2)}) copy-start(f32[1,2,512,128]{3,2,1,0:T(8,128)} %param.13) | copy-start | bytes 1572868
  76.0 29.9 %all-to-all-start.3 = ((bf16[64,2,2,8,128]{4,3,2,1,0:T(8,128)(2,1)}), bf16[64,2,2,8,128]{4,3,2,1,0:T(8,128)(2,1)S(1)}, u32[]{:S(2)}, u32[]{:S(2)}) async-start(bf16[64,2,2,8,128]{4,3,2,1,0:T(8,128)(2,1)} %rotate_rows.1), calls=%async_computation.3 | async-start | bytes 1048576 | tf_op jit(solution)/shard_map/all_to_all | solution.py:320
  86.6 15.9 %collective-permute-start.4 = (bf16[64,2,2,8,128]{4,3,2,1,0:T(8,128)(2,1)S(1)}, bf16[64,2,2,8,128]{4,3,2,1,0:T(8,128)(2,1)S(1)}, u32[]{:S(2)}, u32[]{:S(2)}) collective-permute-start(bf16[64,2,2,8,128]{4,3,2,1,0:T(8,128)(2,1)S(1)} %copy-done.7), channel_id=1, source_target_pairs={{1,0},{2,1},{3,2},{4,3},{5,4},{6,5},{7,6},{0,7},{9,8},{10,9},{11,1... | collective-permute-start | bytes 1572872 | tf_op jit(solution)/shard_map/ppermute | solution.py:24
  88.5 23.4 %collective-permute-start.6 = (bf16[64,2,2,8,128]{4,3,2,1,0:T(8,128)(2,1)S(1)}, bf16[64,2,2,8,128]{4,3,2,1,0:T(8,128)(2,1)}, u32[]{:S(2)}, u32[]{:S(2)}) collective-permute-start(bf16[64,2,2,8,128]{4,3,2,1,0:T(8,128)(2,1)S(1)} %copy-done.7), channel_id=1, source_target_pairs={{7,0},{0,1},{1,2},{2,3},{3,4},{4,5},{5,6},{6,7},{15,8},{8,9},{9,10... | collective-permute-start | bytes 1572872 | tf_op jit(solution)/shard_map/ppermute | solution.py:24
  102.5 18.6 %collective-permute-start.5 = (bf16[64,2,2,8,128]{4,3,2,1,0:T(8,128)(2,1)S(1)}, bf16[64,2,2,8,128]{4,3,2,1,0:T(8,128)(2,1)S(1)}, u32[]{:S(2)}, u32[]{:S(2)}) collective-permute-start(bf16[64,2,2,8,128]{4,3,2,1,0:T(8,128)(2,1)S(1)} %collective-permute-done.4.refs_2_), channel_id=1, source_target_pairs={{1,0},{2,1},{3,2},{4,3},{5,4},{6,5},{7,6},{0,7},{9,8},{10,9},{11,1... | collective-permute-start | bytes 1572872 | tf_op jit(solution)/shard_map/ppermute | solution.py:24
  105.9 6.0 %copy-start.3 = (f32[1,2,512,128]{3,2,1,0:T(8,128)S(1)}, f32[1,2,512,128]{3,2,1,0:T(8,128)}, u32[]{:S(2)}) copy-start(f32[1,2,512,128]{3,2,1,0:T(8,128)} %param.12) | copy-start | bytes 1572868
  106.5 5.4 %copy-start.1 = (bf16[1,2,1024,128]{3,2,1,0:T(8,128)(2,1)S(1)}, bf16[1,2,1024,128]{3,2,1,0:T(8,128)(2,1)}, u32[]{:S(2)}) copy-start(bf16[1,2,1024,128]{3,2,1,0:T(8,128)(2,1)} %param.11) | copy-start | bytes 1572868
  107.4 15.6 %all-to-all-start.4 = ((bf16[8,52,2,128]{3,2,1,0:T(2,128)(2,1)}), bf16[8,52,2,128]{3,2,1,0:T(2,128)(2,1)S(1)}, u32[]{:S(2)}, u32[]{:S(2)}) async-start(bf16[8,52,2,128]{3,2,1,0:T(2,128)(2,1)} %bitcast.33), calls=%async_computation.4 | async-start | bytes 425984 | tf_op jit(solution)/shard_map/all_to_all | solution.py:324
  111.9 1.2 copy-start.9

commit v6 on v5

--- a/solution.py
+++ b/solution.py
@@ -24,7 +24,11 @@
     return lax.ppermute(x, "tensor", [((i + by) % parts, i) for i in range(parts)])
 
 
-def list_kernel(list_ref, count_ref, after_ref, sent_ref):
+def after_kernel(sent_ref, after_ref, out_ref):
+    pass
+
+
+def list_kernel(list_ref, count_ref, sent_ref):
     slots = list_ref.shape[1]
     place = lax.broadcasted_iota(jnp.int32, sent_ref.shape, 2)
     entry = jnp.where(place == slots, count_ref[0], 0)
@@ -271,11 +275,19 @@
     mine = pl.pallas_call(
         list_kernel,
         out_shape=jax.ShapeDtypeStruct((owners, 1, part), jnp.int32),
-        in_specs=[smem, smem, pl.BlockSpec(memory_space=pl.ANY)],
+        in_specs=[smem, smem],
         out_specs=vmem,
         compiler_params=params,
         name="list",
-    )(block_list, block_counts, moved)
+    )(block_list, block_counts)
+    mine = pl.pallas_call(
+        after_kernel,
+        out_shape=jax.ShapeDtypeStruct(mine.shape, mine.dtype),
+        in_specs=[pl.BlockSpec(memory_space=pl.ANY)] * 2,
+        out_specs=pl.BlockSpec(memory_space=pl.ANY),
+        input_output_aliases={0: 0},
+        name="after",
+    )(mine, moved)
     table = lax.all_to_all(mine, "dp", 0, 0, tiled=True).reshape(owners, part)
     lists = table[:, :slot_count]
     live = jnp.arange(slot_count)[None, :] < table[:, slot_count : slot_count + 1]

time: 126 us -> 126 us (level)
  local copies, waits for them, and re-layouts: 9.6 us -> 11.8 us
  Pallas kernels: 12.5 us -> 11 us
  waiting for transfers between devices: 34.6 us -> 33.3 us
    unnamed x28 -> x30, local copies, waits for them, and re-layouts: 3.22 us -> 4.51 us
  transfers between devices with their start and end apart: 12 -> 12, of which waited for: 6 -> 6; matrix products, arithmetic and copies ran while one was open for 4% -> 5% of each run, Pallas kernels for 6% -> 5%
where the time goes in v6:
time: 126 us; the launch traced here: 124 us
  starting transfers between devices  65 us (52%)
  waiting for transfers between devices  33.3 us (26%)
  local copies, waits for them, and re-layouts  11.8 us (9%)
  Pallas kernels  11 us (9%)
  between operations  1.63 us (1%)
    ppermute x7, waiting for transfers between devices, shifted(): lax.ppermute(x, 'tensor', [((i + by) % parts, i) for i in range(parts)])  25.8 us
    ppermute x7, starting transfers between devices, shifted(): lax.ppermute(x, 'tensor', [((i + by) % parts, i) for i in range(parts)])  22.7 us
    all_to_all x1, starting transfers between devices, on_device(): table = lax.all_to_all(mine, 'dp', 0, 0, tiled=True).reshape(owners, part)  13.8 us
    all_to_all x1, starting transfers between devices, on_device(): returned = lax.all_to_all(back, 'dp', 0, 0, tiled=True)  10.5 us
    all_to_all x1, starting transfers between devices, on_device(): moved = lax.all_to_all(leaving, 'tensor', 0, 0, tiled=True)  7.1 us
    all_to_all x1, waiting for transfers between devices, on_device(): table = lax.all_to_all(mine, 'dp', 0, 0, tiled=True).reshape(owners, part)  6.84 us
    all_to_all x1, starting transfers between devices, on_device(): arrived = lax.all_to_all(outgoing, 'dp', 0, 0, tiled=True)  6.28 us
    all_to_all x1, starting transfers between devices, on_device(): lax.all_to_all(placed.reshape(parts, pieces, share, part), 'tensor', 0, 0...  4.53 us
  transfers between devices with their start and end apart: 12, of which 6 were waited for; matrix products, arithmetic and copies ran while one was open for 5% of the time, Pallas kernels for 5%

profile of v6, /device:TPU:6, one launch (start us, length us, event | category | flops | bytes accessed | tf_op | source)
XLA Modules:
  0.0 123.5 jit_solution(15150362572586062420)
XLA Ops:
  0.6 0.0 copy-start.2
  0.6 1.0 reshape.42
  1.7 0.0 copy-start
  1.7 0.1 copy.16
  1.8 0.8 tile.4
  2.6 7.1 %all-to-all-start = ((bf16[8,52,2,128]{3,2,1,0:T(2,128)(2,1)}), bf16[8,52,2,128]{3,2,1,0:T(2,128)(2,1)S(1)}, u32[]{:S(2)}, u32[]{:S(2)}) async-start(bf16[8,52,2,128]{3,2,1,0:T(2,128)(2,1)} %bitcast.1.refs_0_), calls=%async_computation | async-start | bytes 425984 | tf_op jit(solution)/shard_map/all_to_all | solution.py:272
  9.7 0.0 copy-done.2
  9.7 0.0 copy-start.4
  9.7 1.0 copy-done.4
  10.7 0.2 pack.1
  10.9 5.1 %collective-permute-start = (bf16[3584,128]{1,0:T(8,128)(2,1)S(1)}, bf16[3584,128]{1,0:T(8,128)(2,1)S(1)}, u32[]{:S(2)}, u32[]{:S(2)}) collective-permute-start(bf16[3584,128]{1,0:T(8,128)(2,1)S(1)} %get-tuple-element.13), channel_id=1, source_target_pairs={{1,0},{2,1},{3,2},{4,3},{5,4},{6,5},{7,6},{0,7},{9,8},{10,9},{11,1... | collective-permute-start | bytes 2752520 | tf_op jit(solution)/shard_map/ppermute | solution.py:24
  16.1 0.0 copy-start.9
  16.1 1.9 %collective-permute-start.1 = (bf16[3584,128]{1,0:T(8,128)(2,1)S(1)}, bf16[3584,128]{1,0:T(8,128)(2,1)}, u32[]{:S(2)}, u32[]{:S(2)}) collective-permute-start(bf16[3584,128]{1,0:T(8,128)(2,1)S(1)} %get-tuple-element.14), channel_id=1, source_target_pairs={{7,0},{0,1},{1,2},{2,3},{3,4},{4,5},{5,6},{6,7},{15,8},{8,9},{9,10... | collective-permute-start | bytes 2752520 | tf_op jit(solution)/shard_map/ppermute | solution.py:24
  18.7 0.6 list.1.sent_ref
  19.3 0.0 copy-start.8
  19.3 0.6 copy-done.8
  19.9 0.6 all-to-all-done.after_ref
  20.5 0.7 copy-done.11
  21.2 13.8 %all-to-all-start.1 = ((s32[64,1,128]{2,1,0:T(1,128)}), s32[64,1,128]{2,1,0:T(1,128)S(1)}, u32[]{:S(2)}, u32[]{:S(2)}) async-start(s32[64,1,128]{2,1,0:T(1,128)} %after.1), calls=%async_computation.1 | async-start | bytes 65536 | tf_op jit(solution)/shard_map/all_to_all | solution.py:291
  35.0 1.0 copy.20
  36.0 6.8 %all-to-all-done.1 = s32[64,1,128]{2,1,0:T(1,128)S(1)} async-done(((s32[64,1,128]{2,1,0:T(1,128)}), s32[64,1,128]{2,1,0:T(1,128)S(1)}, u32[]{:S(2)}, u32[]{:S(2)}) %all-to-all-start.1) | async-done | bytes 32800 | tf_op jit(solution)/shard_map/all_to_all | solution.py:291
  42.8 0.1 reshape.49
  43.0 1.5 %gather_fusion = bf16[128,2,8,128]{3,2,1,0:T(8,128)(2,1)} fusion(bf16[52,2,8,128]{3,2,1,0:T(8,128)(2,1)S(1)} %bitcast.30, s32[1024]{0:T(1024)S(1)} %pad_clamp_fusion.1), kind=kCustom, calls=%fused_computation | custom fusion | bytes 1049088 | tf_op jit(solution)/shard_map/jit(_take)/gather | solution.py:308
  44.4 6.3 %all-to-all-start.2 = ((bf16[64,2,2,8,128]{4,3,2,1,0:T(8,128)(2,1)}), bf16[64,2,2,8,128]{4,3,2,1,0:T(8,128)(2,1)S(1)}, u32[]{:S(2)}, u32[]{:S(2)}) async-start(bf16[64,2,2,8,128]{4,3,2,1,0:T(8,128)(2,1)} %bitcast.5), calls=%async_computation.2 | async-start | bytes 1048576 | tf_op jit(solution)/shard_map/all_to_all | solution.py:309
  50.7 0.2 slice_reduce_fusion
  50.9 0.0 collective-permute-done.refs_4_
  50.9 0.0 copy-start.12
  51.0 4.5 %collective-permute-start.2 = (bf16[1536,128]{1,0:T(8,128)(2,1)S(1)}, bf16[1536,128]{1,0:T(8,128)(2,1)}, u32[]{:S(2)}, u32[]{:S(2)}) collective-permute-start(bf16[1536,128]{1,0:T(8,128)(2,1)S(1)} %slice.21), channel_id=1, source_target_pairs={{1,0},{2,1},{3,2},{4,3},{5,4},{6,5},{7,6},{0,7},{9,8},{10,9},{11,1... | collective-permute-start | bytes 1179656 | tf_op jit(solution)/shard_map/ppermute | solution.py:24
  55.5 0.0 collective-permute-done.1.refs_5_
  55.5 1.0 slice.22
  56.5 1.9 %collective-permute-start.3 = (bf16[1536,128]{1,0:T(8,128)(2,1)S(1)}, bf16[1536,128]{1,0:T(8,128)(2,1)S(1)}, u32[]{:S(2)}, u32[]{:S(2)}) collective-permute-start(bf16[1536,128]{1,0:T(8,128)(2,1)S(1)} %slice.22), channel_id=1, source_target_pairs={{7,0},{0,1},{1,2},{2,3},{3,4},{4,5},{5,6},{6,7},{15,8},{8,9},{9,10... | collective-permute-start | bytes 1179656 | tf_op jit(solution)/shard_map/ppermute | solution.py:24
  58.4 0.1 iota_compare_fusion
  58.5 0.2 lt.28
  58.7 0.7 iota_reduce_fusion
  59.4 4.8 %collective-permute-done.2.refs_6_ = bf16[1536,128]{1,0:T(8,128)(2,1)} collective-permute-done((bf16[1536,128]{1,0:T(8,128)(2,1)S(1)}, bf16[1536,128]{1,0:T(8,128)(2,1)}, u32[]{:S(2)}, u32[]{:S(2)}) %collective-permute-start.2) | collective-permute-done | bytes 393248 | tf_op jit(solution)/shard_map/ppermute | solution.py:24
  64.1 6.4 %collective-permute-done.3.refs_7_ = bf16[1536,128]{1,0:T(8,128)(2,1)S(1)} collective-permute-done((bf16[1536,128]{1,0:T(8,128)(2,1)S(1)}, bf16[1536,128]{1,0:T(8,128)(2,1)S(1)}, u32[]{:S(2)}, u32[]{:S(2)}) %collective-permute-start.3) | collective-permute-done | bytes 393248 | tf_op jit(solution)/shard_map/ppermute | solution.py:24
  70.5 0.0 all-to-all-done.2.refs_0_.refs_1_
  70.5 0.7 copy-done.14
  71.3 0.2 copy-done.6
  71.4 4.4 %rotate_rows.1 = bf16[64,2,2,8,128]{4,3,2,1,0:T(8,128)(2,1)} custom-call(bf16[64,2,2,8,128]{4,3,2,1,0:T(8,128)(2,1)} %copy-done.6, bf16[2,1024,128]{2,1,0:T(8,128)(2,1)} %bitcast.19, f32[2,512,128]{2,1,0:T(8,128)} %bitcast.23, f32[2,512,128]{2,1,0:T(8,128)} %bitcast.26, bf16[3584,128]{1,0:T(8,128)(2,1)} %copy-done.12, ...), custom_call_target="tpu_custom_call" | custom-call | flops 17179869184 | bytes 8388608 | tf_op jit(solution)/shard_map/rotate_rows/pallas_call | solution.py:314
  75.8 0.0 copy-start.7
  75.8 0.0 copy-start.5
  75.8 10.5 %all-to-all-start.3 = ((bf16[64,2,2,8,128]{4,3,2,1,0:T(8,128)(2,1)}), bf16[64,2,2,8,128]{4,3,2,1,0:T(8,128)(2,1)S(1)}, u32[]{:S(2)}, u32[]{:S(2)}) async-start(bf16[64,2,2,8,128]{4,3,2,1,0:T(8,128)(2,1)} %rotate_rows.1), calls=%async_computation.3 | async-start | bytes 1048576 | tf_op jit(solution)/shard_map/all_to_all | solution.py:332
  86.4 1.9 %collective-permute-start.4 = (bf16[64,2,2,8,128]{4,3,2,1,0:T(8,128)(2,1)S(1)}, bf16[64,2,2,8,128]{4,3,2,1,0:T(8,128)(2,1)S(1)}, u32[]{:S(2)}, u32[]{:S(2)}) collective-permute-start(bf16[64,2,2,8,128]{4,3,2,1,0:T(8,128)(2,1)S(1)} %copy-done.7), channel_id=1, source_target_pairs={{1,0},{2,1},{3,2},{4,3},{5,4},{6,5},{7,6},{0,7},{9,8},{10,9},{11,1... | collective-permute-start | bytes 1572872 | tf_op jit(solution)/shard_map/ppermute | solution.py:24
  88.3 3.9 %collective-permute-start.6 = (bf16[64,2,2,8,128]{4,3,2,1,0:T(8,128)(2,1)S(1)}, bf16[64,2,2,8,128]{4,3,2,1,0:T(8,128)(2,1)}, u32[]{:S(2)}, u32[]{:S(2)}) collective-permute-start(bf16[64,2,2,8,128]{4,3,2,1,0:T(8,128)(2,1)S(1)} %copy-done.7), channel_id=1, source_target_pairs={{7,0},{0,1},{1,2},{2,3},{3,4},{4,5},{5,6},{6,7},{15,8},{8,9},{9,10... | collective-permute-start | bytes 1572872 | tf_op jit(solution)/shard_map/ppermute | solution.py:24
  92.2 10.0 %collective-permute-done.4.refs_2_ = bf16[64,2,2,8,128]{4,3,2,1,0:T(8,128)(2,1)S(1)} collective-permute-done((bf16[64,2,2,8,128]{4,3,2,1,0:T(8,128)(2,1)S(1)}, bf16[64,2,2,8,128]{4,3,2,1,0:T(8,128)(2,1)S(1)}, u32[]{:S(2)}, u32[]{:S(2)}) %collective-permute-start.4) | collective-permute-done | bytes 524320 | tf_op jit(solution)/shard_map/ppermute | solution.py:24
  102.2 3.4 %collective-permute-start.5 = (bf16[64,2,2,8,128]{4,3,2,1,0:T(8,128)(2,1)S(1)}, bf16[64,2,2,8,128]{4,3,2,1,0:T(8,128)(2,1)S(1)}, u32[]{:S(2)}, u32[]{:S(2)}) collective-permute-start(bf16[64,2,2,8,128]{4,3,2,1,0:T(8,128)(2,1)S(1)} %collective-permute-done.4.refs_2_), channel_id=1, source_target_pairs={{1,0},{2,1},{3,2},{4,3},{5,4},{6,5},{7,6},{0,7},{9,8},{10,9},{11,1... | collective-permute-start | bytes 1572872 | tf_op jit(solution)/shard_map/ppermute | solution.py:24
  105.7 0.0 all-to-all-done.3
  105.7 0.0 copy-start.3
  105.7 0.6 gather_fusion.1
  106.3 0.0 copy-start.1
  106.3 0.8 copy.18
  107.2 4.5 %all-to-all-start.4 = ((bf16[8,52,2,128]{3,2,1,0:T(2,128)(2,1)}), bf16[8,52,2,128]{3,2,1,0:T(2,128)(2,1)S(1)}, u32[]{:S(2)}, u32[]{:S(2)}) async-start(bf16[8,52,2,128]{3,2,1,0:T(2,128)(2,1)} %bitcast.33), calls=%async_computation.4 | async-start | bytes 425984 | tf_op jit(solution)/shard_map/all_to_all | solution.py:336
  111.7 0.0 collective-permute-done.6.refs_3_
  111.7 0.0 copy-done.5
  111.7 0.0 copy-done.3
  111.7 0.0 copy-done.1
  111.7 0.0 copy-start.10
  111.7 1.2 copy-done.10
  113.0 3.2 %near_state.1 = (f32[2,1024,128]{2,1,0:T(8,128)S(1)}, f32[2,512,128]{2,1,0:T(8,128)S(1)}, f32[2,512,128]{2,1,0:T(8,128)S(1)}) custom-call(s32[1]{0:T(128)S(6)} %copy.22.count_ref.refs_0_, bf16[64,2,2,8,128]{4,3,2,1,0:T(8,128)(2,1)S(1)} %copy-done.7, bf16[64,2,2,8,128]{4,3,2,1,0:T(8,128)(2,1)S(1)} %collective-permute-done.4.refs_2_, ...), custom_call_target="tpu_custom_call" | custom-call | flops 4294967296 | bytes 16777216 | tf_op jit(solution)/shard_map/near_state/pallas_call | solution.py:351
  116.1 4.7 %collective-permute-done.5.refs_1_ = bf16[64,2,2,8,128]{4,3,2,1,0:T(8,128)(2,1)S(1)} collective-permute-done((bf16[64,2,2,8,128]{4,3,2,1,0:T(8,128)(2,1)S(1)}, bf16[64,2,2,8,128]{4,3,2,1,0:T(8,128)(2,1)S(1)}, u32[]{:S(2)}, u32[]{:S(2)}) %collective-permute-start.5) | collective-permute-done | bytes 524320 | tf_op jit(solution)/shard_map/ppermute | solution.py:24
  120.8 1.9 %far_state.1 = (f32[2,1024,128]{2,1,0:T(8,128)}, f32[2,512,128]{2,1,0:T(8,128)}, f32[2,512,128]{2,1,0:T(8,128)}) custom-call(s32[1]{0:T(128)S(6)} %copy.22.count_ref.refs_0_, bf16[64,2,2,8,128]{4,3,2,1,0:T(8,128)(2,1)S(1)} %collective-permute-done.5.refs_1_, bf16[2,1024,128]{2,1,0:T(8,128)(2,1)S(1)} %bitcast.22, ...), custom_call_target="tpu_custom_call" | custom-call | tf_op jit(solution)/shard_map/far_state/pallas_call | solution.py:365
  122.7 0.0 all-to-all-done.4.partial_ref
  122.7 0.8 add.2
  (13 shorter events, 0.1 us)
Async XLA Ops:
  0.6 9.0 %copy-start.2 = (f32[1,2,512,128]{3,2,1,0:T(8,128)S(1)}, f32[1,2,512,128]{3,2,1,0:T(8,128)}, u32[]{:S(2)}) copy-start(f32[1,2,512,128]{3,2,1,0:T(8,128)} %param.12) | copy-start | bytes 1572868
  1.7 8.0 %copy-start = (bf16[1,2,1024,128]{3,2,1,0:T(8,128)(2,1)S(1)}, bf16[1,2,1024,128]{3,2,1,0:T(8,128)(2,1)}, u32[]{:S(2)}) copy-start(bf16[1,2,1024,128]{3,2,1,0:T(8,128)(2,1)} %param.11) | copy-start | bytes 1572868
  2.6 17.9 %all-to-all-start = ((bf16[8,52,2,128]{3,2,1,0:T(2,128)(2,1)}), bf16[8,52,2,128]{3,2,1,0:T(2,128)(2,1)S(1)}, u32[]{:S(2)}, u32[]{:S(2)}) async-start(bf16[8,52,2,128]{3,2,1,0:T(2,128)(2,1)} %bitcast.1.refs_0_), calls=%async_computation | async-start | bytes 425984 | tf_op jit(solution)/shard_map/all_to_all | solution.py:272
  9.7 1.0 copy-start.4
  10.9 40.0 %collective-permute-start = (bf16[3584,128]{1,0:T(8,128)(2,1)S(1)}, bf16[3584,128]{1,0:T(8,128)(2,1)S(1)}, u32[]{:S(2)}, u32[]{:S(2)}) collective-permute-start(bf16[3584,128]{1,0:T(8,128)(2,1)S(1)} %get-tuple-element.13), channel_id=1, source_target_pairs={{1,0},{2,1},{3,2},{4,3},{5,4},{6,5},{7,6},{0,7},{9,8},{10,9},{11,1... | collective-permute-start | bytes 2752520 | tf_op jit(solution)/shard_map/ppermute | solution.py:24
  16.1 2.6 %copy-start.9 = (s32[1,2]{1,0:T(1,128)S(1)}, s32[1,2]{1,0:T(1,128)}, u32[]{:S(2)}) copy-start(s32[1,2]{1,0:T(1,128)} %list_ref.1) | copy-start | bytes 28
  16.1 39.4 %collective-permute-start.1 = (bf16[3584,128]{1,0:T(8,128)(2,1)S(1)}, bf16[3584,128]{1,0:T(8,128)(2,1)}, u32[]{:S(2)}, u32[]{:S(2)}) collective-permute-start(bf16[3584,128]{1,0:T(8,128)(2,1)S(1)} %get-tuple-element.14), channel_id=1, source_target_pairs={{7,0},{0,1},{1,2},{2,3},{3,4},{4,5},{5,6},{6,7},{15,8},{8,9},{9,10... | collective-permute-start | bytes 2752520 | tf_op jit(solution)/shard_map/ppermute | solution.py:24
  19.3 0.6 copy-start.8
  20.5 0.7 copy-start.11
  21.2 21.6 %all-to-all-start.1 = ((s32[64,1,128]{2,1,0:T(1,128)}), s32[64,1,128]{2,1,0:T(1,128)S(1)}, u32[]{:S(2)}, u32[]{:S(2)}) async-start(s32[64,1,128]{2,1,0:T(1,128)} %after.1), calls=%async_computation.1 | async-start | bytes 65536 | tf_op jit(solution)/shard_map/all_to_all | solution.py:291
  44.4 26.1 %all-to-all-start.2 = ((bf16[64,2,2,8,128]{4,3,2,1,0:T(8,128)(2,1)}), bf16[64,2,2,8,128]{4,3,2,1,0:T(8,128)(2,1)S(1)}, u32[]{:S(2)}, u32[]{:S(2)}) async-start(bf16[64,2,2,8,128]{4,3,2,1,0:T(8,128)(2,1)} %bitcast.5), calls=%async_computation.2 | async-start | bytes 1048576 | tf_op jit(solution)/shard_map/all_to_all | solution.py:309
  50.9 19.6 %copy-start.12 = (bf16[3584,128]{1,0:T(8,128)(2,1)}, bf16[3584,128]{1,0:T(8,128)(2,1)S(1)}, u32[]{:S(2)}) copy-start(bf16[3584,128]{1,0:T(8,128)(2,1)S(1)} %collective-permute-done.refs_4_) | copy-start | bytes 2752516
  51.0 13.2 %collective-permute-start.2 = (bf16[1536,128]{1,0:T(8,128)(2,1)S(1)}, bf16[1536,128]{1,0:T(8,128)(2,1)}, u32[]{:S(2)}, u32[]{:S(2)}) collective-permute-start(bf16[1536,128]{1,0:T(8,128)(2,1)S(1)} %slice.21), channel_id=1, source_target_pairs={{1,0},{2,1},{3,2},{4,3},{5,4},{6,5},{7,6},{0,7},{9,8},{10,9},{11,1... | collective-permute-start | bytes 1179656 | tf_op jit(solution)/shard_map/ppermute | solution.py:24
  56.5 14.0 %collective-permute-start.3 = (bf16[1536,128]{1,0:T(8,128)(2,1)S(1)}, bf16[1536,128]{1,0:T(8,128)(2,1)S(1)}, u32[]{:S(2)}, u32[]{:S(2)}) collective-permute-start(bf16[1536,128]{1,0:T(8,128)(2,1)S(1)} %slice.22), channel_id=1, source_target_pairs={{7,0},{0,1},{1,2},{2,3},{3,4},{4,5},{5,6},{6,7},{15,8},{8,9},{9,10... | collective-permute-start | bytes 1179656 | tf_op jit(solution)/shard_map/ppermute | solution.py:24
  70.5 0.7 copy-start.14
  70.5 0.9 copy-start.6
  71.4 34.2 %copy-start.13 = (s32[52]{0:T(128)S(1)}, s32[52]{0:T(128)}, u32[]{:S(2)}) copy-start(s32[52]{0:T(128)} %get-tuple-element.15.refs_8_) | copy-start | bytes 628
  75.8 10.5 %copy-start.7 = (bf16[64,2,2,8,128]{4,3,2,1,0:T(8,128)(2,1)S(1)}, bf16[64,2,2,8,128]{4,3,2,1,0:T(8,128)(2,1)}, u32[]{:S(2)}) copy-start(bf16[64,2,2,8,128]{4,3,2,1,0:T(8,128)(2,1)} %copy-done.6) | copy-start | bytes 1572868
  75.8 35.9 %copy-start.5 = (f32[1,2,512,128]{3,2,1,0:T(8,128)S(1)}, f32[1,2,512,128]{3,2,1,0:T(8,128)}, u32[]{:S(2)}) copy-start(f32[1,2,512,128]{3,2,1,0:T(8,128)} %param.13) | copy-start | bytes 1572868
  75.8 29.8 %all-to-all-start.3 = ((bf16[64,2,2,8,128]{4,3,2,1,0:T(8,128)(2,1)}), bf16[64,2,2,8,128]{4,3,2,1,0:T(8,128)(2,1)S(1)}, u32[]{:S(2)}, u32[]{:S(2)}) async-start(bf16[64,2,2,8,128]{4,3,2,1,0:T(8,128)(2,1)} %rotate_rows.1), calls=%async_computation.3 | async-start | bytes 1048576 | tf_op jit(solution)/shard_map/all_to_all | solution.py:332
  86.4 15.9 %collective-permute-start.4 = (bf16[64,2,2,8,128]{4,3,2,1,0:T(8,128)(2,1)S(1)}, bf16[64,2,2,8,128]{4,3,2,1,0:T(8,128)(2,1)S(1)}, u32[]{:S(2)}, u32[]{:S(2)}) collective-permute-start(bf16[64,2,2,8,128]{4,3,2,1,0:T(8,128)(2,1)S(1)} %copy-done.7), channel_id=1, source_target_pairs={{1,0},{2,1},{3,2},{4,3},{5,4},{6,5},{7,6},{0,7},{9,8},{10,9},{11,1... | collective-permute-start | bytes 1572872 | tf_op jit(solution)/shard_map/ppermute | solution.py:24
  88.3 23.4 %collective-permute-start.6 = (bf16[64,2,2,8,128]{4,3,2,1,0:T(8,128)(2,1)S(1)}, bf16[64,2,2,8,128]{4,3,2,1,0:T(8,128)(2,1)}, u32[]{:S(2)}, u32[]{:S(2)}) collective-permute-start(bf16[64,2,2,8,128]{4,3,2,1,0:T(8,128)(2,1)S(1)} %copy-done.7), channel_id=1, source_target_pairs={{7,0},{0,1},{1,2},{2,3},{3,4},{4,5},{5,6},{6,7},{15,8},{8,9},{9,10... | collective-permute-start | bytes 1572872 | tf_op jit(solution)/shard_map/ppermute | solution.py:24
  102.2 18.6 %collective-permute-start.5 = (bf16[64,2,2,8,128]{4,3,2,1,0:T(8,128)(2,1)S(1)}, bf16[64,2,2,8,128]{4,3,2,1,0:T(8,128)(2,1)S(1)}, u32[]{:S(2)}, u32[]{:S(2)}) collective-permute-start(bf16[64,2,2,8,128]{4,3,2,1,0:T(8,128)(2,1)S(1)} %collective-permute-done.4.refs_2_), channel_id=1, source_target_pairs={{1,0},{2,1},{3,2},{4,3},{5,4},{6,5},{7,6},{0,7},{9,8},{10,9},{11,1... | collective-permute-start | bytes 1572872 | tf_op jit(solution)/shard_map/ppermute | solution.py:24
  105.7 6.0 %copy-start.3 = (f32[1,2,512,128]{3,2,1,0:T(8,128)S(1)}, f32[1,2,512,128]{3,2,1,0:T(8,128)}, u32[]{:S(2)}) copy-start(f32[1,2,512,128]{3,2,1,0:T(8,128)} %param.12) | copy-start | bytes 1572868
  106.3 5.4 %copy-start.1 = (bf16[1,2,1024,128]{3,2,1,0:T(8,128)(2,1)S(1)}, bf16[1,2,1024,128]{3,2,1,0:T(8,128)(2,1)}, u32[]{:S(2)}) copy-start(bf16[1,2,1024,128]{3,2,1,0:T(8,128)(2,1)} %param.11) | copy-start | bytes 1572868
  107.2 15.6 %all-to-all-start.4 = ((bf16[8,52,2,128]{3,2,1,0:T(2,128)(2,1)}), bf16[8,52,2,128]{3,2,1,0:T(2,128)(2,1)S(1)}, u32[]{:S(2)}, u32[]{:S(2)}) async-start(bf16[8,52,2,128]{3,2,1,0:T(2,128)(2,1)} %bitcast.33), calls=%async_computation.4 | async-start | bytes 425984 | tf_op jit(solution)/shard_map/all_to_all | solution.py:336
  111.7 1.2 copy-start.10

commit v7 on v6

--- a/solution.py
+++ b/solution.py
@@ -17,7 +17,7 @@
 
 GROUPS = 4
 ROWS_VMEM = 58 * 2**20
-ROWS_FLOPS = 2**34
+ROWS_FLOPS = 2**16
 
 
 def shifted(x, parts, by):
@@ -71,10 +71,34 @@
     ).astype(jnp.bfloat16)
 
 
-def rows_kernel(
-    share, arrived_hbm, basis_hbm, first_hbm, second_hbm, right_hbm, left_hbm, far_right_hbm,
-    far_left_hbm, place_hbm, back_ref, rotated_ref, direction_ref, spread_ref, arrived_ref, basis_ref,
-    first_ref, second_ref, right_ref, left_ref, far_ref, sems,
+def toward(turned, first, second):
+    moment_one = beta_one * first + (1.0 - beta_one) * turned
+    moment_two = beta_two * second + (1.0 - beta_two) * turned * turned
+    return moment_one / bias_one / (jnp.sqrt(moment_two / bias_two) + epsilon)
+
+
+def sent_moments(ref, at, r, share, owners):
+    return (
+        ref[pl.ds(at + (2 * m * share + r) * owners, owners), :].astype(jnp.float32)
+        + ref[pl.ds(at + ((2 * m + 1) * share + r) * owners, owners), :].astype(jnp.float32)
+        for m in range(2)
+    )
+
+
+def started(ends, sems):
+    copies = [
+        [pltpu.make_async_copy(*pair, sems.at[s, i]) for i, pair in enumerate(ends(s))]
+        for s in range(sems.shape[0])
+    ]
+    for copy in sum(copies, []):
+        copy.start()
+    return copies
+
+
+def near_rows_kernel(
+    share, arrived_hbm, basis_hbm, first_hbm, second_hbm, right_hbm, left_hbm, place_hbm,
+    grad_ref, total_ref, rotated_ref, direction_ref, spread_ref, arrived_ref, basis_ref,
+    first_ref, second_ref, right_ref, left_ref, sems,
 ):
     owners, slots, _, pieces, part = arrived_ref.shape
     rows = owners * share
@@ -90,31 +114,22 @@
         for hbm, ref, at in ((right_hbm, right_ref, (0, stay)[s]), (left_hbm, left_ref, (stay, 0)[s])):
             for first, size in ((at, width), (near, piece)):
                 yield hbm.at[pl.ds(first, size)], ref.at[pl.ds(first, size)]
-        yield (far_right_hbm, far_left_hbm)[s], far_ref.at[s]
         yield first_hbm.at[s], first_ref.at[s]
         yield second_hbm.at[s], second_ref.at[s]
 
-    copies = [
-        [pltpu.make_async_copy(*ends, sems.at[s, i]) for i, ends in enumerate(needed(s))]
-        for s in range(slots)
-    ]
-    for copy in copies[0] + copies[1]:
-        copy.start()
+    copies = started(needed, sems)
     for s in range(slots):
         for copy in copies[s]:
             copy.wait()
-        near = 2 * width + (1 + s) * piece
-        sources = (
-            (right_ref, (0, width + piece)[s], near),
-            (left_ref, (width + piece, 0)[s], near),
-            (far_ref.at[s], 0, width),
-        )
+        near = stay + width + s * piece
+        sources = ((right_ref, (0, stay)[s]), (left_ref, (stay, 0)[s]))
         basis = jnp.concatenate(
-            [basis_ref[s]] + [ref[pl.ds(at, width), :] for ref, at, _ in sources], axis=1
+            [basis_ref[s]] + [ref[pl.ds(at, width), :] for ref, at in sources], axis=1
         )
         grad = spread_rows(arrived_ref[:, s].reshape(rows, pieces, part), spread_ref)
+        grad_ref[s] = grad
         rotated = jnp.dot(grad, basis, preferred_element_type=jnp.float32)
-        for i in range(GROUPS):
+        for i in range(GROUPS - 1):
             rotated_ref[s, i] = rotated[:, i * part : (i + 1) * part]
             for r in range(share):
                 local = pl.ds(r, owners, stride=share)
@@ -122,23 +137,42 @@
                     here = pl.ds(base + r, owners, stride=GROUPS * share)
                     first, second = first_ref[s, here, :], second_ref[s, here, :]
                 else:
-                    ref, _, at = sources[i - 1]
-                    first, second = (
-                        ref[pl.ds(at + (2 * m * share + r) * owners, owners), :].astype(jnp.float32)
-                        + ref[
-                            pl.ds(at + ((2 * m + 1) * share + r) * owners, owners), :
-                        ].astype(jnp.float32)
-                        for m in range(2)
-                    )
-                turned = rotated_ref[s, i, local, :]
-                moment_one = beta_one * first + (1.0 - beta_one) * turned
-                moment_two = beta_two * second + (1.0 - beta_two) * turned * turned
-                direction_ref[s, i, local, :] = (
-                    moment_one / bias_one / (jnp.sqrt(moment_two / bias_two) + epsilon)
-                )
-        direction = jnp.concatenate([direction_ref[s, i] for i in range(GROUPS)], axis=1)
-        back = lax.dot_general(
+                    first, second = sent_moments(sources[i - 1][0], near, r, share, owners)
+                direction_ref[s, i, local, :] = toward(rotated_ref[s, i, local, :], first, second)
+        direction = jnp.concatenate([direction_ref[s, i] for i in range(GROUPS - 1)], axis=1)
+        total_ref[s] = lax.dot_general(
             direction.astype(jnp.bfloat16),
+            basis,
+            (((1,), (1,)), ((), ())),
+            preferred_element_type=jnp.float32,
+        )
+
+
+def far_rows_kernel(
+    share, grad_hbm, total_hbm, far_right_hbm, far_left_hbm, back_ref,
+    rotated_ref, direction_ref, spread_ref, grad_ref, total_ref, far_ref, sems,
+):
+    owners, slots, _, pieces, part = back_ref.shape
+    rows = owners * share
+    width = pieces * part
+
+    def needed(s):
+        yield grad_hbm.at[s], grad_ref.at[s]
+        yield (far_right_hbm, far_left_hbm)[s], far_ref.at[s]
+        yield total_hbm.at[s], total_ref.at[s]
+
+    copies = started(needed, sems)
+    for s in range(slots):
+        for copy in copies[s]:
+            copy.wait()
+        basis = far_ref[s, pl.ds(0, width), :]
+        rotated_ref[s] = jnp.dot(grad_ref[s], basis, preferred_element_type=jnp.float32)
+        for r in range(share):
+            local = pl.ds(r, owners, stride=share)
+            first, second = sent_moments(far_ref.at[s], width, r, share, owners)
+            direction_ref[s, local, :] = toward(rotated_ref[s, local, :], first, second)
+        back = total_ref[s] + lax.dot_general(
+            direction_ref[s].astype(jnp.bfloat16),
             basis,
             (((1,), (1,)), ((), ())),
             preferred_element_type=jnp.float32,
@@ -310,24 +344,47 @@
     holds = (lists.reshape(-1)[None, :] == jnp.arange(blocks)[:, None]) & live.reshape(-1)[None, :]
     place = jnp.argmax(holds, axis=1)
     rows = owners * share
-    operands = (arrived, basis[0], first_moment[0], second_moment[0], right, left, *far)
+    operands = (arrived, basis[0], first_moment[0], second_moment[0], right, left)
+    anywhere = pl.BlockSpec(memory_space=pl.ANY)
+    rows_params = pltpu.CompilerParams(vmem_limit_bytes=ROWS_VMEM)
+    spread_rows_vmem = pltpu.VMEM((rows * (width // part), part), jnp.float32)
+    grad_rows, total = pl.pallas_call(
+        own(near_rows_kernel),
+        out_shape=(
+            jax.ShapeDtypeStruct((slot_count, rows, width), jnp.bfloat16),
+            jax.ShapeDtypeStruct((slot_count, rows, width), jnp.float32),
+        ),
+        in_specs=[anywhere] * (len(operands) + 1),
+        out_specs=(vmem,) * 2,
+        scratch_shapes=[
+            pltpu.VMEM((slot_count, GROUPS - 1, rows, part), jnp.float32),
+            pltpu.VMEM((slot_count, GROUPS - 1, rows, part), jnp.float32),
+            spread_rows_vmem,
+            *(pltpu.VMEM(x.shape, x.dtype) for x in operands),
+            pltpu.SemaphoreType.DMA((slot_count, 8)),
+        ],
+        compiler_params=rows_params,
+        cost_estimate=pl.CostEstimate(flops=ROWS_FLOPS, bytes_accessed=2**10, transcendentals=0),
+        name="near_rows",
+    )(*operands, place)
+    far_right, far_left = far
     back = pl.pallas_call(
-        own(rows_kernel),
+        own(far_rows_kernel),
         out_shape=jax.ShapeDtypeStruct(arrived.shape, jnp.bfloat16),
-        in_specs=[pl.BlockSpec(memory_space=pl.ANY)] * (len(operands) + 1),
+        in_specs=[anywhere] * 4,
         out_specs=vmem,
         scratch_shapes=[
-            pltpu.VMEM((slot_count, GROUPS, rows, part), jnp.float32),
-            pltpu.VMEM((slot_count, GROUPS, rows, part), jnp.float32),
-            pltpu.VMEM((rows * (width // part), part), jnp.float32),
-            *(pltpu.VMEM(x.shape, x.dtype) for x in operands[:6]),
-            pltpu.VMEM((slot_count, width + piece, part), jnp.bfloat16),
-            pltpu.SemaphoreType.DMA((slot_count, len(operands) + 1)),
+            pltpu.VMEM((slot_count, rows, part), jnp.float32),
+            pltpu.VMEM((slot_count, rows, part), jnp.float32),
+            spread_rows_vmem,
+            pltpu.VMEM(grad_rows.shape, grad_rows.dtype),
+            pltpu.VMEM(total.shape, total.dtype),
+            pltpu.VMEM((slot_count, *far_right.shape), far_right.dtype),
+            pltpu.SemaphoreType.DMA((slot_count, 3)),
         ],
-        compiler_params=pltpu.CompilerParams(vmem_limit_bytes=ROWS_VMEM),
-        cost_estimate=pl.CostEstimate(flops=ROWS_FLOPS, bytes_accessed=2**23, transcendentals=0),
-        name="rotate_rows",
-    )(*operands, place)
+        compiler_params=rows_params,
+        name="far_rows",
+    )(grad_rows, total, far_right, far_left)
 
     returned = lax.all_to_all(back, "dp", 0, 0, tiled=True)
     placed = jnp.take(

time: 126 us -> 125 us (level)
  waiting for transfers between devices: 33.3 us -> 30.2 us
  Pallas kernels: 11 us -> 13.7 us
  starting transfers between devices: 65 us -> 63.1 us
  local copies, waits for them, and re-layouts: 11.8 us -> 13.6 us
    ppermute x7, waiting for transfers between devices: 25.8 us -> 14.7 us  [shifted(): lax.ppermute(x, 'tensor', [((i + by) % parts, i) for i in range(parts)])]
    all_to_all x1, waiting for transfers between devices: 0.01 us -> 8.01 us  [on_device(): arrived = lax.all_to_all(outgoing, 'dp', 0, 0, tiled=True)]
    pallas_call x1 -> x2, Pallas kernels: 4.36 us -> 7.11 us  [the longest x1 4.05 us: on_device(): pl.pallas_call(own(near_rows_kernel), out_shape=(jax.ShapeDtypeStruct((sl...]
    all_to_all x1, starting transfers between devices: 10.5 us -> 8.65 us  [on_device(): returned = lax.all_to_all(back, 'dp', 0, 0, tiled=True)]
  transfers between devices with their start and end apart: 12 -> 12, of which waited for: 6 -> 5; matrix products, arithmetic and copies ran while one was open for 5% -> 6% of each run, Pallas kernels for 5% -> 8%
where the time goes in v7:
time: 125 us; the launch traced here: 123 us
  starting transfers between devices  63.1 us (50%)
  waiting for transfers between devices  30.2 us (24%)
  Pallas kernels  13.7 us (11%)
  local copies, waits for them, and re-layouts  13.6 us (11%)
  between operations  1.66 us (1%)
    ppermute x7, starting transfers between devices, shifted(): lax.ppermute(x, 'tensor', [((i + by) % parts, i) for i in range(parts)])  22.7 us
    ppermute x7, waiting for transfers between devices, shifted(): lax.ppermute(x, 'tensor', [((i + by) % parts, i) for i in range(parts)])  14.7 us
    all_to_all x1, starting transfers between devices, on_device(): table = lax.all_to_all(mine, 'dp', 0, 0, tiled=True).reshape(owners, part)  13.8 us
    all_to_all x1, starting transfers between devices, on_device(): returned = lax.all_to_all(back, 'dp', 0, 0, tiled=True)  8.65 us
    all_to_all x1, waiting for transfers between devices, on_device(): arrived = lax.all_to_all(outgoing, 'dp', 0, 0, tiled=True)  8.01 us
    all_to_all x1, starting transfers between devices, on_device(): moved = lax.all_to_all(leaving, 'tensor', 0, 0, tiled=True)  7.1 us
    all_to_all x1, waiting for transfers between devices, on_device(): table = lax.all_to_all(mine, 'dp', 0, 0, tiled=True).reshape(owners, part)  6.84 us
    all_to_all x1, starting transfers between devices, on_device(): arrived = lax.all_to_all(outgoing, 'dp', 0, 0, tiled=True)  6.28 us
  transfers between devices with their start and end apart: 12, of which 5 were waited for; matrix products, arithmetic and copies ran while one was open for 6% of the time, Pallas kernels for 8%

profile of v7, /device:TPU:6, one launch (start us, length us, event | category | flops | bytes accessed | tf_op | source)
XLA Modules:
  0.0 123.0 jit_solution(1361833879970179271)
XLA Ops:
  0.6 0.0 copy-start.2
  0.6 1.0 reshape.42
  1.7 0.0 copy-start
  1.7 0.1 copy.16
  1.8 0.8 tile.4
  2.6 7.1 %all-to-all-start = ((bf16[8,52,2,128]{3,2,1,0:T(2,128)(2,1)}), bf16[8,52,2,128]{3,2,1,0:T(2,128)(2,1)S(1)}, u32[]{:S(2)}, u32[]{:S(2)}) async-start(bf16[8,52,2,128]{3,2,1,0:T(2,128)(2,1)} %bitcast.1.refs_0_), calls=%async_computation | async-start | bytes 425984 | tf_op jit(solution)/shard_map/all_to_all | solution.py:306
  9.7 0.0 copy-done.2
  9.7 0.0 copy-start.4
  9.7 1.0 copy-done.4
  10.7 0.2 pack.1
  10.9 5.1 %collective-permute-start = (bf16[3584,128]{1,0:T(8,128)(2,1)S(1)}, bf16[3584,128]{1,0:T(8,128)(2,1)}, u32[]{:S(2)}, u32[]{:S(2)}) collective-permute-start(bf16[3584,128]{1,0:T(8,128)(2,1)S(1)} %get-tuple-element.15), channel_id=1, source_target_pairs={{1,0},{2,1},{3,2},{4,3},{5,4},{6,5},{7,6},{0,7},{9,8},{10,9},{11,1... | collective-permute-start | bytes 2752520 | tf_op jit(solution)/shard_map/ppermute | solution.py:24
  16.1 0.0 copy-start.9
  16.1 1.9 %collective-permute-start.1 = (bf16[3584,128]{1,0:T(8,128)(2,1)S(1)}, bf16[3584,128]{1,0:T(8,128)(2,1)}, u32[]{:S(2)}, u32[]{:S(2)}) collective-permute-start(bf16[3584,128]{1,0:T(8,128)(2,1)S(1)} %get-tuple-element.16), channel_id=1, source_target_pairs={{7,0},{0,1},{1,2},{2,3},{3,4},{4,5},{5,6},{6,7},{15,8},{8,9},{9,10... | collective-permute-start | bytes 2752520 | tf_op jit(solution)/shard_map/ppermute | solution.py:24
  18.7 0.6 list.1.sent_ref
  19.3 0.0 copy-start.8
  19.3 0.6 copy-done.8
  19.9 0.6 all-to-all-done.after_ref
  20.5 0.7 copy-done.11
  21.2 13.8 %all-to-all-start.1 = ((s32[64,1,128]{2,1,0:T(1,128)}), s32[64,1,128]{2,1,0:T(1,128)S(1)}, u32[]{:S(2)}, u32[]{:S(2)}) async-start(s32[64,1,128]{2,1,0:T(1,128)} %after.1), calls=%async_computation.1 | async-start | bytes 65536 | tf_op jit(solution)/shard_map/all_to_all | solution.py:325
  35.0 1.0 copy.20
  36.0 6.8 %all-to-all-done.1 = s32[64,1,128]{2,1,0:T(1,128)S(1)} async-done(((s32[64,1,128]{2,1,0:T(1,128)}), s32[64,1,128]{2,1,0:T(1,128)S(1)}, u32[]{:S(2)}, u32[]{:S(2)}) %all-to-all-start.1) | async-done | bytes 32800 | tf_op jit(solution)/shard_map/all_to_all | solution.py:325
  42.8 0.1 reshape.49
  43.0 1.5 %gather_fusion = bf16[128,2,8,128]{3,2,1,0:T(8,128)(2,1)} fusion(bf16[52,2,8,128]{3,2,1,0:T(8,128)(2,1)S(1)} %bitcast.30, s32[1024]{0:T(1024)S(1)} %pad_clamp_fusion.1), kind=kCustom, calls=%fused_computation | custom fusion | bytes 1049088 | tf_op jit(solution)/shard_map/jit(_take)/gather | solution.py:342
  44.4 6.3 %all-to-all-start.2 = ((bf16[64,2,2,8,128]{4,3,2,1,0:T(8,128)(2,1)}), bf16[64,2,2,8,128]{4,3,2,1,0:T(8,128)(2,1)S(1)}, u32[]{:S(2)}, u32[]{:S(2)}) async-start(bf16[64,2,2,8,128]{4,3,2,1,0:T(8,128)(2,1)} %bitcast.5), calls=%async_computation.2 | async-start | bytes 1048576 | tf_op jit(solution)/shard_map/all_to_all | solution.py:343
  50.7 0.2 slice_reduce_fusion
  50.9 0.0 collective-permute-done.refs_4_
  50.9 1.0 slice.22
  51.9 4.5 %collective-permute-start.2 = (bf16[1536,128]{1,0:T(8,128)(2,1)S(1)}, bf16[1536,128]{1,0:T(8,128)(2,1)S(1)}, u32[]{:S(2)}, u32[]{:S(2)}) collective-permute-start(bf16[1536,128]{1,0:T(8,128)(2,1)S(1)} %slice.22), channel_id=1, source_target_pairs={{1,0},{2,1},{3,2},{4,3},{5,4},{6,5},{7,6},{0,7},{9,8},{10,9},{11,1... | collective-permute-start | bytes 1179656 | tf_op jit(solution)/shard_map/ppermute | solution.py:24
  56.5 0.0 collective-permute-done.1.refs_5_
  56.5 1.0 slice.23
  57.5 1.9 %collective-permute-start.3 = (bf16[1536,128]{1,0:T(8,128)(2,1)S(1)}, bf16[1536,128]{1,0:T(8,128)(2,1)S(1)}, u32[]{:S(2)}, u32[]{:S(2)}) collective-permute-start(bf16[1536,128]{1,0:T(8,128)(2,1)S(1)} %slice.23), channel_id=1, source_target_pairs={{7,0},{0,1},{1,2},{2,3},{3,4},{4,5},{5,6},{6,7},{15,8},{8,9},{9,10... | collective-permute-start | bytes 1179656 | tf_op jit(solution)/shard_map/ppermute | solution.py:24
  59.4 0.1 iota_compare_fusion
  59.5 0.2 lt.28
  59.7 0.7 iota_reduce_fusion
  60.4 8.0 %all-to-all-done.2.refs_0_.refs_1_ = bf16[64,2,2,8,128]{4,3,2,1,0:T(8,128)(2,1)S(1)} async-done(((bf16[64,2,2,8,128]{4,3,2,1,0:T(8,128)(2,1)}), bf16[64,2,2,8,128]{4,3,2,1,0:T(8,128)(2,1)S(1)}, u32[]{:S(2)}, u32[]{:S(2)}) %all-to-all-start.2) | async-done | bytes 524320 | tf_op jit(solution)/shard_map/all_to_all | solution.py:343
  68.4 0.8 copy-done.6
  69.2 4.0 %near_rows.1 = (bf16[2,128,1024]{2,1,0:T(8,128)(2,1)}, f32[2,128,1024]{2,1,0:T(8,128)}) custom-call(bf16[64,2,2,8,128]{4,3,2,1,0:T(8,128)(2,1)} %copy-done.6, bf16[2,1024,128]{2,1,0:T(8,128)(2,1)} %bitcast.19, f32[2,512,128]{2,1,0:T(8,128)} %bitcast.23, f32[2,512,128]{2,1,0:T(8,128)} %bitcast.26, bf16[3584,128]{1,0:T(8,128)(2,1)} %collective-permute-done.refs_4_, ...), custom_call_target="tpu_custom_call" | custom-call | flops 65536 | bytes 1024 | tf_op jit(solution)/shard_map/near_rows/pallas_call | solution.py:351
  73.2 0.0 collective-permute-done.2.refs_2_
  73.2 0.0 collective-permute-done.3.refs_3_
  73.3 0.7 copy-done.12
  74.0 0.1 copy-done.13
  74.1 3.1 %far_rows.1 = bf16[64,2,2,8,128]{4,3,2,1,0:T(8,128)(2,1)} custom-call(bf16[2,128,1024]{2,1,0:T(8,128)(2,1)} %get-tuple-element.18.refs_0_, f32[2,128,1024]{2,1,0:T(8,128)} %get-tuple-element.19.refs_1_, bf16[1536,128]{1,0:T(8,128)(2,1)} %copy-done.12, bf16[1536,128]{1,0:T(8,128)(2,1)} %copy-done.13), custom_call_target="tpu_custom_call" | custom-call | tf_op jit(solution)/shard_map/far_rows/pallas_call | solution.py:371
  77.2 0.0 copy-start.7
  77.2 0.0 copy-start.5
  77.2 8.6 %all-to-all-start.3 = ((bf16[64,2,2,8,128]{4,3,2,1,0:T(8,128)(2,1)}), bf16[64,2,2,8,128]{4,3,2,1,0:T(8,128)(2,1)S(1)}, u32[]{:S(2)}, u32[]{:S(2)}) async-start(bf16[64,2,2,8,128]{4,3,2,1,0:T(8,128)(2,1)} %far_rows.1), calls=%async_computation.3 | async-start | bytes 1048576 | tf_op jit(solution)/shard_map/all_to_all | solution.py:389
  85.9 0.0 copy-done.7
  85.9 1.9 %collective-permute-start.4 = (bf16[64,2,2,8,128]{4,3,2,1,0:T(8,128)(2,1)S(1)}, bf16[64,2,2,8,128]{4,3,2,1,0:T(8,128)(2,1)S(1)}, u32[]{:S(2)}, u32[]{:S(2)}) collective-permute-start(bf16[64,2,2,8,128]{4,3,2,1,0:T(8,128)(2,1)S(1)} %copy-done.7), channel_id=1, source_target_pairs={{1,0},{2,1},{3,2},{4,3},{5,4},{6,5},{7,6},{0,7},{9,8},{10,9},{11,1... | collective-permute-start | bytes 1572872 | tf_op jit(solution)/shard_map/ppermute | solution.py:24
  87.8 3.9 %collective-permute-start.6 = (bf16[64,2,2,8,128]{4,3,2,1,0:T(8,128)(2,1)S(1)}, bf16[64,2,2,8,128]{4,3,2,1,0:T(8,128)(2,1)}, u32[]{:S(2)}, u32[]{:S(2)}) collective-permute-start(bf16[64,2,2,8,128]{4,3,2,1,0:T(8,128)(2,1)S(1)} %copy-done.7), channel_id=1, source_target_pairs={{7,0},{0,1},{1,2},{2,3},{3,4},{4,5},{5,6},{6,7},{15,8},{8,9},{9,10... | collective-permute-start | bytes 1572872 | tf_op jit(solution)/shard_map/ppermute | solution.py:24
  91.7 10.0 %collective-permute-done.4.refs_2_ = bf16[64,2,2,8,128]{4,3,2,1,0:T(8,128)(2,1)S(1)} collective-permute-done((bf16[64,2,2,8,128]{4,3,2,1,0:T(8,128)(2,1)S(1)}, bf16[64,2,2,8,128]{4,3,2,1,0:T(8,128)(2,1)S(1)}, u32[]{:S(2)}, u32[]{:S(2)}) %collective-permute-start.4) | collective-permute-done | bytes 524320 | tf_op jit(solution)/shard_map/ppermute | solution.py:24
  101.8 3.4 %collective-permute-start.5 = (bf16[64,2,2,8,128]{4,3,2,1,0:T(8,128)(2,1)S(1)}, bf16[64,2,2,8,128]{4,3,2,1,0:T(8,128)(2,1)S(1)}, u32[]{:S(2)}, u32[]{:S(2)}) collective-permute-start(bf16[64,2,2,8,128]{4,3,2,1,0:T(8,128)(2,1)S(1)} %collective-permute-done.4.refs_2_), channel_id=1, source_target_pairs={{1,0},{2,1},{3,2},{4,3},{5,4},{6,5},{7,6},{0,7},{9,8},{10,9},{11,1... | collective-permute-start | bytes 1572872 | tf_op jit(solution)/shard_map/ppermute | solution.py:24
  105.2 0.0 all-to-all-done.3
  105.2 0.0 copy-start.3
  105.2 0.6 gather_fusion.1
  105.8 0.0 copy-start.1
  105.8 0.8 copy.18
  106.7 4.5 %all-to-all-start.4 = ((bf16[8,52,2,128]{3,2,1,0:T(2,128)(2,1)}), bf16[8,52,2,128]{3,2,1,0:T(2,128)(2,1)S(1)}, u32[]{:S(2)}, u32[]{:S(2)}) async-start(bf16[8,52,2,128]{3,2,1,0:T(2,128)(2,1)} %bitcast.33), calls=%async_computation.4 | async-start | bytes 425984 | tf_op jit(solution)/shard_map/all_to_all | solution.py:393
  111.2 0.0 collective-permute-done.6.refs_3_
  111.3 0.0 copy-start.10
  111.3 1.2 copy-done.10
  112.5 3.2 %near_state.1 = (f32[2,1024,128]{2,1,0:T(8,128)S(1)}, f32[2,512,128]{2,1,0:T(8,128)S(1)}, f32[2,512,128]{2,1,0:T(8,128)S(1)}) custom-call(s32[1]{0:T(128)S(6)} %copy.22.count_ref.refs_0_, bf16[64,2,2,8,128]{4,3,2,1,0:T(8,128)(2,1)S(1)} %copy-done.7, bf16[64,2,2,8,128]{4,3,2,1,0:T(8,128)(2,1)S(1)} %collective-permute-done.4.refs_2_, ...), custom_call_target="tpu_custom_call" | custom-call | flops 4294967296 | bytes 16777216 | tf_op jit(solution)/shard_map/near_state/pallas_call | solution.py:408
  115.6 4.7 %collective-permute-done.5.refs_1_ = bf16[64,2,2,8,128]{4,3,2,1,0:T(8,128)(2,1)S(1)} collective-permute-done((bf16[64,2,2,8,128]{4,3,2,1,0:T(8,128)(2,1)S(1)}, bf16[64,2,2,8,128]{4,3,2,1,0:T(8,128)(2,1)S(1)}, u32[]{:S(2)}, u32[]{:S(2)}) %collective-permute-start.5) | collective-permute-done | bytes 524320 | tf_op jit(solution)/shard_map/ppermute | solution.py:24
  120.3 1.9 %far_state.1 = (f32[2,1024,128]{2,1,0:T(8,128)}, f32[2,512,128]{2,1,0:T(8,128)}, f32[2,512,128]{2,1,0:T(8,128)}) custom-call(s32[1]{0:T(128)S(6)} %copy.22.count_ref.refs_0_, bf16[64,2,2,8,128]{4,3,2,1,0:T(8,128)(2,1)S(1)} %collective-permute-done.5.refs_1_, bf16[2,1024,128]{2,1,0:T(8,128)(2,1)S(1)} %bitcast.22, ...), custom_call_target="tpu_custom_call" | custom-call | tf_op jit(solution)/shard_map/far_state/pallas_call | solution.py:422
  122.3 0.0 all-to-all-done.4.partial_ref
  122.3 0.8 add.2
  (14 shorter events, 0.0 us)
Async XLA Ops:
  0.6 9.0 %copy-start.2 = (f32[1,2,512,128]{3,2,1,0:T(8,128)S(1)}, f32[1,2,512,128]{3,2,1,0:T(8,128)}, u32[]{:S(2)}) copy-start(f32[1,2,512,128]{3,2,1,0:T(8,128)} %param.12) | copy-start | bytes 1572868
  1.7 8.0 %copy-start = (bf16[1,2,1024,128]{3,2,1,0:T(8,128)(2,1)S(1)}, bf16[1,2,1024,128]{3,2,1,0:T(8,128)(2,1)}, u32[]{:S(2)}) copy-start(bf16[1,2,1024,128]{3,2,1,0:T(8,128)(2,1)} %param.11) | copy-start | bytes 1572868
  2.6 17.9 %all-to-all-start = ((bf16[8,52,2,128]{3,2,1,0:T(2,128)(2,1)}), bf16[8,52,2,128]{3,2,1,0:T(2,128)(2,1)S(1)}, u32[]{:S(2)}, u32[]{:S(2)}) async-start(bf16[8,52,2,128]{3,2,1,0:T(2,128)(2,1)} %bitcast.1.refs_0_), calls=%async_computation | async-start | bytes 425984 | tf_op jit(solution)/shard_map/all_to_all | solution.py:306
  9.7 1.0 copy-start.4
  10.9 39.9 %collective-permute-start = (bf16[3584,128]{1,0:T(8,128)(2,1)S(1)}, bf16[3584,128]{1,0:T(8,128)(2,1)}, u32[]{:S(2)}, u32[]{:S(2)}) collective-permute-start(bf16[3584,128]{1,0:T(8,128)(2,1)S(1)} %get-tuple-element.15), channel_id=1, source_target_pairs={{1,0},{2,1},{3,2},{4,3},{5,4},{6,5},{7,6},{0,7},{9,8},{10,9},{11,1... | collective-permute-start | bytes 2752520 | tf_op jit(solution)/shard_map/ppermute | solution.py:24
  16.1 2.6 %copy-start.9 = (s32[1,2]{1,0:T(1,128)S(1)}, s32[1,2]{1,0:T(1,128)}, u32[]{:S(2)}) copy-start(s32[1,2]{1,0:T(1,128)} %list_ref.1) | copy-start | bytes 28
  16.1 40.4 %collective-permute-start.1 = (bf16[3584,128]{1,0:T(8,128)(2,1)S(1)}, bf16[3584,128]{1,0:T(8,128)(2,1)}, u32[]{:S(2)}, u32[]{:S(2)}) collective-permute-start(bf16[3584,128]{1,0:T(8,128)(2,1)S(1)} %get-tuple-element.16), channel_id=1, source_target_pairs={{7,0},{0,1},{1,2},{2,3},{3,4},{4,5},{5,6},{6,7},{15,8},{8,9},{9,10... | collective-permute-start | bytes 2752520 | tf_op jit(solution)/shard_map/ppermute | solution.py:24
  19.3 0.6 copy-start.8
  20.5 0.7 copy-start.11
  21.2 21.6 %all-to-all-start.1 = ((s32[64,1,128]{2,1,0:T(1,128)}), s32[64,1,128]{2,1,0:T(1,128)S(1)}, u32[]{:S(2)}, u32[]{:S(2)}) async-start(s32[64,1,128]{2,1,0:T(1,128)} %after.1), calls=%async_computation.1 | async-start | bytes 65536 | tf_op jit(solution)/shard_map/all_to_all | solution.py:325
  44.4 23.9 %all-to-all-start.2 = ((bf16[64,2,2,8,128]{4,3,2,1,0:T(8,128)(2,1)}), bf16[64,2,2,8,128]{4,3,2,1,0:T(8,128)(2,1)S(1)}, u32[]{:S(2)}, u32[]{:S(2)}) async-start(bf16[64,2,2,8,128]{4,3,2,1,0:T(8,128)(2,1)} %bitcast.5), calls=%async_computation.2 | async-start | bytes 1048576 | tf_op jit(solution)/shard_map/all_to_all | solution.py:343
  51.9 21.3 %collective-permute-start.2 = (bf16[1536,128]{1,0:T(8,128)(2,1)S(1)}, bf16[1536,128]{1,0:T(8,128)(2,1)S(1)}, u32[]{:S(2)}, u32[]{:S(2)}) collective-permute-start(bf16[1536,128]{1,0:T(8,128)(2,1)S(1)} %slice.22), channel_id=1, source_target_pairs={{1,0},{2,1},{3,2},{4,3},{5,4},{6,5},{7,6},{0,7},{9,8},{10,9},{11,1... | collective-permute-start | bytes 1179656 | tf_op jit(solution)/shard_map/ppermute | solution.py:24
  57.5 15.7 %collective-permute-start.3 = (bf16[1536,128]{1,0:T(8,128)(2,1)S(1)}, bf16[1536,128]{1,0:T(8,128)(2,1)S(1)}, u32[]{:S(2)}, u32[]{:S(2)}) collective-permute-start(bf16[1536,128]{1,0:T(8,128)(2,1)S(1)} %slice.23), channel_id=1, source_target_pairs={{7,0},{0,1},{1,2},{2,3},{3,4},{4,5},{5,6},{6,7},{15,8},{8,9},{9,10... | collective-permute-start | bytes 1179656 | tf_op jit(solution)/shard_map/ppermute | solution.py:24
  68.4 0.8 copy-start.6
  73.2 0.8 copy-start.12
  73.3 0.9 copy-start.13
  74.1 31.1 %copy-start.14 = (s32[52]{0:T(128)S(1)}, s32[52]{0:T(128)}, u32[]{:S(2)}) copy-start(s32[52]{0:T(128)} %get-tuple-element.17.refs_6_) | copy-start | bytes 628
  77.2 8.7 %copy-start.7 = (bf16[64,2,2,8,128]{4,3,2,1,0:T(8,128)(2,1)S(1)}, bf16[64,2,2,8,128]{4,3,2,1,0:T(8,128)(2,1)}, u32[]{:S(2)}) copy-start(bf16[64,2,2,8,128]{4,3,2,1,0:T(8,128)(2,1)} %copy-done.6) | copy-start | bytes 1572868
  77.2 34.0 %copy-start.5 = (f32[1,2,512,128]{3,2,1,0:T(8,128)S(1)}, f32[1,2,512,128]{3,2,1,0:T(8,128)}, u32[]{:S(2)}) copy-start(f32[1,2,512,128]{3,2,1,0:T(8,128)} %param.13) | copy-start | bytes 1572868
  77.2 28.0 %all-to-all-start.3 = ((bf16[64,2,2,8,128]{4,3,2,1,0:T(8,128)(2,1)}), bf16[64,2,2,8,128]{4,3,2,1,0:T(8,128)(2,1)S(1)}, u32[]{:S(2)}, u32[]{:S(2)}) async-start(bf16[64,2,2,8,128]{4,3,2,1,0:T(8,128)(2,1)} %far_rows.1), calls=%async_computation.3 | async-start | bytes 1048576 | tf_op jit(solution)/shard_map/all_to_all | solution.py:389
  85.9 15.9 %collective-permute-start.4 = (bf16[64,2,2,8,128]{4,3,2,1,0:T(8,128)(2,1)S(1)}, bf16[64,2,2,8,128]{4,3,2,1,0:T(8,128)(2,1)S(1)}, u32[]{:S(2)}, u32[]{:S(2)}) collective-permute-start(bf16[64,2,2,8,128]{4,3,2,1,0:T(8,128)(2,1)S(1)} %copy-done.7), channel_id=1, source_target_pairs={{1,0},{2,1},{3,2},{4,3},{5,4},{6,5},{7,6},{0,7},{9,8},{10,9},{11,1... | collective-permute-start | bytes 1572872 | tf_op jit(solution)/shard_map/ppermute | solution.py:24
  87.8 23.4 %collective-permute-start.6 = (bf16[64,2,2,8,128]{4,3,2,1,0:T(8,128)(2,1)S(1)}, bf16[64,2,2,8,128]{4,3,2,1,0:T(8,128)(2,1)}, u32[]{:S(2)}, u32[]{:S(2)}) collective-permute-start(bf16[64,2,2,8,128]{4,3,2,1,0:T(8,128)(2,1)S(1)} %copy-done.7), channel_id=1, source_target_pairs={{7,0},{0,1},{1,2},{2,3},{3,4},{4,5},{5,6},{6,7},{15,8},{8,9},{9,10... | collective-permute-start | bytes 1572872 | tf_op jit(solution)/shard_map/ppermute | solution.py:24
  101.8 18.6 %collective-permute-start.5 = (bf16[64,2,2,8,128]{4,3,2,1,0:T(8,128)(2,1)S(1)}, bf16[64,2,2,8,128]{4,3,2,1,0:T(8,128)(2,1)S(1)}, u32[]{:S(2)}, u32[]{:S(2)}) collective-permute-start(bf16[64,2,2,8,128]{4,3,2,1,0:T(8,128)(2,1)S(1)} %collective-permute-done.4.refs_2_), channel_id=1, source_target_pairs={{1,0},{2,1},{3,2},{4,3},{5,4},{6,5},{7,6},{0,7},{9,8},{10,9},{11,1... | collective-permute-start | bytes 1572872 | tf_op jit(solution)/shard_map/ppermute | solution.py:24
  105.2 6.0 %copy-start.3 = (f32[1,2,512,128]{3,2,1,0:T(8,128)S(1)}, f32[1,2,512,128]{3,2,1,0:T(8,128)}, u32[]{:S(2)}) copy-start(f32[1,2,512,128]{3,2,1,0:T(8,128)} %param.12) | copy-start | bytes 1572868
  105.8 5.4 %copy-start.1 = (bf16[1,2,1024,128]{3,2,1,0:T(8,128)(2,1)S(1)}, bf16[1,2,1024,128]{3,2,1,0:T(8,128)(2,1)}, u32[]{:S(2)}) copy-start(bf16[1,2,1024,128]{3,2,1,0:T(8,128)(2,1)} %param.11) | copy-start | bytes 1572868
  106.7 15.6 %all-to-all-start.4 = ((bf16[8,52,2,128]{3,2,1,0:T(2,128)(2,1)}), bf16[8,52,2,128]{3,2,1,0:T(2,128)(2,1)S(1)}, u32[]{:S(2)}, u32[]{:S(2)}) async-start(bf16[8,52,2,128]{3,2,1,0:T(2,128)(2,1)} %bitcast.33), calls=%async_computation.4 | async-start | bytes 425984 | tf_op jit(solution)/shard_map/all_to_all | solution.py:393
  111.3 1.2 copy-start.10

commit v8 on v7

--- a/solution.py
+++ b/solution.py
@@ -382,7 +382,7 @@
             pltpu.VMEM((slot_count, *far_right.shape), far_right.dtype),
             pltpu.SemaphoreType.DMA((slot_count, 3)),
         ],
-        compiler_params=rows_params,
+        compiler_params=params,
         name="far_rows",
     )(grad_rows, total, far_right, far_left)
 

time: 125 us -> 126 us (level)
  local copies, waits for them, and re-layouts: 13.6 us -> 15 us
    unnamed x30, local copies, waits for them, and re-layouts: 5.25 us -> 6.65 us
where the time goes in v8:
time: 126 us; the launch traced here: 124 us
  starting transfers between devices  63.2 us (50%)
  waiting for transfers between devices  30.2 us (24%)
  local copies, waits for them, and re-layouts  15 us (12%)
  Pallas kernels  13 us (10%)
  between operations  1.65 us (1%)
    ppermute x7, starting transfers between devices, shifted(): lax.ppermute(x, 'tensor', [((i + by) % parts, i) for i in range(parts)])  22.7 us
    ppermute x7, waiting for transfers between devices, shifted(): lax.ppermute(x, 'tensor', [((i + by) % parts, i) for i in range(parts)])  14.7 us
    all_to_all x1, starting transfers between devices, on_device(): table = lax.all_to_all(mine, 'dp', 0, 0, tiled=True).reshape(owners, part)  13.8 us
    all_to_all x1, starting transfers between devices, on_device(): returned = lax.all_to_all(back, 'dp', 0, 0, tiled=True)  8.77 us
    all_to_all x1, waiting for transfers between devices, on_device(): arrived = lax.all_to_all(outgoing, 'dp', 0, 0, tiled=True)  8.01 us
    all_to_all x1, starting transfers between devices, on_device(): moved = lax.all_to_all(leaving, 'tensor', 0, 0, tiled=True)  7.1 us
    all_to_all x1, waiting for transfers between devices, on_device(): table = lax.all_to_all(mine, 'dp', 0, 0, tiled=True).reshape(owners, part)  6.84 us
    unnamed x30, local copies, waits for them, and re-layouts  6.65 us
  transfers between devices with their start and end apart: 12, of which 5 were waited for; matrix products, arithmetic and copies ran while one was open for 6% of the time, Pallas kernels for 8%

profile of v8, /device:TPU:6, one launch (start us, length us, event | category | flops | bytes accessed | tf_op | source)
XLA Modules:
  0.0 123.8 jit_solution(5766159888960180230)
XLA Ops:
  0.6 0.0 copy-start.2
  0.6 1.0 reshape.42
  1.7 0.0 copy-start
  1.7 0.1 copy.16
  1.8 0.8 tile.4
  2.6 7.1 %all-to-all-start = ((bf16[8,52,2,128]{3,2,1,0:T(2,128)(2,1)}), bf16[8,52,2,128]{3,2,1,0:T(2,128)(2,1)S(1)}, u32[]{:S(2)}, u32[]{:S(2)}) async-start(bf16[8,52,2,128]{3,2,1,0:T(2,128)(2,1)} %bitcast.1.refs_0_), calls=%async_computation | async-start | bytes 425984 | tf_op jit(solution)/shard_map/all_to_all | solution.py:306
  9.7 0.0 copy-done.2
  9.7 0.0 copy-start.4
  9.7 1.0 copy-done.4
  10.7 0.2 pack.1
  10.9 5.1 %collective-permute-start = (bf16[3584,128]{1,0:T(8,128)(2,1)S(1)}, bf16[3584,128]{1,0:T(8,128)(2,1)}, u32[]{:S(2)}, u32[]{:S(2)}) collective-permute-start(bf16[3584,128]{1,0:T(8,128)(2,1)S(1)} %get-tuple-element.15), channel_id=1, source_target_pairs={{1,0},{2,1},{3,2},{4,3},{5,4},{6,5},{7,6},{0,7},{9,8},{10,9},{11,1... | collective-permute-start | bytes 2752520 | tf_op jit(solution)/shard_map/ppermute | solution.py:24
  16.1 0.0 copy-start.11
  16.1 1.9 %collective-permute-start.1 = (bf16[3584,128]{1,0:T(8,128)(2,1)S(1)}, bf16[3584,128]{1,0:T(8,128)(2,1)}, u32[]{:S(2)}, u32[]{:S(2)}) collective-permute-start(bf16[3584,128]{1,0:T(8,128)(2,1)S(1)} %get-tuple-element.16), channel_id=1, source_target_pairs={{7,0},{0,1},{1,2},{2,3},{3,4},{4,5},{5,6},{6,7},{15,8},{8,9},{9,10... | collective-permute-start | bytes 2752520 | tf_op jit(solution)/shard_map/ppermute | solution.py:24
  18.7 0.6 list.1.sent_ref
  19.3 0.0 copy-start.10
  19.3 0.6 copy-done.10
  19.9 0.6 all-to-all-done.after_ref
  20.5 0.7 copy-done.13
  21.2 13.8 %all-to-all-start.1 = ((s32[64,1,128]{2,1,0:T(1,128)}), s32[64,1,128]{2,1,0:T(1,128)S(1)}, u32[]{:S(2)}, u32[]{:S(2)}) async-start(s32[64,1,128]{2,1,0:T(1,128)} %after.1), calls=%async_computation.1 | async-start | bytes 65536 | tf_op jit(solution)/shard_map/all_to_all | solution.py:325
  35.0 1.0 copy.20
  36.0 6.8 %all-to-all-done.1 = s32[64,1,128]{2,1,0:T(1,128)S(1)} async-done(((s32[64,1,128]{2,1,0:T(1,128)}), s32[64,1,128]{2,1,0:T(1,128)S(1)}, u32[]{:S(2)}, u32[]{:S(2)}) %all-to-all-start.1) | async-done | bytes 32800 | tf_op jit(solution)/shard_map/all_to_all | solution.py:325
  42.8 0.1 reshape.49
  43.0 1.5 %gather_fusion = bf16[128,2,8,128]{3,2,1,0:T(8,128)(2,1)} fusion(bf16[52,2,8,128]{3,2,1,0:T(8,128)(2,1)S(1)} %bitcast.30, s32[1024]{0:T(1024)S(1)} %pad_clamp_fusion.1), kind=kCustom, calls=%fused_computation | custom fusion | bytes 1049088 | tf_op jit(solution)/shard_map/jit(_take)/gather | solution.py:342
  44.4 6.3 %all-to-all-start.2 = ((bf16[64,2,2,8,128]{4,3,2,1,0:T(8,128)(2,1)}), bf16[64,2,2,8,128]{4,3,2,1,0:T(8,128)(2,1)S(1)}, u32[]{:S(2)}, u32[]{:S(2)}) async-start(bf16[64,2,2,8,128]{4,3,2,1,0:T(8,128)(2,1)} %bitcast.5), calls=%async_computation.2 | async-start | bytes 1048576 | tf_op jit(solution)/shard_map/all_to_all | solution.py:343
  50.7 0.2 slice_reduce_fusion
  50.9 0.0 collective-permute-done.refs_4_
  50.9 1.0 slice.22
  51.9 4.5 %collective-permute-start.2 = (bf16[1536,128]{1,0:T(8,128)(2,1)S(1)}, bf16[1536,128]{1,0:T(8,128)(2,1)S(1)}, u32[]{:S(2)}, u32[]{:S(2)}) collective-permute-start(bf16[1536,128]{1,0:T(8,128)(2,1)S(1)} %slice.22), channel_id=1, source_target_pairs={{1,0},{2,1},{3,2},{4,3},{5,4},{6,5},{7,6},{0,7},{9,8},{10,9},{11,1... | collective-permute-start | bytes 1179656 | tf_op jit(solution)/shard_map/ppermute | solution.py:24
  56.5 0.0 collective-permute-done.1.refs_5_
  56.5 1.0 slice.23
  57.5 1.9 %collective-permute-start.3 = (bf16[1536,128]{1,0:T(8,128)(2,1)S(1)}, bf16[1536,128]{1,0:T(8,128)(2,1)S(1)}, u32[]{:S(2)}, u32[]{:S(2)}) collective-permute-start(bf16[1536,128]{1,0:T(8,128)(2,1)S(1)} %slice.23), channel_id=1, source_target_pairs={{7,0},{0,1},{1,2},{2,3},{3,4},{4,5},{5,6},{6,7},{15,8},{8,9},{9,10... | collective-permute-start | bytes 1179656 | tf_op jit(solution)/shard_map/ppermute | solution.py:24
  59.4 0.1 iota_compare_fusion
  59.5 0.2 lt.28
  59.7 0.7 iota_reduce_fusion
  60.4 8.0 %all-to-all-done.2.refs_0_.refs_1_ = bf16[64,2,2,8,128]{4,3,2,1,0:T(8,128)(2,1)S(1)} async-done(((bf16[64,2,2,8,128]{4,3,2,1,0:T(8,128)(2,1)}), bf16[64,2,2,8,128]{4,3,2,1,0:T(8,128)(2,1)S(1)}, u32[]{:S(2)}, u32[]{:S(2)}) %all-to-all-start.2) | async-done | bytes 524320 | tf_op jit(solution)/shard_map/all_to_all | solution.py:343
  68.4 0.8 copy-done.6
  69.2 4.0 %near_rows.1 = (bf16[2,128,1024]{2,1,0:T(8,128)(2,1)}, f32[2,128,1024]{2,1,0:T(8,128)}) custom-call(bf16[64,2,2,8,128]{4,3,2,1,0:T(8,128)(2,1)} %copy-done.6, bf16[2,1024,128]{2,1,0:T(8,128)(2,1)} %bitcast.19, f32[2,512,128]{2,1,0:T(8,128)} %bitcast.23, f32[2,512,128]{2,1,0:T(8,128)} %bitcast.26, bf16[3584,128]{1,0:T(8,128)(2,1)} %collective-permute-done.refs_4_, ...), custom_call_target="tpu_custom_call" | custom-call | flops 65536 | bytes 1024 | tf_op jit(solution)/shard_map/near_rows/pallas_call | solution.py:351
  73.2 0.0 collective-permute-done.2.refs_2_
  73.2 0.0 collective-permute-done.3.refs_3_
  73.2 0.0 copy-start.8
  73.3 1.2 copy-done.8
  74.5 1.0 copy-done.9
  75.5 2.3 %far_rows.1 = bf16[64,2,2,8,128]{4,3,2,1,0:T(8,128)(2,1)} custom-call(bf16[2,128,1024]{2,1,0:T(8,128)(2,1)S(1)} %copy-done.9, f32[2,128,1024]{2,1,0:T(8,128)S(1)} %copy-done.8, bf16[1536,128]{1,0:T(8,128)(2,1)S(1)} %collective-permute-done.2.refs_2_, bf16[1536,128]{1,0:T(8,128)(2,1)S(1)} %collective-permute-done.3.refs_3_), custom_call_target="tpu_custom_call" | custom-call | tf_op jit(solution)/shard_map/far_rows/pallas_call | solution.py:371
  77.8 0.0 copy-start.7
  77.8 0.0 copy-start.5
  77.8 8.8 %all-to-all-start.3 = ((bf16[64,2,2,8,128]{4,3,2,1,0:T(8,128)(2,1)}), bf16[64,2,2,8,128]{4,3,2,1,0:T(8,128)(2,1)S(1)}, u32[]{:S(2)}, u32[]{:S(2)}) async-start(bf16[64,2,2,8,128]{4,3,2,1,0:T(8,128)(2,1)} %far_rows.1), calls=%async_computation.3 | async-start | bytes 1048576 | tf_op jit(solution)/shard_map/all_to_all | solution.py:389
  86.6 1.9 %collective-permute-start.4 = (bf16[64,2,2,8,128]{4,3,2,1,0:T(8,128)(2,1)S(1)}, bf16[64,2,2,8,128]{4,3,2,1,0:T(8,128)(2,1)S(1)}, u32[]{:S(2)}, u32[]{:S(2)}) collective-permute-start(bf16[64,2,2,8,128]{4,3,2,1,0:T(8,128)(2,1)S(1)} %copy-done.7), channel_id=1, source_target_pairs={{1,0},{2,1},{3,2},{4,3},{5,4},{6,5},{7,6},{0,7},{9,8},{10,9},{11,1... | collective-permute-start | bytes 1572872 | tf_op jit(solution)/shard_map/ppermute | solution.py:24
  88.6 3.9 %collective-permute-start.6 = (bf16[64,2,2,8,128]{4,3,2,1,0:T(8,128)(2,1)S(1)}, bf16[64,2,2,8,128]{4,3,2,1,0:T(8,128)(2,1)}, u32[]{:S(2)}, u32[]{:S(2)}) collective-permute-start(bf16[64,2,2,8,128]{4,3,2,1,0:T(8,128)(2,1)S(1)} %copy-done.7), channel_id=1, source_target_pairs={{7,0},{0,1},{1,2},{2,3},{3,4},{4,5},{5,6},{6,7},{15,8},{8,9},{9,10... | collective-permute-start | bytes 1572872 | tf_op jit(solution)/shard_map/ppermute | solution.py:24
  92.5 10.0 %collective-permute-done.4.refs_2_ = bf16[64,2,2,8,128]{4,3,2,1,0:T(8,128)(2,1)S(1)} collective-permute-done((bf16[64,2,2,8,128]{4,3,2,1,0:T(8,128)(2,1)S(1)}, bf16[64,2,2,8,128]{4,3,2,1,0:T(8,128)(2,1)S(1)}, u32[]{:S(2)}, u32[]{:S(2)}) %collective-permute-start.4) | collective-permute-done | bytes 524320 | tf_op jit(solution)/shard_map/ppermute | solution.py:24
  102.5 3.4 %collective-permute-start.5 = (bf16[64,2,2,8,128]{4,3,2,1,0:T(8,128)(2,1)S(1)}, bf16[64,2,2,8,128]{4,3,2,1,0:T(8,128)(2,1)S(1)}, u32[]{:S(2)}, u32[]{:S(2)}) collective-permute-start(bf16[64,2,2,8,128]{4,3,2,1,0:T(8,128)(2,1)S(1)} %collective-permute-done.4.refs_2_), channel_id=1, source_target_pairs={{1,0},{2,1},{3,2},{4,3},{5,4},{6,5},{7,6},{0,7},{9,8},{10,9},{11,1... | collective-permute-start | bytes 1572872 | tf_op jit(solution)/shard_map/ppermute | solution.py:24
  105.9 0.0 all-to-all-done.3
  105.9 0.0 copy-start.3
  106.0 0.6 gather_fusion.1
  106.6 0.0 copy-start.1
  106.6 0.8 copy.18
  107.4 4.5 %all-to-all-start.4 = ((bf16[8,52,2,128]{3,2,1,0:T(2,128)(2,1)}), bf16[8,52,2,128]{3,2,1,0:T(2,128)(2,1)S(1)}, u32[]{:S(2)}, u32[]{:S(2)}) async-start(bf16[8,52,2,128]{3,2,1,0:T(2,128)(2,1)} %bitcast.33), calls=%async_computation.4 | async-start | bytes 425984 | tf_op jit(solution)/shard_map/all_to_all | solution.py:393
  112.0 0.0 collective-permute-done.6.refs_3_
  112.0 0.0 copy-start.12
  112.0 1.2 copy-done.12
  113.2 3.2 %near_state.1 = (f32[2,1024,128]{2,1,0:T(8,128)S(1)}, f32[2,512,128]{2,1,0:T(8,128)S(1)}, f32[2,512,128]{2,1,0:T(8,128)S(1)}) custom-call(s32[1]{0:T(128)S(6)} %copy.22.count_ref.refs_0_, bf16[64,2,2,8,128]{4,3,2,1,0:T(8,128)(2,1)S(1)} %copy-done.7, bf16[64,2,2,8,128]{4,3,2,1,0:T(8,128)(2,1)S(1)} %collective-permute-done.4.refs_2_, ...), custom_call_target="tpu_custom_call" | custom-call | flops 4294967296 | bytes 16777216 | tf_op jit(solution)/shard_map/near_state/pallas_call | solution.py:408
  116.4 4.7 %collective-permute-done.5.refs_1_ = bf16[64,2,2,8,128]{4,3,2,1,0:T(8,128)(2,1)S(1)} collective-permute-done((bf16[64,2,2,8,128]{4,3,2,1,0:T(8,128)(2,1)S(1)}, bf16[64,2,2,8,128]{4,3,2,1,0:T(8,128)(2,1)S(1)}, u32[]{:S(2)}, u32[]{:S(2)}) %collective-permute-start.5) | collective-permute-done | bytes 524320 | tf_op jit(solution)/shard_map/ppermute | solution.py:24
  121.1 1.9 %far_state.1 = (f32[2,1024,128]{2,1,0:T(8,128)}, f32[2,512,128]{2,1,0:T(8,128)}, f32[2,512,128]{2,1,0:T(8,128)}) custom-call(s32[1]{0:T(128)S(6)} %copy.22.count_ref.refs_0_, bf16[64,2,2,8,128]{4,3,2,1,0:T(8,128)(2,1)S(1)} %collective-permute-done.5.refs_1_, bf16[2,1024,128]{2,1,0:T(8,128)(2,1)S(1)} %bitcast.22, ...), custom_call_target="tpu_custom_call" | custom-call | tf_op jit(solution)/shard_map/far_state/pallas_call | solution.py:422
  123.0 0.0 all-to-all-done.4.partial_ref
  123.0 0.8 add.2
  (14 shorter events, 0.0 us)
Async XLA Ops:
  0.6 9.0 %copy-start.2 = (f32[1,2,512,128]{3,2,1,0:T(8,128)S(1)}, f32[1,2,512,128]{3,2,1,0:T(8,128)}, u32[]{:S(2)}) copy-start(f32[1,2,512,128]{3,2,1,0:T(8,128)} %param.12) | copy-start | bytes 1572868
  1.7 8.0 %copy-start = (bf16[1,2,1024,128]{3,2,1,0:T(8,128)(2,1)S(1)}, bf16[1,2,1024,128]{3,2,1,0:T(8,128)(2,1)}, u32[]{:S(2)}) copy-start(bf16[1,2,1024,128]{3,2,1,0:T(8,128)(2,1)} %param.11) | copy-start | bytes 1572868
  2.6 17.9 %all-to-all-start = ((bf16[8,52,2,128]{3,2,1,0:T(2,128)(2,1)}), bf16[8,52,2,128]{3,2,1,0:T(2,128)(2,1)S(1)}, u32[]{:S(2)}, u32[]{:S(2)}) async-start(bf16[8,52,2,128]{3,2,1,0:T(2,128)(2,1)} %bitcast.1.refs_0_), calls=%async_computation | async-start | bytes 425984 | tf_op jit(solution)/shard_map/all_to_all | solution.py:306
  9.7 1.0 copy-start.4
  10.9 40.0 %collective-permute-start = (bf16[3584,128]{1,0:T(8,128)(2,1)S(1)}, bf16[3584,128]{1,0:T(8,128)(2,1)}, u32[]{:S(2)}, u32[]{:S(2)}) collective-permute-start(bf16[3584,128]{1,0:T(8,128)(2,1)S(1)} %get-tuple-element.15), channel_id=1, source_target_pairs={{1,0},{2,1},{3,2},{4,3},{5,4},{6,5},{7,6},{0,7},{9,8},{10,9},{11,1... | collective-permute-start | bytes 2752520 | tf_op jit(solution)/shard_map/ppermute | solution.py:24
  16.1 2.6 %copy-start.11 = (s32[1,2]{1,0:T(1,128)S(1)}, s32[1,2]{1,0:T(1,128)}, u32[]{:S(2)}) copy-start(s32[1,2]{1,0:T(1,128)} %list_ref.1) | copy-start | bytes 28
  16.1 40.4 %collective-permute-start.1 = (bf16[3584,128]{1,0:T(8,128)(2,1)S(1)}, bf16[3584,128]{1,0:T(8,128)(2,1)}, u32[]{:S(2)}, u32[]{:S(2)}) collective-permute-start(bf16[3584,128]{1,0:T(8,128)(2,1)S(1)} %get-tuple-element.16), channel_id=1, source_target_pairs={{7,0},{0,1},{1,2},{2,3},{3,4},{4,5},{5,6},{6,7},{15,8},{8,9},{9,10... | collective-permute-start | bytes 2752520 | tf_op jit(solution)/shard_map/ppermute | solution.py:24
  19.3 0.6 copy-start.10
  20.5 0.7 copy-start.13
  21.2 21.6 %all-to-all-start.1 = ((s32[64,1,128]{2,1,0:T(1,128)}), s32[64,1,128]{2,1,0:T(1,128)S(1)}, u32[]{:S(2)}, u32[]{:S(2)}) async-start(s32[64,1,128]{2,1,0:T(1,128)} %after.1), calls=%async_computation.1 | async-start | bytes 65536 | tf_op jit(solution)/shard_map/all_to_all | solution.py:325
  44.4 23.9 %all-to-all-start.2 = ((bf16[64,2,2,8,128]{4,3,2,1,0:T(8,128)(2,1)}), bf16[64,2,2,8,128]{4,3,2,1,0:T(8,128)(2,1)S(1)}, u32[]{:S(2)}, u32[]{:S(2)}) async-start(bf16[64,2,2,8,128]{4,3,2,1,0:T(8,128)(2,1)} %bitcast.5), calls=%async_computation.2 | async-start | bytes 1048576 | tf_op jit(solution)/shard_map/all_to_all | solution.py:343
  51.9 21.3 %collective-permute-start.2 = (bf16[1536,128]{1,0:T(8,128)(2,1)S(1)}, bf16[1536,128]{1,0:T(8,128)(2,1)S(1)}, u32[]{:S(2)}, u32[]{:S(2)}) collective-permute-start(bf16[1536,128]{1,0:T(8,128)(2,1)S(1)} %slice.22), channel_id=1, source_target_pairs={{1,0},{2,1},{3,2},{4,3},{5,4},{6,5},{7,6},{0,7},{9,8},{10,9},{11,1... | collective-permute-start | bytes 1179656 | tf_op jit(solution)/shard_map/ppermute | solution.py:24
  57.5 15.7 %collective-permute-start.3 = (bf16[1536,128]{1,0:T(8,128)(2,1)S(1)}, bf16[1536,128]{1,0:T(8,128)(2,1)S(1)}, u32[]{:S(2)}, u32[]{:S(2)}) collective-permute-start(bf16[1536,128]{1,0:T(8,128)(2,1)S(1)} %slice.23), channel_id=1, source_target_pairs={{7,0},{0,1},{1,2},{2,3},{3,4},{4,5},{5,6},{6,7},{15,8},{8,9},{9,10... | collective-permute-start | bytes 1179656 | tf_op jit(solution)/shard_map/ppermute | solution.py:24
  68.4 0.8 copy-start.6
  73.2 1.2 copy-start.8
  74.5 1.0 copy-start.9
  75.5 30.4 %copy-start.14 = (s32[52]{0:T(128)S(1)}, s32[52]{0:T(128)}, u32[]{:S(2)}) copy-start(s32[52]{0:T(128)} %get-tuple-element.17.refs_6_) | copy-start | bytes 628
  77.8 8.8 %copy-start.7 = (bf16[64,2,2,8,128]{4,3,2,1,0:T(8,128)(2,1)S(1)}, bf16[64,2,2,8,128]{4,3,2,1,0:T(8,128)(2,1)}, u32[]{:S(2)}) copy-start(bf16[64,2,2,8,128]{4,3,2,1,0:T(8,128)(2,1)} %copy-done.6) | copy-start | bytes 1572868
  77.8 34.1 %copy-start.5 = (f32[1,2,512,128]{3,2,1,0:T(8,128)S(1)}, f32[1,2,512,128]{3,2,1,0:T(8,128)}, u32[]{:S(2)}) copy-start(f32[1,2,512,128]{3,2,1,0:T(8,128)} %param.13) | copy-start | bytes 1572868
  77.8 28.1 %all-to-all-start.3 = ((bf16[64,2,2,8,128]{4,3,2,1,0:T(8,128)(2,1)}), bf16[64,2,2,8,128]{4,3,2,1,0:T(8,128)(2,1)S(1)}, u32[]{:S(2)}, u32[]{:S(2)}) async-start(bf16[64,2,2,8,128]{4,3,2,1,0:T(8,128)(2,1)} %far_rows.1), calls=%async_computation.3 | async-start | bytes 1048576 | tf_op jit(solution)/shard_map/all_to_all | solution.py:389
  86.6 15.9 %collective-permute-start.4 = (bf16[64,2,2,8,128]{4,3,2,1,0:T(8,128)(2,1)S(1)}, bf16[64,2,2,8,128]{4,3,2,1,0:T(8,128)(2,1)S(1)}, u32[]{:S(2)}, u32[]{:S(2)}) collective-permute-start(bf16[64,2,2,8,128]{4,3,2,1,0:T(8,128)(2,1)S(1)} %copy-done.7), channel_id=1, source_target_pairs={{1,0},{2,1},{3,2},{4,3},{5,4},{6,5},{7,6},{0,7},{9,8},{10,9},{11,1... | collective-permute-start | bytes 1572872 | tf_op jit(solution)/shard_map/ppermute | solution.py:24
  88.6 23.4 %collective-permute-start.6 = (bf16[64,2,2,8,128]{4,3,2,1,0:T(8,128)(2,1)S(1)}, bf16[64,2,2,8,128]{4,3,2,1,0:T(8,128)(2,1)}, u32[]{:S(2)}, u32[]{:S(2)}) collective-permute-start(bf16[64,2,2,8,128]{4,3,2,1,0:T(8,128)(2,1)S(1)} %copy-done.7), channel_id=1, source_target_pairs={{7,0},{0,1},{1,2},{2,3},{3,4},{4,5},{5,6},{6,7},{15,8},{8,9},{9,10... | collective-permute-start | bytes 1572872 | tf_op jit(solution)/shard_map/ppermute | solution.py:24
  102.5 18.6 %collective-permute-start.5 = (bf16[64,2,2,8,128]{4,3,2,1,0:T(8,128)(2,1)S(1)}, bf16[64,2,2,8,128]{4,3,2,1,0:T(8,128)(2,1)S(1)}, u32[]{:S(2)}, u32[]{:S(2)}) collective-permute-start(bf16[64,2,2,8,128]{4,3,2,1,0:T(8,128)(2,1)S(1)} %collective-permute-done.4.refs_2_), channel_id=1, source_target_pairs={{1,0},{2,1},{3,2},{4,3},{5,4},{6,5},{7,6},{0,7},{9,8},{10,9},{11,1... | collective-permute-start | bytes 1572872 | tf_op jit(solution)/shard_map/ppermute | solution.py:24
  105.9 6.0 %copy-start.3 = (f32[1,2,512,128]{3,2,1,0:T(8,128)S(1)}, f32[1,2,512,128]{3,2,1,0:T(8,128)}, u32[]{:S(2)}) copy-start(f32[1,2,512,128]{3,2,1,0:T(8,128)} %param.12) | copy-start | bytes 1572868
  106.6 5.4 %copy-start.1 = (bf16[1,2,1024,128]{3,2,1,0:T(8,128)(2,1)S(1)}, bf16[1,2,1024,128]{3,2,1,0:T(8,128)(2,1)}, u32[]{:S(2)}) copy-start(bf16[1,2,1024,128]{3,2,1,0:T(8,128)(2,1)} %param.11) | copy-start | bytes 1572868
  107.4 15.6 %all-to-all-start.4 = ((bf16[8,52,2,128]{3,2,1,0:T(2,128)(2,1)}), bf16[8,52,2,128]{3,2,1,0:T(2,128)(2,1)S(1)}, u32[]{:S(2)}, u32[]{:S(2)}) async-start(bf16[8,52,2,128]{3,2,1,0:T(2,128)(2,1)} %bitcast.33), calls=%async_computation.4 | async-start | bytes 425984 | tf_op jit(solution)/shard_map/all_to_all | solution.py:393
  112.0 1.2 copy-start.12
